TPU v7x, 256 devices: a whole 4x4x8 slice. The times are simulated.
256 devices in a mesh: sec: 4 (over y), gz: 4 (over z_lo, core), ta: 16 (over z_hi, x).
Axes of the slice: x: 4, y: 4, z: 8 (z_hi: 4, z_lo: 2; z = z_hi * 2 + z_lo), core: 2. Of those that a mesh axis runs over, the one named last changes fastest.
Arguments:
- source: bfloat16 [16, 8, 6, 8, 32, 128], P('sec', None, None, 'gz', 'ta'), may hold values from -6 to 6
- coarse_links: bfloat16 [8, 6, 8, 32, 9, 64, 128], P('sec', None, 'gz', 'ta'), may hold values from -0.09375 to 0.09375
Outputs:
- correction: float32 [16, 8, 6, 8, 32, 128], P('sec', None, None, 'gz', 'ta')
All inputs are finite; a program needn't handle non-finite values.
Results may differ from a plain program's by a relative error of at most 0.0014.
Values may be sent and summed in bfloat16 or wider, within the bound.
No kernel may reach another device: no remote copies, remote signals or barrier semaphores. Data moves between devices by JAX's collectives and lax.ppermute only.
A program may use at most 128 MiB of HBM per device.

v0:
```python
import jax
import jax.numpy as jnp
from jax import lax
from jax.sharding import PartitionSpec as P

SWEEPS = 3


def extended(block, sides, width):
    for axis, dim in sides:
        count = lax.axis_size(axis)
        forward = [(i, i + 1) for i in range(count - 1)]
        forward.append((count - 1, 0))
        backward = [(target, source) for source, target in forward]
        low = lax.ppermute(
            lax.slice_in_dim(block, block.shape[dim] - width, None, axis=dim), axis, forward
        )
        high = lax.ppermute(lax.slice_in_dim(block, 0, width, axis=dim), axis, backward)
        block = jnp.concatenate([low, block, high], axis=dim)
    return block


def real_blocks(coarse_links):
    components = coarse_links.shape[-1] // 2
    site_count = (
        coarse_links.shape[0]
        * coarse_links.shape[1]
        * coarse_links.shape[2]
        * coarse_links.shape[3]
    )
    flat_links = coarse_links.reshape(site_count, 9, components, 2 * components)
    link_real = jnp.swapaxes(flat_links[..., :components], -1, -2)
    link_imag = jnp.swapaxes(flat_links[..., components:], -1, -2)
    upper = jnp.concatenate([link_real, link_imag], -1)
    lower = jnp.concatenate([-link_imag, link_real], -1)
    return jnp.concatenate([upper, lower], 2)


def apply_hops(current, block_links):
    padded = extended(current, (("sec", 2), ("gz", 4), ("ta", 5)), 1)
    center = padded[:, :, 1:-1, :, 1:-1, 1:-1]
    shifted = [
        center,
        padded[:, :, 2:, :, 1:-1, 1:-1],
        padded[:, :, :-2, :, 1:-1, 1:-1],
        jnp.roll(center, -1, axis=3),
        jnp.roll(center, 1, axis=3),
        padded[:, :, 1:-1, :, 2:, 1:-1],
        padded[:, :, 1:-1, :, :-2, 1:-1],
        padded[:, :, 1:-1, :, 1:-1, 2:],
        padded[:, :, 1:-1, :, 1:-1, :-2],
    ]
    width = current.shape[-1]
    columns = current.shape[0] * current.shape[1]
    site_count = center.shape[2] * center.shape[3] * center.shape[4] * center.shape[5]
    hopping = jnp.zeros((columns, site_count, width), jnp.float32)
    for direction in range(9):
        flat_slice = shifted[direction].reshape(columns, site_count, width)
        hopping = hopping + jnp.einsum(
            "csn,sno->cso",
            flat_slice,
            block_links[:, direction],
            preferred_element_type=jnp.float32,
        )
    return hopping.reshape(current.shape)


def richardson(source_blocks, block_links):
    target = source_blocks.astype(jnp.float32)
    iterate = target
    for repeat in range(SWEEPS - 1):
        iterate = target - apply_hops(iterate.astype(jnp.bfloat16), block_links)
    return iterate


def give_back(iterate):
    return lax.all_to_all(iterate, "sec", split_axis=0, concat_axis=2, tiled=True)


def local(source, coarse_links):
    blocks = source.reshape((1,) + source.shape)
    block_links = real_blocks(coarse_links)
    arrived = lax.all_to_all(blocks, "sec", split_axis=2, concat_axis=0, tiled=True)
    result = give_back(richardson(arrived, block_links))
    return result.reshape(source.shape)


def solution(mesh):
    return jax.shard_map(
        local,
        mesh=mesh,
        in_specs=(
            P("sec", None, None, "gz", "ta", None),
            P("sec", None, "gz", "ta", None, None, None),
        ),
        out_specs=P("sec", None, None, "gz", "ta", None),
        check_vma=False,
    )
```

profile of v0, /device:TPU:102, one launch (start us, length us, event | category | flops | bytes accessed | tf_op | source)
XLA Modules:
  0.0 162.1 jit_solution(737632971801376586)
XLA Ops:
  0.0 1.7 %copy.38 = bf16[4,8,6,2,2,128]{5,4,3,2,0,1:T(2,128)(2,1)} copy(bf16[4,8,6,2,2,128]{5,4,3,2,1,0:T(2,128)(2,1)} %param.2) | data formatting | bytes 393216 | tf_op args[0]
  1.7 4.5 %all-to-all-start = ((bf16[1,4,8,6,2,2,128]{6,5,4,3,1,0,2:T(2,128)(2,1)}), bf16[1,4,8,6,2,2,128]{6,5,4,3,1,0,2:T(2,128)(2,1)S(1)}, u32[]{:S(2)}, u32[]{:S(2)}) async-start(bf16[1,4,8,6,2,2,128]{6,5,4,3,1,0,2:T(2,128)(2,1)} %bitcast.136), calls=%async_computation | async-start | bytes 393216 | tf_op jit(solution)/shard_map/all_to_all | solution.py:83
  6.2 14.4 %copy.8 = bf16[2,6,2,2,9,64,128]{5,6,3,2,1,0,4:T(8,128)(2,1)} copy(bf16[2,6,2,2,9,64,128]{6,5,4,3,2,1,0:T(8,128)(2,1)} %param.3) | data formatting | bytes 14155776 | tf_op args[1]
  20.6 12.6 %slice_bitcast_fusion = (bf16[48,9,64,64]{3,2,0,1:T(8,128)(2,1)}, bf16[48,9,64,64]{3,2,0,1:T(8,128)(2,1)}) fusion(bf16[48,9,64,128]{2,3,0,1:T(8,128)(2,1)} %bitcast.138), kind=kLoop, calls=%fused_computation.1 | loop fusion | bytes 14155776 | tf_op jit(solution)/shard_map/transpose | solution.py:33
  33.2 1.6 %copy-done.1 = bf16[2,6,2,2,9,64,128]{5,6,3,2,1,0,4:T(8,128)(2,1)S(1)} copy-done((bf16[2,6,2,2,9,64,128]{5,6,3,2,1,0,4:T(8,128)(2,1)S(1)}, bf16[2,6,2,2,9,64,128]{5,6,3,2,1,0,4:T(8,128)(2,1)}, u32[]{:S(2)}) %copy-start.1) | copy-done | bytes 7077912
  34.9 3.8 %fusion.37 = bf16[48,9,64,64]{3,2,0,1:T(8,128)(2,1)} fusion(bf16[48,9,64,128]{2,3,0,1:T(8,128)(2,1)S(1)} %bitcast.139), kind=kLoop, calls=%fused_computation.98 | loop fusion | flops 1769472 | bytes 7077888 | tf_op jit(solution)/shard_map/neg | solution.py:35
  38.6 19.9 %maximum_maximum_fusion = bf16[48,9,128,128]{3,2,0,1:T(8,128)(2,1)} fusion(bf16[48,9,64,64]{3,2,0,1:T(8,128)(2,1)} %get-tuple-element.6, bf16[48,9,64,64]{3,2,0,1:T(8,128)(2,1)} %fusion.37, bf16[48,9,64,64]{3,2,0,1:T(8,128)(2,1)} %get-tuple-element.5), kind=kLoop, calls=%fused_computation | loop fusion | flops 56623104 | bytes 24772608 | tf_op jit(solution)/shard_map/concatenate | solution.py:36
  58.9 3.3 %collective-permute-start = (bf16[4,4,1,6,2,2,128]{6,1,5,4,3,2,0:T(4,128)(2,1)S(1)}, bf16[4,4,1,6,2,2,128]{6,1,5,4,3,2,0:T(4,128)(2,1)S(1)}, u32[]{:S(2)}, u32[]{:S(2)}) collective-permute-start(bf16[4,4,1,6,2,2,128]{6,1,5,4,3,2,0:T(4,128)(2,1)S(1)} %get-tuple-element.38), channel_id=1, source_target_pairs={{64,0},{128,64},{192,128},{0,192},{65,1},{129,65},{193,129},{1,193... | collective-permute-start | bytes 294920 | tf_op jit(solution)/shard_map/ppermute | solution.py:18
  62.7 1.8 %collective-permute-done = bf16[4,4,1,6,2,2,128]{6,1,5,4,3,2,0:T(4,128)(2,1)S(1)} collective-permute-done((bf16[4,4,1,6,2,2,128]{6,1,5,4,3,2,0:T(4,128)(2,1)S(1)}, bf16[4,4,1,6,2,2,128]{6,1,5,4,3,2,0:T(4,128)(2,1)S(1)}, u32[]{:S(2)}, u32[]{:S(2)}) %collective-permute-start) | collective-permute-done | bytes 98336 | tf_op jit(solution)/shard_map/ppermute | solution.py:18
  64.5 3.6 %collective-permute-done.1 = bf16[4,4,1,6,2,2,128]{6,1,5,4,3,2,0:T(4,128)(2,1)S(1)} collective-permute-done((bf16[4,4,1,6,2,2,128]{6,1,5,4,3,2,0:T(4,128)(2,1)S(1)}, bf16[4,4,1,6,2,2,128]{6,1,5,4,3,2,0:T(4,128)(2,1)S(1)}, u32[]{:S(2)}, u32[]{:S(2)}) %collective-permute-start.1) | collective-permute-done | bytes 98336 | tf_op jit(solution)/shard_map/ppermute | solution.py:15
  69.1 1.9 %fusion = f32[48,128,16]{1,2,0:T(8,128)S(1)} fusion(bf16[16,48,128]{2,0,1:T(8,128)(2,1)S(1)} %bitcast.152, bf16[48,9,128,128]{3,2,0,1:T(8,128)(2,1)} %maximum_maximum_fusion), kind=kOutput, calls=%fused_computation.12 | convolution fusion | flops 25165824 | bytes 2162688 | tf_op jit(solution)/shard_map/csn,sno->cso/dot_general | solution.py:59
  71.0 2.7 %collective-permute-done.2 = bf16[4,4,4,6,1,2,128]{6,1,5,4,3,2,0:T(4,128)(2,1)S(1)} collective-permute-done((bf16[4,4,4,6,1,2,128]{6,1,5,4,3,2,0:T(4,128)(2,1)S(1)}, bf16[4,4,4,6,1,2,128]{6,1,5,4,3,2,0:T(4,128)(2,1)S(1)}, u32[]{:S(2)}, u32[]{:S(2)}) %collective-permute-start.2) | collective-permute-done | bytes 196640 | tf_op jit(solution)/shard_map/ppermute | solution.py:18
  73.7 0.7 collective-permute-done.3
  74.5 0.6 pad_maximum_fusion
  75.4 4.5 %collective-permute-start.5 = (bf16[4,4,4,6,4,1,128]{6,1,5,4,3,2,0:T(4,128)(2,1)S(1)}, bf16[4,4,4,6,4,1,128]{6,1,5,4,3,2,0:T(4,128)(2,1)S(1)}, u32[]{:S(2)}, u32[]{:S(2)}) collective-permute-start(bf16[4,4,4,6,4,1,128]{6,1,5,4,3,2,0:T(4,128)(2,1)S(1)} %get-tuple-element.13), channel_id=1, source_target_pairs={{0,1},{1,2},{2,3},{3,4},{4,5},{5,6},{6,7},{7,8},{8,9},{9,10},{10,1... | collective-permute-start | bytes 1179656 | tf_op jit(solution)/shard_map/ppermute | solution.py:15
  80.3 1.9 %fusion.33 = f32[48,128,16]{1,2,0:T(8,128)S(1)} fusion(f32[48,128,16]{1,2,0:T(8,128)S(1)} %fusion, bf16[16,48,128]{2,0,1:T(8,128)(2,1)S(1)} %bitcast.170, bf16[48,9,128,128]{3,2,0,1:T(8,128)(2,1)} %maximum_maximum_fusion), kind=kOutput, calls=%fused_computation.45 | convolution fusion | flops 25264128 | bytes 2555904 | tf_op jit(solution)/shard_map/csn,sno->cso/dot_general | solution.py:59
  82.2 14.2 %collective-permute-done.5 = bf16[4,4,4,6,4,1,128]{6,1,5,4,3,2,0:T(4,128)(2,1)S(1)} collective-permute-done((bf16[4,4,4,6,4,1,128]{6,1,5,4,3,2,0:T(4,128)(2,1)S(1)}, bf16[4,4,4,6,4,1,128]{6,1,5,4,3,2,0:T(4,128)(2,1)S(1)}, u32[]{:S(2)}, u32[]{:S(2)}) %collective-permute-start.5) | collective-permute-done | bytes 393248 | tf_op jit(solution)/shard_map/ppermute | solution.py:15
  96.5 6.0 %collective-permute-done.4 = bf16[4,4,4,6,4,1,128]{6,1,5,4,3,2,0:T(4,128)(2,1)S(1)} collective-permute-done((bf16[4,4,4,6,4,1,128]{6,1,5,4,3,2,0:T(4,128)(2,1)S(1)}, bf16[4,4,4,6,4,1,128]{6,1,5,4,3,2,0:T(4,128)(2,1)S(1)}, u32[]{:S(2)}, u32[]{:S(2)}) %collective-permute-start.4) | collective-permute-done | bytes 393248 | tf_op jit(solution)/shard_map/ppermute | solution.py:18
  102.5 0.6 pad_maximum_fusion.22
  107.6 2.0 %collective-permute-start.7 = (bf16[4,4,1,6,2,2,128]{6,1,5,4,3,2,0:T(4,128)(2,1)S(1)}, bf16[4,4,1,6,2,2,128]{6,1,5,4,3,2,0:T(4,128)(2,1)S(1)}, u32[]{:S(2)}, u32[]{:S(2)}) collective-permute-start(bf16[4,4,1,6,2,2,128]{6,1,5,4,3,2,0:T(4,128)(2,1)S(1)} %get-tuple-element.31), channel_id=1, source_target_pairs={{0,64},{64,128},{128,192},{192,0},{1,65},{65,129},{129,193},{193,1... | collective-permute-start | bytes 294920 | tf_op jit(solution)/shard_map/ppermute | solution.py:15
  110.0 2.1 %collective-permute-done.6 = bf16[4,4,1,6,2,2,128]{6,1,5,4,3,2,0:T(4,128)(2,1)S(1)} collective-permute-done((bf16[4,4,1,6,2,2,128]{6,1,5,4,3,2,0:T(4,128)(2,1)S(1)}, bf16[4,4,1,6,2,2,128]{6,1,5,4,3,2,0:T(4,128)(2,1)S(1)}, u32[]{:S(2)}, u32[]{:S(2)}) %collective-permute-start.6) | collective-permute-done | bytes 98336 | tf_op jit(solution)/shard_map/ppermute | solution.py:18
  112.2 1.3 collective-permute-done.7
  115.0 3.3 %collective-permute-done.8 = bf16[4,4,4,6,1,2,128]{6,1,5,4,3,2,0:T(4,128)(2,1)S(1)} collective-permute-done((bf16[4,4,4,6,1,2,128]{6,1,5,4,3,2,0:T(4,128)(2,1)S(1)}, bf16[4,4,4,6,1,2,128]{6,1,5,4,3,2,0:T(4,128)(2,1)S(1)}, u32[]{:S(2)}, u32[]{:S(2)}) %collective-permute-start.8) | collective-permute-done | bytes 196640 | tf_op jit(solution)/shard_map/ppermute | solution.py:18
  118.3 3.0 %collective-permute-done.9 = bf16[4,4,4,6,1,2,128]{6,1,5,4,3,2,0:T(4,128)(2,1)S(1)} collective-permute-done((bf16[4,4,4,6,1,2,128]{6,1,5,4,3,2,0:T(4,128)(2,1)S(1)}, bf16[4,4,4,6,1,2,128]{6,1,5,4,3,2,0:T(4,128)(2,1)S(1)}, u32[]{:S(2)}, u32[]{:S(2)}) %collective-permute-start.9) | collective-permute-done | bytes 196640 | tf_op jit(solution)/shard_map/ppermute | solution.py:15
  121.3 0.6 pad_maximum_fusion.1
  122.3 2.0 %collective-permute-start.10 = (bf16[4,4,4,6,4,1,128]{6,1,5,4,3,2,0:T(4,128)(2,1)S(1)}, bf16[4,4,4,6,4,1,128]{6,1,5,4,3,2,0:T(4,128)(2,1)S(1)}, u32[]{:S(2)}, u32[]{:S(2)}) collective-permute-start(bf16[4,4,4,6,4,1,128]{6,1,5,4,3,2,0:T(4,128)(2,1)S(1)} %get-tuple-element.10), channel_id=1, source_target_pairs={{1,0},{2,1},{3,2},{4,3},{5,4},{6,5},{7,6},{8,7},{9,8},{10,9},{11,1... | collective-permute-start | bytes 1179656 | tf_op jit(solution)/shard_map/ppermute | solution.py:18
  125.3 14.3 %collective-permute-done.11 = bf16[4,4,4,6,4,1,128]{6,1,5,4,3,2,0:T(4,128)(2,1)S(1)} collective-permute-done((bf16[4,4,4,6,4,1,128]{6,1,5,4,3,2,0:T(4,128)(2,1)S(1)}, bf16[4,4,4,6,4,1,128]{6,1,5,4,3,2,0:T(4,128)(2,1)S(1)}, u32[]{:S(2)}, u32[]{:S(2)}) %collective-permute-start.11) | collective-permute-done | bytes 393248 | tf_op jit(solution)/shard_map/ppermute | solution.py:15
  139.6 6.6 %collective-permute-done.10 = bf16[4,4,4,6,4,1,128]{6,1,5,4,3,2,0:T(4,128)(2,1)S(1)} collective-permute-done((bf16[4,4,4,6,4,1,128]{6,1,5,4,3,2,0:T(4,128)(2,1)S(1)}, bf16[4,4,4,6,4,1,128]{6,1,5,4,3,2,0:T(4,128)(2,1)S(1)}, u32[]{:S(2)}, u32[]{:S(2)}) %collective-permute-start.10) | collective-permute-done | bytes 393248 | tf_op jit(solution)/shard_map/ppermute | solution.py:18
  146.2 0.6 pad_maximum_fusion.4
  147.7 0.5 fusion.28
  151.0 10.1 %all_to_all.36 = f32[4,4,2,6,2,2,128]{6,1,5,4,3,2,0:T(4,128)S(1)} all-to-all(f32[4,4,2,6,2,2,128]{6,1,5,4,3,2,0:T(4,128)S(1)} %convert_subtract_fusion), channel_id=1, replica_groups=mesh['sec'=4,'gz'=4,'ta'=16] {'sec'}, dimensions={0} | all-to-all | bytes 786432 | tf_op jit(solution)/shard_map/all_to_all | solution.py:77
  161.2 0.9 copy.28
  (64 shorter events, 13.8 us)
Async XLA Ops:
  1.7 56.8 %all-to-all-start = ((bf16[1,4,8,6,2,2,128]{6,5,4,3,1,0,2:T(2,128)(2,1)}), bf16[1,4,8,6,2,2,128]{6,5,4,3,1,0,2:T(2,128)(2,1)S(1)}, u32[]{:S(2)}, u32[]{:S(2)}) async-start(bf16[1,4,8,6,2,2,128]{6,5,4,3,1,0,2:T(2,128)(2,1)} %bitcast.136), calls=%async_computation | async-start | bytes 393216 | tf_op jit(solution)/shard_map/all_to_all | solution.py:83
  20.6 14.3 %copy-start.1 = (bf16[2,6,2,2,9,64,128]{5,6,3,2,1,0,4:T(8,128)(2,1)S(1)}, bf16[2,6,2,2,9,64,128]{5,6,3,2,1,0,4:T(8,128)(2,1)}, u32[]{:S(2)}) copy-start(bf16[2,6,2,2,9,64,128]{5,6,3,2,1,0,4:T(8,128)(2,1)} %copy.8) | copy-start | bytes 21233668
  58.6 44.9 %copy-start = (bf16[48,9,128,128]{3,2,0,1:T(8,128)(2,1)S(1)}, bf16[48,9,128,128]{3,2,0,1:T(8,128)(2,1)}, u32[]{:S(2)}) copy-start(bf16[48,9,128,128]{3,2,0,1:T(8,128)(2,1)} %maximum_maximum_fusion) | copy-start | bytes 42467332
  58.9 5.5 %collective-permute-start = (bf16[4,4,1,6,2,2,128]{6,1,5,4,3,2,0:T(4,128)(2,1)S(1)}, bf16[4,4,1,6,2,2,128]{6,1,5,4,3,2,0:T(4,128)(2,1)S(1)}, u32[]{:S(2)}, u32[]{:S(2)}) collective-permute-start(bf16[4,4,1,6,2,2,128]{6,1,5,4,3,2,0:T(4,128)(2,1)S(1)} %get-tuple-element.38), channel_id=1, source_target_pairs={{64,0},{128,64},{192,128},{0,192},{65,1},{129,65},{193,129},{1,193... | collective-permute-start | bytes 294920 | tf_op jit(solution)/shard_map/ppermute | solution.py:18
  62.3 5.8 %collective-permute-start.1 = (bf16[4,4,1,6,2,2,128]{6,1,5,4,3,2,0:T(4,128)(2,1)S(1)}, bf16[4,4,1,6,2,2,128]{6,1,5,4,3,2,0:T(4,128)(2,1)S(1)}, u32[]{:S(2)}, u32[]{:S(2)}) collective-permute-start(bf16[4,4,1,6,2,2,128]{6,1,5,4,3,2,0:T(4,128)(2,1)S(1)} %get-tuple-element.37), channel_id=1, source_target_pairs={{0,64},{64,128},{128,192},{192,0},{1,65},{65,129},{129,193},{193,1... | collective-permute-start | bytes 294920 | tf_op jit(solution)/shard_map/ppermute | solution.py:15
  68.5 5.2 %collective-permute-start.2 = (bf16[4,4,4,6,1,2,128]{6,1,5,4,3,2,0:T(4,128)(2,1)S(1)}, bf16[4,4,4,6,1,2,128]{6,1,5,4,3,2,0:T(4,128)(2,1)S(1)}, u32[]{:S(2)}, u32[]{:S(2)}) collective-permute-start(bf16[4,4,4,6,1,2,128]{6,1,5,4,3,2,0:T(4,128)(2,1)S(1)} %get-tuple-element.20), channel_id=1, source_target_pairs={{16,0},{32,16},{48,32},{0,48},{17,1},{33,17},{49,33},{1,49},{18,2}... | collective-permute-start | bytes 589832 | tf_op jit(solution)/shard_map/ppermute | solution.py:18
  68.6 5.9 %collective-permute-start.3 = (bf16[4,4,4,6,1,2,128]{6,1,5,4,3,2,0:T(4,128)(2,1)S(1)}, bf16[4,4,4,6,1,2,128]{6,1,5,4,3,2,0:T(4,128)(2,1)S(1)}, u32[]{:S(2)}, u32[]{:S(2)}) collective-permute-start(bf16[4,4,4,6,1,2,128]{6,1,5,4,3,2,0:T(4,128)(2,1)S(1)} %get-tuple-element.19), channel_id=1, source_target_pairs={{0,16},{16,32},{32,48},{48,0},{1,17},{17,33},{33,49},{49,1},{2,18}... | collective-permute-start | bytes 589832 | tf_op jit(solution)/shard_map/ppermute | solution.py:15
  75.4 21.1 %collective-permute-start.5 = (bf16[4,4,4,6,4,1,128]{6,1,5,4,3,2,0:T(4,128)(2,1)S(1)}, bf16[4,4,4,6,4,1,128]{6,1,5,4,3,2,0:T(4,128)(2,1)S(1)}, u32[]{:S(2)}, u32[]{:S(2)}) collective-permute-start(bf16[4,4,4,6,4,1,128]{6,1,5,4,3,2,0:T(4,128)(2,1)S(1)} %get-tuple-element.13), channel_id=1, source_target_pairs={{0,1},{1,2},{2,3},{3,4},{4,5},{5,6},{6,7},{7,8},{8,9},{9,10},{10,1... | collective-permute-start | bytes 1179656 | tf_op jit(solution)/shard_map/ppermute | solution.py:15
  79.8 22.6 %collective-permute-start.4 = (bf16[4,4,4,6,4,1,128]{6,1,5,4,3,2,0:T(4,128)(2,1)S(1)}, bf16[4,4,4,6,4,1,128]{6,1,5,4,3,2,0:T(4,128)(2,1)S(1)}, u32[]{:S(2)}, u32[]{:S(2)}) collective-permute-start(bf16[4,4,4,6,4,1,128]{6,1,5,4,3,2,0:T(4,128)(2,1)S(1)} %get-tuple-element.14), channel_id=1, source_target_pairs={{1,0},{2,1},{3,2},{4,3},{5,4},{6,5},{7,6},{8,7},{9,8},{10,9},{11,1... | collective-permute-start | bytes 1179656 | tf_op jit(solution)/shard_map/ppermute | solution.py:18
  107.5 4.7 %collective-permute-start.6 = (bf16[4,4,1,6,2,2,128]{6,1,5,4,3,2,0:T(4,128)(2,1)S(1)}, bf16[4,4,1,6,2,2,128]{6,1,5,4,3,2,0:T(4,128)(2,1)S(1)}, u32[]{:S(2)}, u32[]{:S(2)}) collective-permute-start(bf16[4,4,1,6,2,2,128]{6,1,5,4,3,2,0:T(4,128)(2,1)S(1)} %get-tuple-element.32), channel_id=1, source_target_pairs={{64,0},{128,64},{192,128},{0,192},{65,1},{129,65},{193,129},{1,193... | collective-permute-start | bytes 294920 | tf_op jit(solution)/shard_map/ppermute | solution.py:18
  107.6 5.9 %collective-permute-start.7 = (bf16[4,4,1,6,2,2,128]{6,1,5,4,3,2,0:T(4,128)(2,1)S(1)}, bf16[4,4,1,6,2,2,128]{6,1,5,4,3,2,0:T(4,128)(2,1)S(1)}, u32[]{:S(2)}, u32[]{:S(2)}) collective-permute-start(bf16[4,4,1,6,2,2,128]{6,1,5,4,3,2,0:T(4,128)(2,1)S(1)} %get-tuple-element.31), channel_id=1, source_target_pairs={{0,64},{64,128},{128,192},{192,0},{1,65},{65,129},{129,193},{193,1... | collective-permute-start | bytes 294920 | tf_op jit(solution)/shard_map/ppermute | solution.py:15
  113.9 4.4 %collective-permute-start.8 = (bf16[4,4,4,6,1,2,128]{6,1,5,4,3,2,0:T(4,128)(2,1)S(1)}, bf16[4,4,4,6,1,2,128]{6,1,5,4,3,2,0:T(4,128)(2,1)S(1)}, u32[]{:S(2)}, u32[]{:S(2)}) collective-permute-start(bf16[4,4,4,6,1,2,128]{6,1,5,4,3,2,0:T(4,128)(2,1)S(1)} %get-tuple-element.18), channel_id=1, source_target_pairs={{16,0},{32,16},{48,32},{0,48},{17,1},{33,17},{49,33},{1,49},{18,2}... | collective-permute-start | bytes 589832 | tf_op jit(solution)/shard_map/ppermute | solution.py:18
  114.0 7.3 %collective-permute-start.9 = (bf16[4,4,4,6,1,2,128]{6,1,5,4,3,2,0:T(4,128)(2,1)S(1)}, bf16[4,4,4,6,1,2,128]{6,1,5,4,3,2,0:T(4,128)(2,1)S(1)}, u32[]{:S(2)}, u32[]{:S(2)}) collective-permute-start(bf16[4,4,4,6,1,2,128]{6,1,5,4,3,2,0:T(4,128)(2,1)S(1)} %get-tuple-element.17), channel_id=1, source_target_pairs={{0,16},{16,32},{32,48},{48,0},{1,17},{17,33},{33,49},{49,1},{2,18}... | collective-permute-start | bytes 589832 | tf_op jit(solution)/shard_map/ppermute | solution.py:15
  122.2 17.4 %collective-permute-start.11 = (bf16[4,4,4,6,4,1,128]{6,1,5,4,3,2,0:T(4,128)(2,1)S(1)}, bf16[4,4,4,6,4,1,128]{6,1,5,4,3,2,0:T(4,128)(2,1)S(1)}, u32[]{:S(2)}, u32[]{:S(2)}) collective-permute-start(bf16[4,4,4,6,4,1,128]{6,1,5,4,3,2,0:T(4,128)(2,1)S(1)} %get-tuple-element.9), channel_id=1, source_target_pairs={{0,1},{1,2},{2,3},{3,4},{4,5},{5,6},{6,7},{7,8},{8,9},{9,10},{10,1... | collective-permute-start | bytes 1179656 | tf_op jit(solution)/shard_map/ppermute | solution.py:15
  122.3 23.9 %collective-permute-start.10 = (bf16[4,4,4,6,4,1,128]{6,1,5,4,3,2,0:T(4,128)(2,1)S(1)}, bf16[4,4,4,6,4,1,128]{6,1,5,4,3,2,0:T(4,128)(2,1)S(1)}, u32[]{:S(2)}, u32[]{:S(2)}) collective-permute-start(bf16[4,4,4,6,4,1,128]{6,1,5,4,3,2,0:T(4,128)(2,1)S(1)} %get-tuple-element.10), channel_id=1, source_target_pairs={{1,0},{2,1},{3,2},{4,3},{5,4},{6,5},{7,6},{8,7},{9,8},{10,9},{11,1... | collective-permute-start | bytes 1179656 | tf_op jit(solution)/shard_map/ppermute | solution.py:18
where the time goes:
time: 163 us; the launch traced here: 162 us
  waiting for transfers between devices  59.7 us (37%)
  local copies, waits for them, and re-layouts  34 us (21%)
  other arithmetic  28 us (17%)
  starting transfers between devices  17.6 us (11%)
  matrix products  12.3 us (8%)
  blocking collectives  10.1 us (6%)
    ppermute x6, waiting for transfers between devices, extended(): lax.ppermute(lax.slice_in_dim(block, block.shape[dim] - width, None, axis...  37.2 us
    ppermute x6, waiting for transfers between devices, extended(): lax.ppermute(lax.slice_in_dim(block, 0, width, axis=dim), axis, backward)  22.5 us
    concatenate x1, other arithmetic, real_blocks(): return jnp.concatenate([upper, lower], 2)  19.9 us
    unnamed x6, local copies, waits for them, and re-layouts  17.8 us
    transpose x1, local copies, waits for them, and re-layouts, real_blocks(): link_imag = jnp.swapaxes(flat_links[..., components:], -1, -2)  12.6 us
    dot_general x18, matrix products, apply_hops(): jnp.einsum('csn,sno->cso', flat_slice, block_links[:, direction], preferr...  12.3 us
    all_to_all x1, blocking collectives, give_back(): lax.all_to_all(iterate, 'sec', split_axis=0, concat_axis=2, tiled=True)  10.1 us
    ppermute x6, starting transfers between devices, extended(): lax.ppermute(lax.slice_in_dim(block, block.shape[dim] - width, None, axis...  7.57 us
  transfers between devices with their start and end apart: 13, of which 12 were waited for; matrix products, arithmetic and copies ran while one was open for 35% of the time, Pallas kernels for 0%

commit v1 on v0

v1 whole, which is shorter than its diff:
```python
import functools

import jax
import jax.numpy as jnp
from jax import lax
from jax.experimental import pallas as pl
from jax.experimental.pallas import tpu as pltpu
from jax.sharding import PartitionSpec as P

BF = jnp.bfloat16
F32 = jnp.float32
VM = pl.BlockSpec(memory_space=pltpu.VMEM)


def permute(array, axis, shift):
    count = lax.axis_size(axis)
    return lax.ppermute(array, axis, [(i, (i + shift) % count) for i in range(count)])


def exchange(faces):
    moved = []
    for number, face in enumerate(faces):
        axis = ("sec", "gz", "ta")[number // 2]
        moved.append(permute(face, axis, -1 if number % 2 == 0 else 1))
    return moved


def site_of(x, y, z, t, ny):
    return ((x * ny + y) * 2 + z) * 2 + t


def store_faces(faces, value, x, y, z, t, ny):
    faces[0 + x][(y * 2 + z) * 2 + t] = value
    faces[2 + z][(x * ny + y) * 2 + t] = value
    faces[4 + t][(x * ny + y) * 2 + z] = value


def pack_kernel(ny, arrived, v_ref, *rest):
    faces, wide = rest[:6], rest[6]
    columns, sites = arrived.shape[0], arrived.shape[1]
    for c in range(columns):
        wide[c * sites:(c + 1) * sites, :] = arrived[c].astype(F32)
    for x in range(2):
        for y in range(ny):
            for z in range(2):
                for t in range(2):
                    site = site_of(x, y, z, t, ny)
                    value = wide[pl.ds(site, columns, stride=sites), :].astype(BF)
                    v_ref[site] = value
                    store_faces(faces, value, x, y, z, t, ny)


def variants(value):
    wide = value.astype(F32)
    half = wide.shape[-1] // 2
    lane = lax.broadcasted_iota(jnp.int32, wide.shape, 1)
    first = jnp.where(lane < half, wide, -wide)
    second = pltpu.roll(wide, half, 1)
    return jnp.concatenate([first, second], 0).astype(BF)


def hop_kernel(ny, last, links, v_ref, *rest):
    near = rest[:6]
    if last:
        source, out, vv = rest[6:]
    else:
        source = v_ref
        v_out, faces, vv = rest[6], rest[7:13], rest[13]
    sites, columns = v_ref.shape[0], v_ref.shape[1]
    half_sites = sites // 2

    def fill(i, carry):
        vv[i] = variants(v_ref[i])
        return carry

    lax.fori_loop(0, sites, fill, 0, unroll=4)
    for number in range(6):
        def fill_near(i, carry, number=number):
            vv[sites + number * half_sites + i] = variants(near[number][i])
            return carry
        lax.fori_loop(0, half_sites, fill_near, 0, unroll=4)

    def row(y, carry):
        up = jnp.where(y == ny - 1, 0, y + 1)
        down = jnp.where(y == 0, ny - 1, y - 1)
        for x in range(2):
            for z in range(2):
                for t in range(2):
                    site = site_of(x, y, z, t, ny)
                    at_x = sites + (y * 2 + z) * 2 + t
                    at_z = sites + 2 * half_sites + (x * ny + y) * 2 + t
                    at_t = sites + 4 * half_sites + (x * ny + y) * 2 + z
                    other_x = site_of(1 - x, y, z, t, ny)
                    other_z = site_of(x, y, 1 - z, t, ny)
                    other_t = site_of(x, y, z, 1 - t, ny)
                    places = [
                        site,
                        other_x if x == 0 else at_x,
                        other_x if x == 1 else at_x + half_sites,
                        site_of(x, up, z, t, ny),
                        site_of(x, down, z, t, ny),
                        other_z if z == 0 else at_z,
                        other_z if z == 1 else at_z + half_sites,
                        other_t if t == 0 else at_t,
                        other_t if t == 1 else at_t + half_sites,
                    ]
                    vectors = jnp.concatenate([vv[p] for p in places], 1)
                    matrix = jnp.concatenate([links[site, k] for k in range(9)], 1)
                    product = lax.dot_general(
                        vectors, matrix, (((1,), (1,)), ((), ())), preferred_element_type=F32
                    )
                    hop = jnp.concatenate([product[:columns], product[columns:]], 1)
                    value = source[site].astype(F32) - hop
                    if last:
                        out[pl.ds(site, columns, stride=sites), :] = value
                    else:
                        value = value.astype(BF)
                        v_out[site] = value
                        store_faces(faces, value, x, y, z, t, ny)
        return carry

    lax.fori_loop(0, ny, row, 0)


def params():
    return pltpu.CompilerParams(vmem_limit_bytes=40 * 1024 * 1024)


def local(ny, source, coarse_links):
    own, planes = source.shape[0], source.shape[1]
    parts = lax.axis_size("sec")
    width = source.shape[-1]
    sites = planes // parts * ny * 4
    columns = own * parts
    links = coarse_links.reshape((sites,) + coarse_links.shape[4:])
    blocks = source.reshape(own, parts, sites, width)
    arrived = lax.all_to_all(blocks, "sec", split_axis=1, concat_axis=0, tiled=True)
    arrived = arrived.reshape(columns, sites, width)
    whole = jax.ShapeDtypeStruct((sites, columns, width), BF)
    face = jax.ShapeDtypeStruct((sites // 2, columns, width), BF)
    v1, *faces = pl.pallas_call(
        functools.partial(pack_kernel, ny),
        out_shape=[whole] + [face] * 6,
        in_specs=[VM],
        out_specs=[VM] * 7,
        scratch_shapes=[pltpu.VMEM((columns * sites, width), F32)],
        compiler_params=params(),
        name="pack",
    )(arrived)
    scratch = [pltpu.VMEM((sites * 4, 2 * columns, width), BF)]
    cost = pl.CostEstimate(
        flops=2 * 9 * sites * 2 * columns * width * width // 2,
        bytes_accessed=links.size * 2,
        transcendentals=0,
    )
    v2, *faces = pl.pallas_call(
        functools.partial(hop_kernel, ny, False),
        out_shape=[whole] + [face] * 6,
        in_specs=[VM] * 8,
        out_specs=[VM] * 7,
        scratch_shapes=scratch,
        compiler_params=params(),
        cost_estimate=cost,
        name="hop_one",
    )(links, v1, *exchange(faces))
    result = pl.pallas_call(
        functools.partial(hop_kernel, ny, True),
        out_shape=jax.ShapeDtypeStruct((columns * sites, width), F32),
        in_specs=[VM] * 9,
        out_specs=VM,
        scratch_shapes=scratch,
        compiler_params=params(),
        cost_estimate=cost,
        name="hop_two",
    )(links, v2, *exchange(faces), v1)
    result = result.reshape(columns, 1, sites, width)
    result = lax.all_to_all(result, "sec", split_axis=0, concat_axis=1, tiled=True)
    return result.reshape(source.shape)


def solution(mesh):
    def whole(source, coarse_links):
        return jax.shard_map(
            functools.partial(local, source.shape[2]),
            mesh=mesh,
            in_specs=(
                P("sec", None, None, "gz", "ta", None),
                P("sec", None, "gz", "ta", None, None, None),
            ),
            out_specs=P("sec", None, None, "gz", "ta", None),
            check_vma=False,
        )(source, coarse_links)

    return whole
```

time: 163 us -> 77.8 us (0.48)
  the two profiles are of different devices: /device:TPU:102 before, /device:TPU:32 now
where the time goes in v1:
time: 77.8 us; the launch traced here: 77.5 us
  blocking collectives  22.9 us (29%)
  waiting for transfers between devices  19.7 us (25%)
  starting transfers between devices  16.5 us (21%)
  Pallas kernels  13.7 us (18%)
  local copies, waits for them, and re-layouts  4.72 us (6%)
    ppermute x12, waiting for transfers between devices, permute(): lax.ppermute(array, axis, [(i, (i + shift) % count) for i in range(count)])  19.7 us
    ppermute x12, starting transfers between devices, permute(): lax.ppermute(array, axis, [(i, (i + shift) % count) for i in range(count)])  16.5 us
    all_to_all x1, blocking collectives, local(): lax.all_to_all(result, 'sec', split_axis=0, concat_axis=1, tiled=True)  12.3 us
    all_to_all x1, blocking collectives, local(): lax.all_to_all(blocks, 'sec', split_axis=1, concat_axis=0, tiled=True)  10.6 us
    pallas_call x1, Pallas kernels, local(): pl.pallas_call(functools.partial(hop_kernel, ny, False), out_shape=[whole...  6.8 us
    pallas_call x1, Pallas kernels, local(): pl.pallas_call(functools.partial(hop_kernel, ny, True), out_shape=jax.Sha...  6.79 us
    unnamed x2, local copies, waits for them, and re-layouts  3.01 us
  transfers between devices with their start and end apart: 12, of which 6 were waited for; matrix products, arithmetic and copies ran while one was open for 0% of the time, Pallas kernels for 0%

profile of v1, /device:TPU:32, one launch (start us, length us, event | category | flops | bytes accessed | tf_op | source)
XLA Modules:
  0.0 77.5 jit_solution(15100696256012851199)
XLA Ops:
  0.0 0.9 %copy.5 = bf16[4,4,48,128]{3,2,0,1:T(8,128)(2,1)S(1)} copy(bf16[4,4,48,128]{3,2,1,0:T(8,128)(2,1)} %bitcast.19) | data formatting | bytes 393216 | tf_op jit(solution)/shard_map/reshape | solution.py:136
  0.9 10.6 %all_to_all.30 = bf16[4,4,48,128]{3,2,0,1:T(8,128)(2,1)S(1)} all-to-all(bf16[4,4,48,128]{3,2,0,1:T(8,128)(2,1)S(1)} %copy.5), channel_id=1, replica_groups=mesh['sec'=4,'gz'=4,'ta'=16] {'sec'}, dimensions={1} | all-to-all | bytes 393216 | tf_op jit(solution)/shard_map/all_to_all | solution.py:137
  11.5 0.2 pack.1
  11.7 1.2 %collective-permute-start = (bf16[24,16,128]{2,1,0:T(8,128)(2,1)S(1)}, bf16[24,16,128]{2,1,0:T(8,128)(2,1)S(1)}, u32[]{:S(2)}, u32[]{:S(2)}) collective-permute-start(bf16[24,16,128]{2,1,0:T(8,128)(2,1)S(1)} %get-tuple-element.20), channel_id=1, source_target_pairs={{0,192},{64,0},{128,64},{192,128},{1,193},{65,1},{129,65},{193,129... | collective-permute-start | bytes 294920 | tf_op jit(solution)/shard_map/ppermute | solution.py:17
  12.9 0.9 %collective-permute-start.1 = (bf16[24,16,128]{2,1,0:T(8,128)(2,1)S(1)}, bf16[24,16,128]{2,1,0:T(8,128)(2,1)S(1)}, u32[]{:S(2)}, u32[]{:S(2)}) collective-permute-start(bf16[24,16,128]{2,1,0:T(8,128)(2,1)S(1)} %get-tuple-element.21), channel_id=1, source_target_pairs={{0,64},{64,128},{128,192},{192,0},{1,65},{65,129},{129,193},{193,1... | collective-permute-start | bytes 294920 | tf_op jit(solution)/shard_map/ppermute | solution.py:17
  13.8 0.0 collective-permute-start.2
  13.8 0.5 collective-permute-start.3
  14.3 7.6 %collective-permute-start.4 = (bf16[24,16,128]{2,1,0:T(8,128)(2,1)S(1)}, bf16[24,16,128]{2,1,0:T(8,128)(2,1)S(1)}, u32[]{:S(2)}, u32[]{:S(2)}) collective-permute-start(bf16[24,16,128]{2,1,0:T(8,128)(2,1)S(1)} %get-tuple-element.24), channel_id=1, source_target_pairs={{0,15},{1,0},{2,1},{3,2},{4,3},{5,4},{6,5},{7,6},{8,7},{9,8},{10,9... | collective-permute-start | bytes 294920 | tf_op jit(solution)/shard_map/ppermute | solution.py:17
  21.9 0.0 collective-permute-done.rest_0_
  21.9 0.0 collective-permute-start.5
  21.9 0.0 collective-permute-done.1.rest_1_
  21.9 0.0 collective-permute-done.2.rest_2_
  21.9 0.0 collective-permute-done.3.rest_3_
  21.9 3.0 %collective-permute-done.4.rest_4_ = bf16[24,16,128]{2,1,0:T(8,128)(2,1)S(1)} collective-permute-done((bf16[24,16,128]{2,1,0:T(8,128)(2,1)S(1)}, bf16[24,16,128]{2,1,0:T(8,128)(2,1)S(1)}, u32[]{:S(2)}, u32[]{:S(2)}) %collective-permute-start.4) | collective-permute-done | bytes 98336 | tf_op jit(solution)/shard_map/ppermute | solution.py:17
  25.0 6.3 %collective-permute-done.5.rest_5_ = bf16[24,16,128]{2,1,0:T(8,128)(2,1)S(1)} collective-permute-done((bf16[24,16,128]{2,1,0:T(8,128)(2,1)S(1)}, bf16[24,16,128]{2,1,0:T(8,128)(2,1)S(1)}, u32[]{:S(2)}, u32[]{:S(2)}) %collective-permute-start.5) | collective-permute-done | bytes 98336 | tf_op jit(solution)/shard_map/ppermute | solution.py:17
  31.3 3.0 %copy-done = bf16[2,6,2,2,9,64,128]{6,5,4,3,2,1,0:T(8,128)(2,1)S(1)} copy-done((bf16[2,6,2,2,9,64,128]{6,5,4,3,2,1,0:T(8,128)(2,1)S(1)}, bf16[2,6,2,2,9,64,128]{6,5,4,3,2,1,0:T(8,128)(2,1)}, u32[]{:S(2)}) %copy-start) | copy-done | bytes 7077912
  34.3 6.8 %hop_one.1 = (bf16[48,16,128]{2,1,0:T(8,128)(2,1)S(1)}, bf16[24,16,128]{2,1,0:T(8,128)(2,1)S(1)}, bf16[24,16,128]{2,1,0:T(8,128)(2,1)S(1)}, bf16[24,16,128]{2,1,...) custom-call(bf16[48,9,64,128]{3,2,1,0:T(8,128)(2,1)S(1)} %bitcast.14, ...), custom_call_target="tpu_custom_call" | custom-call | flops 226492416 | bytes 7077888 | tf_op jit(solution)/shard_map/hop_one/pallas_call | solution.py:156
  41.1 2.4 %collective-permute-start.6 = (bf16[24,16,128]{2,1,0:T(8,128)(2,1)S(1)}, bf16[24,16,128]{2,1,0:T(8,128)(2,1)S(1)}, u32[]{:S(2)}, u32[]{:S(2)}) collective-permute-start(bf16[24,16,128]{2,1,0:T(8,128)(2,1)S(1)} %get-tuple-element.27), channel_id=1, source_target_pairs={{0,192},{64,0},{128,64},{192,128},{1,193},{65,1},{129,65},{193,129... | collective-permute-start | bytes 294920 | tf_op jit(solution)/shard_map/ppermute | solution.py:17
  43.5 0.0 collective-permute-start.7
  43.5 1.8 %collective-permute-start.8 = (bf16[24,16,128]{2,1,0:T(8,128)(2,1)S(1)}, bf16[24,16,128]{2,1,0:T(8,128)(2,1)S(1)}, u32[]{:S(2)}, u32[]{:S(2)}) collective-permute-start(bf16[24,16,128]{2,1,0:T(8,128)(2,1)S(1)} %get-tuple-element.29), channel_id=1, source_target_pairs={{0,48},{16,0},{32,16},{48,32},{1,49},{17,1},{33,17},{49,33},{2,50}... | collective-permute-start | bytes 294920 | tf_op jit(solution)/shard_map/ppermute | solution.py:17
  45.3 0.0 collective-permute-start.9
  45.4 0.6 collective-permute-start.10
  45.9 0.0 collective-permute-done.6.rest_0_
  45.9 1.5 %collective-permute-start.11 = (bf16[24,16,128]{2,1,0:T(8,128)(2,1)S(1)}, bf16[24,16,128]{2,1,0:T(8,128)(2,1)S(1)}, u32[]{:S(2)}, u32[]{:S(2)}) collective-permute-start(bf16[24,16,128]{2,1,0:T(8,128)(2,1)S(1)} %get-tuple-element.32), channel_id=1, source_target_pairs={{0,1},{1,2},{2,3},{3,4},{4,5},{5,6},{6,7},{7,8},{8,9},{9,10},{10,1... | collective-permute-start | bytes 294920 | tf_op jit(solution)/shard_map/ppermute | solution.py:17
  47.4 2.0 %collective-permute-done.7.rest_1_ = bf16[24,16,128]{2,1,0:T(8,128)(2,1)S(1)} collective-permute-done((bf16[24,16,128]{2,1,0:T(8,128)(2,1)S(1)}, bf16[24,16,128]{2,1,0:T(8,128)(2,1)S(1)}, u32[]{:S(2)}, u32[]{:S(2)}) %collective-permute-start.7) | collective-permute-done | bytes 98336 | tf_op jit(solution)/shard_map/ppermute | solution.py:17
  49.3 0.0 collective-permute-done.8.rest_2_
  49.4 0.4 collective-permute-done.9.rest_3_
  49.7 1.2 %collective-permute-done.10.rest_4_ = bf16[24,16,128]{2,1,0:T(8,128)(2,1)S(1)} collective-permute-done((bf16[24,16,128]{2,1,0:T(8,128)(2,1)S(1)}, bf16[24,16,128]{2,1,0:T(8,128)(2,1)S(1)}, u32[]{:S(2)}, u32[]{:S(2)}) %collective-permute-start.10) | collective-permute-done | bytes 98336 | tf_op jit(solution)/shard_map/ppermute | solution.py:17
  50.9 6.8 %collective-permute-done.11.rest_5_ = bf16[24,16,128]{2,1,0:T(8,128)(2,1)S(1)} collective-permute-done((bf16[24,16,128]{2,1,0:T(8,128)(2,1)S(1)}, bf16[24,16,128]{2,1,0:T(8,128)(2,1)S(1)}, u32[]{:S(2)}, u32[]{:S(2)}) %collective-permute-start.11) | collective-permute-done | bytes 98336 | tf_op jit(solution)/shard_map/ppermute | solution.py:17
  57.7 6.8 %hop_two.1 = f32[768,128]{1,0:T(8,128)S(1)} custom-call(bf16[48,9,64,128]{3,2,1,0:T(8,128)(2,1)S(1)} %bitcast.15, bf16[48,16,128]{2,1,0:T(8,128)(2,1)S(1)} %get-tuple-element.26.v_ref, bf16[24,16,128]{2,1,0:T(8,128)(2,1)S(1)} %collective-permute-done.6.rest_0_, bf16[24,16,128]{2,1,0:T(8,128)(2,1)S(1)} %collective-permute-done.7.rest_1_, ...), custom_call_target="tpu_custom_call" | custom-call | flops 226492416 | bytes 7077888 | tf_op jit(solution)/shard_map/hop_two/pallas_call | solution.py:166
  64.5 12.3 %all_to_all.31 = f32[16,1,48,128]{3,2,1,0:T(8,128)S(1)} all-to-all(f32[16,1,48,128]{3,2,1,0:T(8,128)S(1)} %bitcast.16), channel_id=1, replica_groups=mesh['sec'=4,'gz'=4,'ta'=16] {'sec'}, dimensions={0} | all-to-all | bytes 786432 | tf_op jit(solution)/shard_map/all_to_all | solution.py:177
  76.8 0.8 copy.7
  (1 shorter events, 0.0 us)
Async XLA Ops:
  11.7 10.2 %collective-permute-start = (bf16[24,16,128]{2,1,0:T(8,128)(2,1)S(1)}, bf16[24,16,128]{2,1,0:T(8,128)(2,1)S(1)}, u32[]{:S(2)}, u32[]{:S(2)}) collective-permute-start(bf16[24,16,128]{2,1,0:T(8,128)(2,1)S(1)} %get-tuple-element.20), channel_id=1, source_target_pairs={{0,192},{64,0},{128,64},{192,128},{1,193},{65,1},{129,65},{193,129... | collective-permute-start | bytes 294920 | tf_op jit(solution)/shard_map/ppermute | solution.py:17
  12.9 9.0 %collective-permute-start.1 = (bf16[24,16,128]{2,1,0:T(8,128)(2,1)S(1)}, bf16[24,16,128]{2,1,0:T(8,128)(2,1)S(1)}, u32[]{:S(2)}, u32[]{:S(2)}) collective-permute-start(bf16[24,16,128]{2,1,0:T(8,128)(2,1)S(1)} %get-tuple-element.21), channel_id=1, source_target_pairs={{0,64},{64,128},{128,192},{192,0},{1,65},{65,129},{129,193},{193,1... | collective-permute-start | bytes 294920 | tf_op jit(solution)/shard_map/ppermute | solution.py:17
  13.8 8.1 %collective-permute-start.2 = (bf16[24,16,128]{2,1,0:T(8,128)(2,1)S(1)}, bf16[24,16,128]{2,1,0:T(8,128)(2,1)S(1)}, u32[]{:S(2)}, u32[]{:S(2)}) collective-permute-start(bf16[24,16,128]{2,1,0:T(8,128)(2,1)S(1)} %get-tuple-element.22), channel_id=1, source_target_pairs={{0,48},{16,0},{32,16},{48,32},{1,49},{17,1},{33,17},{49,33},{2,50}... | collective-permute-start | bytes 294920 | tf_op jit(solution)/shard_map/ppermute | solution.py:17
  13.8 8.1 %collective-permute-start.3 = (bf16[24,16,128]{2,1,0:T(8,128)(2,1)S(1)}, bf16[24,16,128]{2,1,0:T(8,128)(2,1)S(1)}, u32[]{:S(2)}, u32[]{:S(2)}) collective-permute-start(bf16[24,16,128]{2,1,0:T(8,128)(2,1)S(1)} %get-tuple-element.23), channel_id=1, source_target_pairs={{0,16},{16,32},{32,48},{48,0},{1,17},{17,33},{33,49},{49,1},{2,18}... | collective-permute-start | bytes 294920 | tf_op jit(solution)/shard_map/ppermute | solution.py:17
  14.3 10.6 %collective-permute-start.4 = (bf16[24,16,128]{2,1,0:T(8,128)(2,1)S(1)}, bf16[24,16,128]{2,1,0:T(8,128)(2,1)S(1)}, u32[]{:S(2)}, u32[]{:S(2)}) collective-permute-start(bf16[24,16,128]{2,1,0:T(8,128)(2,1)S(1)} %get-tuple-element.24), channel_id=1, source_target_pairs={{0,15},{1,0},{2,1},{3,2},{4,3},{5,4},{6,5},{7,6},{8,7},{9,8},{10,9... | collective-permute-start | bytes 294920 | tf_op jit(solution)/shard_map/ppermute | solution.py:17
  21.9 9.4 %collective-permute-start.5 = (bf16[24,16,128]{2,1,0:T(8,128)(2,1)S(1)}, bf16[24,16,128]{2,1,0:T(8,128)(2,1)S(1)}, u32[]{:S(2)}, u32[]{:S(2)}) collective-permute-start(bf16[24,16,128]{2,1,0:T(8,128)(2,1)S(1)} %get-tuple-element.25), channel_id=1, source_target_pairs={{0,1},{1,2},{2,3},{3,4},{4,5},{5,6},{6,7},{7,8},{8,9},{9,10},{10,1... | collective-permute-start | bytes 294920 | tf_op jit(solution)/shard_map/ppermute | solution.py:17
  31.3 3.0 %copy-start = (bf16[2,6,2,2,9,64,128]{6,5,4,3,2,1,0:T(8,128)(2,1)S(1)}, bf16[2,6,2,2,9,64,128]{6,5,4,3,2,1,0:T(8,128)(2,1)}, u32[]{:S(2)}) copy-start(bf16[2,6,2,2,9,64,128]{6,5,4,3,2,1,0:T(8,128)(2,1)} %param.3) | copy-start | bytes 21233668
  41.1 4.8 %collective-permute-start.6 = (bf16[24,16,128]{2,1,0:T(8,128)(2,1)S(1)}, bf16[24,16,128]{2,1,0:T(8,128)(2,1)S(1)}, u32[]{:S(2)}, u32[]{:S(2)}) collective-permute-start(bf16[24,16,128]{2,1,0:T(8,128)(2,1)S(1)} %get-tuple-element.27), channel_id=1, source_target_pairs={{0,192},{64,0},{128,64},{192,128},{1,193},{65,1},{129,65},{193,129... | collective-permute-start | bytes 294920 | tf_op jit(solution)/shard_map/ppermute | solution.py:17
  43.5 5.8 %collective-permute-start.7 = (bf16[24,16,128]{2,1,0:T(8,128)(2,1)S(1)}, bf16[24,16,128]{2,1,0:T(8,128)(2,1)S(1)}, u32[]{:S(2)}, u32[]{:S(2)}) collective-permute-start(bf16[24,16,128]{2,1,0:T(8,128)(2,1)S(1)} %get-tuple-element.28), channel_id=1, source_target_pairs={{0,64},{64,128},{128,192},{192,0},{1,65},{65,129},{129,193},{193,1... | collective-permute-start | bytes 294920 | tf_op jit(solution)/shard_map/ppermute | solution.py:17
  43.5 5.8 %collective-permute-start.8 = (bf16[24,16,128]{2,1,0:T(8,128)(2,1)S(1)}, bf16[24,16,128]{2,1,0:T(8,128)(2,1)S(1)}, u32[]{:S(2)}, u32[]{:S(2)}) collective-permute-start(bf16[24,16,128]{2,1,0:T(8,128)(2,1)S(1)} %get-tuple-element.29), channel_id=1, source_target_pairs={{0,48},{16,0},{32,16},{48,32},{1,49},{17,1},{33,17},{49,33},{2,50}... | collective-permute-start | bytes 294920 | tf_op jit(solution)/shard_map/ppermute | solution.py:17
  45.3 4.4 %collective-permute-start.9 = (bf16[24,16,128]{2,1,0:T(8,128)(2,1)S(1)}, bf16[24,16,128]{2,1,0:T(8,128)(2,1)S(1)}, u32[]{:S(2)}, u32[]{:S(2)}) collective-permute-start(bf16[24,16,128]{2,1,0:T(8,128)(2,1)S(1)} %get-tuple-element.30), channel_id=1, source_target_pairs={{0,16},{16,32},{32,48},{48,0},{1,17},{17,33},{33,49},{49,1},{2,18}... | collective-permute-start | bytes 294920 | tf_op jit(solution)/shard_map/ppermute | solution.py:17
  45.4 5.5 %collective-permute-start.10 = (bf16[24,16,128]{2,1,0:T(8,128)(2,1)S(1)}, bf16[24,16,128]{2,1,0:T(8,128)(2,1)S(1)}, u32[]{:S(2)}, u32[]{:S(2)}) collective-permute-start(bf16[24,16,128]{2,1,0:T(8,128)(2,1)S(1)} %get-tuple-element.31), channel_id=1, source_target_pairs={{0,15},{1,0},{2,1},{3,2},{4,3},{5,4},{6,5},{7,6},{8,7},{9,8},{10,9... | collective-permute-start | bytes 294920 | tf_op jit(solution)/shard_map/ppermute | solution.py:17
  45.9 11.8 %collective-permute-start.11 = (bf16[24,16,128]{2,1,0:T(8,128)(2,1)S(1)}, bf16[24,16,128]{2,1,0:T(8,128)(2,1)S(1)}, u32[]{:S(2)}, u32[]{:S(2)}) collective-permute-start(bf16[24,16,128]{2,1,0:T(8,128)(2,1)S(1)} %get-tuple-element.32), channel_id=1, source_target_pairs={{0,1},{1,2},{2,3},{3,4},{4,5},{5,6},{6,7},{7,8},{8,9},{9,10},{10,1... | collective-permute-start | bytes 294920 | tf_op jit(solution)/shard_map/ppermute | solution.py:17

commit v2 on v1

v2 whole, which is shorter than its diff:
```python
import functools

import jax
import jax.numpy as jnp
from jax import lax
from jax.experimental import pallas as pl
from jax.experimental.pallas import tpu as pltpu
from jax.sharding import PartitionSpec as P

BF = jnp.bfloat16
F32 = jnp.float32
VM = pl.BlockSpec(memory_space=pltpu.VMEM)
HBM = pl.BlockSpec(memory_space=pl.ANY)
AXES = ("sec", "gz", "ta")


def swap(array, axis, distance):
    count = lax.axis_size(axis)
    return lax.ppermute(array, axis, [(i, i ^ distance) for i in range(count)])


def swap_other(array, axis):
    count = lax.axis_size(axis)
    pairs = [(i, (i + (1 if i % 2 else count - 1)) % count) for i in range(count)]
    return lax.ppermute(array, axis, pairs)


def exchange(faces):
    late = swap_other(faces[5], "ta")
    t_near = swap(faces[4], "ta", 1)
    x_far = swap_other(faces[1], "sec")
    x_near = swap(faces[0], "sec", 1)
    z_far = swap_other(faces[3], "gz")
    z_near = swap(faces[2], "gz", 1)
    return [x_near, x_far, z_near, z_far, t_near], late


def parities():
    return [lax.rem(lax.axis_index(axis), 2) for axis in AXES]


def site_of(x, y, z, t, ny):
    return ((x * ny + y) * 2 + z) * 2 + t


def face_sites(axis, coordinate, i, ny):
    if axis == 0:
        return coordinate * ny * 4 + i
    if axis == 1:
        return (i // 2) * 4 + coordinate * 2 + i % 2
    return i * 2 + coordinate


def write_faces(ny, v_ref, faces):
    odd = parities()
    for axis in range(3):
        for i in range(ny * 4):
            faces[2 * axis][i] = v_ref[face_sites(axis, 1 - odd[axis], i, ny)]
            faces[2 * axis + 1][i] = v_ref[face_sites(axis, odd[axis], i, ny)]


def variants(value):
    wide = value.astype(F32)
    half = wide.shape[-1] // 2
    lane = lax.broadcasted_iota(jnp.int32, wide.shape, 1)
    first = jnp.where(lane < half, wide, -wide)
    second = pltpu.roll(wide, half, 1)
    return jnp.concatenate([first, second], 0).astype(BF)


def fill(target, at, source, count):
    def one(i, carry):
        target[at + i] = variants(source[i])
        return carry

    lax.fori_loop(0, count, one, 0, unroll=8)


def product(vectors, matrices):
    columns = vectors[0].shape[0] // 2
    both = lax.dot_general(
        jnp.concatenate(vectors, 1),
        jnp.concatenate(matrices, 1),
        (((1,), (1,)), ((), ())),
        preferred_element_type=F32,
    )
    return jnp.concatenate([both[:columns], both[columns:]], 1)


def split_kernel(source, *rest):
    outs, sems = rest[:-1], rest[-1]
    me = lax.axis_index("sec")
    copies = []
    for k, out in enumerate(outs):
        copies.append(pltpu.make_async_copy(source.at[:, me ^ k], out, sems.at[k]))
        copies[-1].start()
    for copy in copies:
        copy.wait()


def join_kernel(*refs):
    parts, out, sems = refs[:-2], refs[-2], refs[-1]
    me = lax.axis_index("sec")
    copies = []
    for k, part in enumerate(parts):
        copies.append(pltpu.make_async_copy(part, out.at[:, me ^ k], sems.at[k]))
        copies[-1].start()
    for copy in copies:
        copy.wait()


def pack_kernel(ny, parts, *refs):
    blocks, v_ref, faces, wide = refs[:parts], refs[parts], refs[parts + 1:parts + 7], refs[-1]
    own, sites = blocks[0].shape[0], blocks[0].shape[1]
    me = lax.axis_index("sec")
    for k in range(parts):
        at = (me ^ k) * (own * sites)
        for c in range(own):
            start = pl.multiple_of(at + c * sites, 8)
            wide[pl.ds(start, sites), :] = blocks[k][c].astype(F32)
    for site in range(sites):
        v_ref[site] = wide[pl.ds(site, own * parts, stride=sites), :].astype(BF)
    write_faces(ny, v_ref, faces)


def local_kernel(ny, links, v_ref, source, total, vv):
    sites = v_ref.shape[0]
    fill(vv, 0, v_ref, sites)

    def row(y, carry):
        up = jnp.where(y == ny - 1, 0, y + 1)
        down = jnp.where(y == 0, ny - 1, y - 1)
        for x in range(2):
            for z in range(2):
                for t in range(2):
                    site = site_of(x, y, z, t, ny)
                    terms = [
                        (0, site),
                        (1 + x, site_of(1 - x, y, z, t, ny)),
                        (3, site_of(x, up, z, t, ny)),
                        (4, site_of(x, down, z, t, ny)),
                        (5 + z, site_of(x, y, 1 - z, t, ny)),
                        (7 + t, site_of(x, y, z, 1 - t, ny)),
                    ]
                    hop = product([vv[p] for _, p in terms], [links[site, k] for k, _ in terms])
                    total[site] = source[site].astype(F32) - hop
        return carry

    lax.fori_loop(0, ny, row, 0)


def near_kernel(ny, links, total, *refs):
    near, out, vv = refs[:5], refs[5], refs[6]
    half = near[0].shape[0]
    odd = parities()
    for number in range(5):
        fill(vv, number * half, near[number], half)

    def row(y, carry):
        for side_x in range(2):
            x = 1 - odd[0] if side_x == 0 else odd[0]
            link_x = 1 + (odd[0] if side_x == 0 else 1 - odd[0])
            for side_z in range(2):
                z = 1 - odd[1] if side_z == 0 else odd[1]
                link_z = 5 + (odd[1] if side_z == 0 else 1 - odd[1])
                for side_t in range(2):
                    t = 1 - odd[2] if side_t == 0 else odd[2]
                    site = site_of(x, y, z, t, ny)
                    terms = [
                        (link_x, side_x * half + (y * 2 + z) * 2 + t),
                        (link_z, (2 + side_z) * half + (x * ny + y) * 2 + t),
                    ]
                    if side_t == 0:
                        terms.append((7 + odd[2], 4 * half + (x * ny + y) * 2 + z))
                    hop = product([vv[p] for _, p in terms], [links[site, k] for k, _ in terms])
                    out[site] = total[site] - hop
        return carry

    lax.fori_loop(0, ny, row, 0)


def late_terms(links, late, total, store):
    odd = parities()[2]
    for i in range(late.shape[0]):
        site = i * 2 + odd
        hop = product([variants(late[i])], [links[site, 8 - odd]])
        store(site, total[site] - hop)
        store(i * 2 + 1 - odd, total[i * 2 + 1 - odd])


def late_kernel(ny, links, late, total, v_ref, *faces):
    def store(site, value):
        v_ref[site] = value.astype(BF)

    late_terms(links, late, total, store)
    write_faces(ny, v_ref, faces)


def last_kernel(ny, links, late, total, *refs):
    outs, wide = refs[:-1], refs[-1]
    own, sites = outs[0].shape[0], outs[0].shape[1]
    columns = own * len(outs)

    def store(site, value):
        wide[pl.ds(site, columns, stride=sites), :] = value

    late_terms(links, late, total, store)
    me = lax.axis_index("sec")
    for k, out in enumerate(outs):
        at = (me ^ k) * (own * sites)
        for c in range(own):
            start = pl.multiple_of(at + c * sites, 8)
            out[c] = wide[pl.ds(start, sites), :]


def call(kernel, name, out_shape, inputs, scratch, flops=0, bytes_accessed=0, places=None, out_place=VM):
    several = isinstance(out_shape, list)
    return pl.pallas_call(
        kernel,
        out_shape=out_shape,
        in_specs=places or [VM] * len(inputs),
        out_specs=[out_place] * len(out_shape) if several else out_place,
        scratch_shapes=scratch,
        compiler_params=pltpu.CompilerParams(vmem_limit_bytes=40 * 1024 * 1024),
        cost_estimate=pl.CostEstimate(
            flops=flops, bytes_accessed=bytes_accessed, transcendentals=0
        ),
        name=name,
    )(*inputs)


def local(ny, source, coarse_links):
    own, planes = source.shape[0], source.shape[1]
    parts = lax.axis_size("sec")
    width = source.shape[-1]
    sites = planes // parts * ny * 4
    columns = own * parts
    half = sites // 2
    links = coarse_links.reshape((sites,) + coarse_links.shape[4:])
    shape = jax.ShapeDtypeStruct
    whole = shape((sites, columns, width), BF)
    total_shape = shape((sites, columns, width), F32)
    face = shape((half, columns, width), BF)
    block = shape((own, sites, width), BF)
    wide = pltpu.VMEM((columns * sites, width), F32)
    sems = pltpu.SemaphoreType.DMA((parts,))
    per_term = 2 * sites * 2 * columns * width * width // 2
    link_bytes = links.size * 2 // 9

    blocks = call(
        split_kernel, "split", [block] * parts, [source.reshape(own, parts, sites, width)],
        [sems], bytes_accessed=source.size * 4, places=[HBM],
    )
    blocks = [blocks[0]] + [swap(blocks[k], "sec", k) for k in range(1, parts)]
    v, *faces = call(
        functools.partial(pack_kernel, ny, parts), "pack", [whole] + [face] * 6, blocks,
        [wide], bytes_accessed=source.size * 8,
    )
    first = v
    for sweep in range(2):
        near, late = exchange(faces)
        total = call(
            functools.partial(local_kernel, ny), "local", total_shape, [links, v, first],
            [pltpu.VMEM((sites, 2 * columns, width), BF)],
            flops=6 * per_term, bytes_accessed=6 * link_bytes,
        )
        total = call(
            functools.partial(near_kernel, ny), "near", total_shape, [links, total] + near,
            [pltpu.VMEM((5 * half, 2 * columns, width), BF)],
            flops=5 * per_term // 2, bytes_accessed=5 * link_bytes // 2,
        )
        if sweep == 0:
            v, *faces = call(
                functools.partial(late_kernel, ny), "late", [whole] + [face] * 6,
                [links, late, total], [],
                flops=per_term // 2, bytes_accessed=link_bytes // 2,
            )
        else:
            result = call(
                functools.partial(last_kernel, ny), "last",
                [shape((own, sites, width), F32)] * parts, [links, late, total], [wide],
                flops=per_term // 2, bytes_accessed=link_bytes // 2,
            )
    result = [result[0]] + [swap(result[k], "sec", k) for k in range(1, parts)]
    joined = call(
        join_kernel, "join", shape((own, parts, sites, width), F32), result, [sems],
        bytes_accessed=source.size * 8, out_place=HBM,
    )
    return joined.reshape(source.shape)


def solution(mesh):
    def whole(source, coarse_links):
        return jax.shard_map(
            functools.partial(local, source.shape[2]),
            mesh=mesh,
            in_specs=(
                P("sec", None, None, "gz", "ta", None),
                P("sec", None, "gz", "ta", None, None, None),
            ),
            out_specs=P("sec", None, None, "gz", "ta", None),
            check_vma=False,
        )(source, coarse_links)

    return whole
```

time: 77.8 us -> 57.3 us (0.74)
  blocking collectives: 22.9 us -> 0 us
  starting transfers between devices: 16.5 us -> 23.3 us
  waiting for transfers between devices: 19.7 us -> 16 us
    all_to_all x2 -> x0, blocking collectives: 22.9 us -> none  [the longest x1 12.3 us: local(): lax.all_to_all(result, 'sec', split_axis=0, concat_axis=1, tiled=True)]
    ppermute x12 -> x18, starting transfers between devices: 16.5 us -> 23.3 us  [the longest x6 13.3 us: swap_other(): return lax.ppermute(array, axis, pairs)]
    ppermute x12 -> x18, waiting for transfers between devices: 19.7 us -> 16 us  [the longest x12 12.3 us: swap(): return lax.ppermute(array, axis, [(i, i ^ distance) for i in range(count)])]
    unnamed x2 -> x6, local copies, waits for them, and re-layouts: 3.01 us -> 3.98 us
    reshape x1 -> x0, local copies, waits for them, and re-layouts: 0.94 us -> none  [local(): blocks = source.reshape(own, parts, sites, width)]
    pallas_call x3 -> x9, Pallas kernels: 13.7 us -> 13.7 us  [call(): pl.pallas_call(kernel, out_shape=out_shape, in_specs=places or [VM] * len...]
  transfers between devices with their start and end apart: 12 -> 18, of which waited for: 6 -> 7; matrix products, arithmetic and copies ran while one was open for 0% -> 0% of each run, Pallas kernels for 0% -> 21%
where the time goes in v2:
time: 57.3 us; the launch traced here: 57.1 us
  starting transfers between devices  23.3 us (41%)
  waiting for transfers between devices  16 us (28%)
  Pallas kernels  13.7 us (24%)
  local copies, waits for them, and re-layouts  3.98 us (7%)
    pallas_call x9, Pallas kernels, call(): pl.pallas_call(kernel, out_shape=out_shape, in_specs=places or [VM] * len...  13.7 us
    ppermute x6, starting transfers between devices, swap_other(): return lax.ppermute(array, axis, pairs)  13.3 us
    ppermute x12, waiting for transfers between devices, swap(): return lax.ppermute(array, axis, [(i, i ^ distance) for i in range(count)])  12.3 us
    ppermute x12, starting transfers between devices, swap(): return lax.ppermute(array, axis, [(i, i ^ distance) for i in range(count)])  10.1 us
    unnamed x6, local copies, waits for them, and re-layouts  3.98 us
    ppermute x6, waiting for transfers between devices, swap_other(): return lax.ppermute(array, axis, pairs)  3.69 us
  transfers between devices with their start and end apart: 18, of which 7 were waited for; matrix products, arithmetic and copies ran while one was open for 0% of the time, Pallas kernels for 21%

profile of v2, /device:TPU:32, one launch (start us, length us, event | category | flops | bytes accessed | tf_op | source)
XLA Modules:
  0.0 57.1 jit_solution(1089626947789173093)
XLA Ops:
  0.0 0.9 %copy-done.2 = bf16[4,8,6,2,2,128]{5,4,3,2,1,0:T(2,128)(2,1)S(1)} copy-done((bf16[4,8,6,2,2,128]{5,4,3,2,1,0:T(2,128)(2,1)S(1)}, bf16[4,8,6,2,2,128]{5,4,3,2,1,0:T(2,128)(2,1)}, u32[]{:S(2)}) %copy-start.2) | copy-done | bytes 196632
  0.9 0.1 split.1
  1.0 1.7 %collective-permute-start = (bf16[4,48,128]{2,1,0:T(8,128)(2,1)S(1)}, bf16[4,48,128]{2,1,0:T(8,128)(2,1)S(1)}, u32[]{:S(2)}, u32[]{:S(2)}) collective-permute-start(bf16[4,48,128]{2,1,0:T(8,128)(2,1)S(1)} %get-tuple-element.28), channel_id=1, source_target_pairs={{0,64},{64,0},{128,192},{192,128},{1,65},{65,1},{129,193},{193,129... | collective-permute-start | bytes 147464 | tf_op jit(solution)/shard_map/ppermute | solution.py:19
  2.7 2.9 %collective-permute-start.1 = (bf16[4,48,128]{2,1,0:T(8,128)(2,1)S(1)}, bf16[4,48,128]{2,1,0:T(8,128)(2,1)S(1)}, u32[]{:S(2)}, u32[]{:S(2)}) collective-permute-start(bf16[4,48,128]{2,1,0:T(8,128)(2,1)S(1)} %get-tuple-element.29), channel_id=1, source_target_pairs={{0,128},{64,192},{128,0},{192,64},{1,129},{65,193},{129,1},{193,65... | collective-permute-start | bytes 147464 | tf_op jit(solution)/shard_map/ppermute | solution.py:19
  5.6 0.2 collective-permute-start.2
  5.8 2.5 %collective-permute-done.1.refs_2_ = bf16[4,48,128]{2,1,0:T(8,128)(2,1)S(1)} collective-permute-done((bf16[4,48,128]{2,1,0:T(8,128)(2,1)S(1)}, bf16[4,48,128]{2,1,0:T(8,128)(2,1)S(1)}, u32[]{:S(2)}, u32[]{:S(2)}) %collective-permute-start.1) | collective-permute-done | bytes 49184 | tf_op jit(solution)/shard_map/ppermute | solution.py:19
  8.3 2.6 %collective-permute-done.2.refs_3_ = bf16[4,48,128]{2,1,0:T(8,128)(2,1)S(1)} collective-permute-done((bf16[4,48,128]{2,1,0:T(8,128)(2,1)S(1)}, bf16[4,48,128]{2,1,0:T(8,128)(2,1)S(1)}, u32[]{:S(2)}, u32[]{:S(2)}) %collective-permute-start.2) | collective-permute-done | bytes 49184 | tf_op jit(solution)/shard_map/ppermute | solution.py:19
  10.9 0.2 pack.1
  11.1 0.1 collective-permute-start.4
  11.2 0.8 %collective-permute-start.5 = (bf16[24,16,128]{2,1,0:T(8,128)(2,1)S(1)}, bf16[24,16,128]{2,1,0:T(8,128)(2,1)S(1)}, u32[]{:S(2)}, u32[]{:S(2)}) collective-permute-start(bf16[24,16,128]{2,1,0:T(8,128)(2,1)S(1)} %get-tuple-element.34), channel_id=1, source_target_pairs={{0,192},{64,128},{128,64},{192,0},{1,193},{65,129},{129,65},{193,1... | collective-permute-start | bytes 294920 | tf_op jit(solution)/shard_map/ppermute | solution.py:25
  12.1 1.4 %collective-permute-start.7 = (bf16[24,16,128]{2,1,0:T(8,128)(2,1)S(1)}, bf16[24,16,128]{2,1,0:T(8,128)(2,1)S(1)}, u32[]{:S(2)}, u32[]{:S(2)}) collective-permute-start(bf16[24,16,128]{2,1,0:T(8,128)(2,1)S(1)} %get-tuple-element.36), channel_id=1, source_target_pairs={{0,48},{16,32},{32,16},{48,0},{1,49},{17,33},{33,17},{49,1},{2,50}... | collective-permute-start | bytes 294920 | tf_op jit(solution)/shard_map/ppermute | solution.py:25
  13.5 0.3 collective-permute-start.8
  13.8 2.0 %collective-permute-done.4.refs_0_ = bf16[24,16,128]{2,1,0:T(8,128)(2,1)S(1)} collective-permute-done((bf16[24,16,128]{2,1,0:T(8,128)(2,1)S(1)}, bf16[24,16,128]{2,1,0:T(8,128)(2,1)S(1)}, u32[]{:S(2)}, u32[]{:S(2)}) %collective-permute-start.4) | collective-permute-done | bytes 98336 | tf_op jit(solution)/shard_map/ppermute | solution.py:19
  15.8 7.6 %collective-permute-start.3 = (bf16[24,16,128]{2,1,0:T(8,128)(2,1)S(1)}, bf16[24,16,128]{2,1,0:T(8,128)(2,1)S(1)}, u32[]{:S(2)}, u32[]{:S(2)}) collective-permute-start(bf16[24,16,128]{2,1,0:T(8,128)(2,1)S(1)} %get-tuple-element.31), channel_id=1, source_target_pairs={{0,15},{1,2},{2,1},{3,4},{4,3},{5,6},{6,5},{7,8},{8,7},{9,10},{10,... | collective-permute-start | bytes 294920 | tf_op jit(solution)/shard_map/ppermute | solution.py:25
  23.4 3.0 %copy-done = bf16[2,6,2,2,9,64,128]{6,5,4,3,2,1,0:T(8,128)(2,1)S(1)} copy-done((bf16[2,6,2,2,9,64,128]{6,5,4,3,2,1,0:T(8,128)(2,1)S(1)}, bf16[2,6,2,2,9,64,128]{6,5,4,3,2,1,0:T(8,128)(2,1)}, u32[]{:S(2)}) %copy-start) | copy-done | bytes 7077912
  26.4 2.9 %local.2.total = f32[48,16,128]{2,1,0:T(8,128)S(1)} custom-call(bf16[48,9,64,128]{3,2,1,0:T(8,128)(2,1)S(1)} %bitcast.3, bf16[48,16,128]{2,1,0:T(8,128)(2,1)S(1)} %get-tuple-element.32.v_ref.source, bf16[48,16,128]{2,1,0:T(8,128)(2,1)S(1)} %get-tuple-element.32.v_ref.source), custom_call_target="tpu_custom_call" | custom-call | flops 150994944 | bytes 4718592 | tf_op jit(solution)/shard_map/local/pallas_call | solution.py:218
  29.4 2.9 %near.2.total = f32[48,16,128]{2,1,0:T(8,128)S(1)} custom-call(bf16[48,9,64,128]{3,2,1,0:T(8,128)(2,1)S(1)} %bitcast.4, f32[48,16,128]{2,1,0:T(8,128)S(1)} %local.2.total, bf16[24,16,128]{2,1,0:T(8,128)(2,1)S(1)} %collective-permute-done.4.refs_0_, bf16[24,16,128]{2,1,0:T(8,128)(2,1)S(1)} %collective-permute-done.5.refs_1_, ...), custom_call_target="tpu_custom_call" | custom-call | flops 62914560 | bytes 1966080 | tf_op jit(solution)/shard_map/near/pallas_call | solution.py:218
  32.4 0.5 late.1
  32.9 2.0 %collective-permute-start.11 = (bf16[24,16,128]{2,1,0:T(8,128)(2,1)S(1)}, bf16[24,16,128]{2,1,0:T(8,128)(2,1)S(1)}, u32[]{:S(2)}, u32[]{:S(2)}) collective-permute-start(bf16[24,16,128]{2,1,0:T(8,128)(2,1)S(1)} %get-tuple-element.41), channel_id=1, source_target_pairs={{0,192},{64,128},{128,64},{192,0},{1,193},{65,129},{129,65},{193,1... | collective-permute-start | bytes 294920 | tf_op jit(solution)/shard_map/ppermute | solution.py:25
  34.9 1.1 %collective-permute-start.13 = (bf16[24,16,128]{2,1,0:T(8,128)(2,1)S(1)}, bf16[24,16,128]{2,1,0:T(8,128)(2,1)S(1)}, u32[]{:S(2)}, u32[]{:S(2)}) collective-permute-start(bf16[24,16,128]{2,1,0:T(8,128)(2,1)S(1)} %get-tuple-element.43), channel_id=1, source_target_pairs={{0,48},{16,32},{32,16},{48,0},{1,49},{17,33},{33,17},{49,1},{2,50}... | collective-permute-start | bytes 294920 | tf_op jit(solution)/shard_map/ppermute | solution.py:25
  36.1 1.5 %collective-permute-done.10.refs_0_ = bf16[24,16,128]{2,1,0:T(8,128)(2,1)S(1)} collective-permute-done((bf16[24,16,128]{2,1,0:T(8,128)(2,1)S(1)}, bf16[24,16,128]{2,1,0:T(8,128)(2,1)S(1)}, u32[]{:S(2)}, u32[]{:S(2)}) %collective-permute-start.10) | collective-permute-done | bytes 98336 | tf_op jit(solution)/shard_map/ppermute | solution.py:19
  37.5 0.3 collective-permute-start.9
  37.8 2.9 %local.3.total = f32[48,16,128]{2,1,0:T(8,128)S(1)} custom-call(bf16[48,9,64,128]{3,2,1,0:T(8,128)(2,1)S(1)} %bitcast.6, bf16[48,16,128]{2,1,0:T(8,128)(2,1)S(1)} %get-tuple-element.39.v_ref, bf16[48,16,128]{2,1,0:T(8,128)(2,1)S(1)} %get-tuple-element.32.v_ref.source), custom_call_target="tpu_custom_call" | custom-call | flops 150994944 | bytes 4718592 | tf_op jit(solution)/shard_map/local/pallas_call | solution.py:218
  40.8 3.0 %near.3.total = f32[48,16,128]{2,1,0:T(8,128)S(1)} custom-call(bf16[48,9,64,128]{3,2,1,0:T(8,128)(2,1)S(1)} %bitcast.7, f32[48,16,128]{2,1,0:T(8,128)S(1)} %local.3.total, bf16[24,16,128]{2,1,0:T(8,128)(2,1)S(1)} %collective-permute-done.10.refs_0_, bf16[24,16,128]{2,1,0:T(8,128)(2,1)S(1)} %collective-permute-done.11.refs_1_, ...), custom_call_target="tpu_custom_call" | custom-call | flops 62914560 | bytes 1966080 | tf_op jit(solution)/shard_map/near/pallas_call | solution.py:218
  43.8 3.7 %collective-permute-done.9.late = bf16[24,16,128]{2,1,0:T(8,128)(2,1)S(1)} collective-permute-done((bf16[24,16,128]{2,1,0:T(8,128)(2,1)S(1)}, bf16[24,16,128]{2,1,0:T(8,128)(2,1)S(1)}, u32[]{:S(2)}, u32[]{:S(2)}) %collective-permute-start.9) | collective-permute-done | bytes 98336 | tf_op jit(solution)/shard_map/ppermute | solution.py:25
  47.4 0.5 last.1
  47.9 0.1 collective-permute-start.15
  48.0 2.5 %collective-permute-start.16 = (f32[4,48,128]{2,1,0:T(8,128)S(1)}, f32[4,48,128]{2,1,0:T(8,128)S(1)}, u32[]{:S(2)}, u32[]{:S(2)}) collective-permute-start(f32[4,48,128]{2,1,0:T(8,128)S(1)} %get-tuple-element.47), channel_id=1, source_target_pairs={{0,128},{64,192},{128,0},{192,64},{1,129},{65,193},{129,1},{193,65... | collective-permute-start | bytes 294920 | tf_op jit(solution)/shard_map/ppermute | solution.py:19
  50.5 2.2 %collective-permute-start.17 = (f32[4,48,128]{2,1,0:T(8,128)S(1)}, f32[4,48,128]{2,1,0:T(8,128)S(1)}, u32[]{:S(2)}, u32[]{:S(2)}) collective-permute-start(f32[4,48,128]{2,1,0:T(8,128)S(1)} %get-tuple-element.48), channel_id=1, source_target_pairs={{0,192},{64,128},{128,64},{192,0},{1,193},{65,129},{129,65},{193,1... | collective-permute-start | bytes 294920 | tf_op jit(solution)/shard_map/ppermute | solution.py:19
  52.7 1.5 %collective-permute-done.16.refs_2_ = f32[4,48,128]{2,1,0:T(8,128)S(1)} collective-permute-done((f32[4,48,128]{2,1,0:T(8,128)S(1)}, f32[4,48,128]{2,1,0:T(8,128)S(1)}, u32[]{:S(2)}, u32[]{:S(2)}) %collective-permute-start.16) | collective-permute-done | bytes 98336 | tf_op jit(solution)/shard_map/ppermute | solution.py:19
  54.2 2.1 %collective-permute-done.17.refs_3_ = f32[4,48,128]{2,1,0:T(8,128)S(1)} collective-permute-done((f32[4,48,128]{2,1,0:T(8,128)S(1)}, f32[4,48,128]{2,1,0:T(8,128)S(1)}, u32[]{:S(2)}, u32[]{:S(2)}) %collective-permute-start.17) | collective-permute-done | bytes 98336 | tf_op jit(solution)/shard_map/ppermute | solution.py:19
  56.4 0.8 %join.1 = f32[4,4,48,128]{3,2,1,0:T(8,128)} custom-call(f32[4,48,128]{2,1,0:T(8,128)S(1)} %get-tuple-element.45.refs_0_, f32[4,48,128]{2,1,0:T(8,128)S(1)} %collective-permute-done.15.refs_1_, f32[4,48,128]{2,1,0:T(8,128)S(1)} %collective-permute-done.16.refs_2_, f32[4,48,128]{2,1,0:T(8,128)S(1)} %collective-permute-done.17.refs_3_), custom_call_target="tpu_custom_call" | custom-call | bytes 786432 | tf_op jit(solution)/shard_map/join/pallas_call | solution.py:218
  (19 shorter events, 0.2 us)
Async XLA Ops:
  0.0 0.9 %copy-start.2 = (bf16[4,8,6,2,2,128]{5,4,3,2,1,0:T(2,128)(2,1)S(1)}, bf16[4,8,6,2,2,128]{5,4,3,2,1,0:T(2,128)(2,1)}, u32[]{:S(2)}) copy-start(bf16[4,8,6,2,2,128]{5,4,3,2,1,0:T(2,128)(2,1)} %param.2) | copy-start | bytes 589828
  1.0 4.8 %collective-permute-start = (bf16[4,48,128]{2,1,0:T(8,128)(2,1)S(1)}, bf16[4,48,128]{2,1,0:T(8,128)(2,1)S(1)}, u32[]{:S(2)}, u32[]{:S(2)}) collective-permute-start(bf16[4,48,128]{2,1,0:T(8,128)(2,1)S(1)} %get-tuple-element.28), channel_id=1, source_target_pairs={{0,64},{64,0},{128,192},{192,128},{1,65},{65,1},{129,193},{193,129... | collective-permute-start | bytes 147464 | tf_op jit(solution)/shard_map/ppermute | solution.py:19
  2.7 5.6 %collective-permute-start.1 = (bf16[4,48,128]{2,1,0:T(8,128)(2,1)S(1)}, bf16[4,48,128]{2,1,0:T(8,128)(2,1)S(1)}, u32[]{:S(2)}, u32[]{:S(2)}) collective-permute-start(bf16[4,48,128]{2,1,0:T(8,128)(2,1)S(1)} %get-tuple-element.29), channel_id=1, source_target_pairs={{0,128},{64,192},{128,0},{192,64},{1,129},{65,193},{129,1},{193,65... | collective-permute-start | bytes 147464 | tf_op jit(solution)/shard_map/ppermute | solution.py:19
  5.6 5.3 %collective-permute-start.2 = (bf16[4,48,128]{2,1,0:T(8,128)(2,1)S(1)}, bf16[4,48,128]{2,1,0:T(8,128)(2,1)S(1)}, u32[]{:S(2)}, u32[]{:S(2)}) collective-permute-start(bf16[4,48,128]{2,1,0:T(8,128)(2,1)S(1)} %get-tuple-element.30), channel_id=1, source_target_pairs={{0,192},{64,128},{128,64},{192,0},{1,193},{65,129},{129,65},{193,1... | collective-permute-start | bytes 147464 | tf_op jit(solution)/shard_map/ppermute | solution.py:19
  11.1 4.7 %collective-permute-start.4 = (bf16[24,16,128]{2,1,0:T(8,128)(2,1)S(1)}, bf16[24,16,128]{2,1,0:T(8,128)(2,1)S(1)}, u32[]{:S(2)}, u32[]{:S(2)}) collective-permute-start(bf16[24,16,128]{2,1,0:T(8,128)(2,1)S(1)} %get-tuple-element.33), channel_id=1, source_target_pairs={{0,64},{64,0},{128,192},{192,128},{1,65},{65,1},{129,193},{193,129... | collective-permute-start | bytes 294920 | tf_op jit(solution)/shard_map/ppermute | solution.py:19
  11.2 18.1 %collective-permute-start.5 = (bf16[24,16,128]{2,1,0:T(8,128)(2,1)S(1)}, bf16[24,16,128]{2,1,0:T(8,128)(2,1)S(1)}, u32[]{:S(2)}, u32[]{:S(2)}) collective-permute-start(bf16[24,16,128]{2,1,0:T(8,128)(2,1)S(1)} %get-tuple-element.34), channel_id=1, source_target_pairs={{0,192},{64,128},{128,64},{192,0},{1,193},{65,129},{129,65},{193,1... | collective-permute-start | bytes 294920 | tf_op jit(solution)/shard_map/ppermute | solution.py:25
  12.1 17.3 %collective-permute-start.6 = (bf16[24,16,128]{2,1,0:T(8,128)(2,1)S(1)}, bf16[24,16,128]{2,1,0:T(8,128)(2,1)S(1)}, u32[]{:S(2)}, u32[]{:S(2)}) collective-permute-start(bf16[24,16,128]{2,1,0:T(8,128)(2,1)S(1)} %get-tuple-element.35), channel_id=1, source_target_pairs={{0,16},{16,0},{32,48},{48,32},{1,17},{17,1},{33,49},{49,33},{2,18}... | collective-permute-start | bytes 294920 | tf_op jit(solution)/shard_map/ppermute | solution.py:19
  12.1 17.3 %collective-permute-start.7 = (bf16[24,16,128]{2,1,0:T(8,128)(2,1)S(1)}, bf16[24,16,128]{2,1,0:T(8,128)(2,1)S(1)}, u32[]{:S(2)}, u32[]{:S(2)}) collective-permute-start(bf16[24,16,128]{2,1,0:T(8,128)(2,1)S(1)} %get-tuple-element.36), channel_id=1, source_target_pairs={{0,48},{16,32},{32,16},{48,0},{1,49},{17,33},{33,17},{49,1},{2,50}... | collective-permute-start | bytes 294920 | tf_op jit(solution)/shard_map/ppermute | solution.py:25
  13.5 15.9 %collective-permute-start.8 = (bf16[24,16,128]{2,1,0:T(8,128)(2,1)S(1)}, bf16[24,16,128]{2,1,0:T(8,128)(2,1)S(1)}, u32[]{:S(2)}, u32[]{:S(2)}) collective-permute-start(bf16[24,16,128]{2,1,0:T(8,128)(2,1)S(1)} %get-tuple-element.37), channel_id=1, source_target_pairs={{0,1},{1,0},{2,3},{3,2},{4,5},{5,4},{6,7},{7,6},{8,9},{9,8},{10,11... | collective-permute-start | bytes 294920 | tf_op jit(solution)/shard_map/ppermute | solution.py:19
  15.8 16.6 %collective-permute-start.3 = (bf16[24,16,128]{2,1,0:T(8,128)(2,1)S(1)}, bf16[24,16,128]{2,1,0:T(8,128)(2,1)S(1)}, u32[]{:S(2)}, u32[]{:S(2)}) collective-permute-start(bf16[24,16,128]{2,1,0:T(8,128)(2,1)S(1)} %get-tuple-element.31), channel_id=1, source_target_pairs={{0,15},{1,2},{2,1},{3,4},{4,3},{5,6},{6,5},{7,8},{8,7},{9,10},{10,... | collective-permute-start | bytes 294920 | tf_op jit(solution)/shard_map/ppermute | solution.py:25
  23.4 3.0 %copy-start = (bf16[2,6,2,2,9,64,128]{6,5,4,3,2,1,0:T(8,128)(2,1)S(1)}, bf16[2,6,2,2,9,64,128]{6,5,4,3,2,1,0:T(8,128)(2,1)}, u32[]{:S(2)}) copy-start(bf16[2,6,2,2,9,64,128]{6,5,4,3,2,1,0:T(8,128)(2,1)} %param.3) | copy-start | bytes 21233668
  26.4 3.0 %copy-start.1 = (bf16[2,6,2,2,9,64,128]{6,5,4,3,2,1,0:T(8,128)(2,1)S(1)}, bf16[2,6,2,2,9,64,128]{6,5,4,3,2,1,0:T(8,128)(2,1)}, u32[]{:S(2)}) copy-start(bf16[2,6,2,2,9,64,128]{6,5,4,3,2,1,0:T(8,128)(2,1)} %param.3) | copy-start | bytes 21233668
  32.8 4.7 %collective-permute-start.10 = (bf16[24,16,128]{2,1,0:T(8,128)(2,1)S(1)}, bf16[24,16,128]{2,1,0:T(8,128)(2,1)S(1)}, u32[]{:S(2)}, u32[]{:S(2)}) collective-permute-start(bf16[24,16,128]{2,1,0:T(8,128)(2,1)S(1)} %get-tuple-element.40), channel_id=1, source_target_pairs={{0,64},{64,0},{128,192},{192,128},{1,65},{65,1},{129,193},{193,129... | collective-permute-start | bytes 294920 | tf_op jit(solution)/shard_map/ppermute | solution.py:19
  32.9 7.8 %collective-permute-start.11 = (bf16[24,16,128]{2,1,0:T(8,128)(2,1)S(1)}, bf16[24,16,128]{2,1,0:T(8,128)(2,1)S(1)}, u32[]{:S(2)}, u32[]{:S(2)}) collective-permute-start(bf16[24,16,128]{2,1,0:T(8,128)(2,1)S(1)} %get-tuple-element.41), channel_id=1, source_target_pairs={{0,192},{64,128},{128,64},{192,0},{1,193},{65,129},{129,65},{193,1... | collective-permute-start | bytes 294920 | tf_op jit(solution)/shard_map/ppermute | solution.py:25
  34.9 5.8 %collective-permute-start.12 = (bf16[24,16,128]{2,1,0:T(8,128)(2,1)S(1)}, bf16[24,16,128]{2,1,0:T(8,128)(2,1)S(1)}, u32[]{:S(2)}, u32[]{:S(2)}) collective-permute-start(bf16[24,16,128]{2,1,0:T(8,128)(2,1)S(1)} %get-tuple-element.42), channel_id=1, source_target_pairs={{0,16},{16,0},{32,48},{48,32},{1,17},{17,1},{33,49},{49,33},{2,18}... | collective-permute-start | bytes 294920 | tf_op jit(solution)/shard_map/ppermute | solution.py:19
  34.9 5.8 %collective-permute-start.13 = (bf16[24,16,128]{2,1,0:T(8,128)(2,1)S(1)}, bf16[24,16,128]{2,1,0:T(8,128)(2,1)S(1)}, u32[]{:S(2)}, u32[]{:S(2)}) collective-permute-start(bf16[24,16,128]{2,1,0:T(8,128)(2,1)S(1)} %get-tuple-element.43), channel_id=1, source_target_pairs={{0,48},{16,32},{32,16},{48,0},{1,49},{17,33},{33,17},{49,1},{2,50}... | collective-permute-start | bytes 294920 | tf_op jit(solution)/shard_map/ppermute | solution.py:25
  36.1 4.7 %collective-permute-start.14 = (bf16[24,16,128]{2,1,0:T(8,128)(2,1)S(1)}, bf16[24,16,128]{2,1,0:T(8,128)(2,1)S(1)}, u32[]{:S(2)}, u32[]{:S(2)}) collective-permute-start(bf16[24,16,128]{2,1,0:T(8,128)(2,1)S(1)} %get-tuple-element.44), channel_id=1, source_target_pairs={{0,1},{1,0},{2,3},{3,2},{4,5},{5,4},{6,7},{7,6},{8,9},{9,8},{10,11... | collective-permute-start | bytes 294920 | tf_op jit(solution)/shard_map/ppermute | solution.py:19
  37.5 9.9 %collective-permute-start.9 = (bf16[24,16,128]{2,1,0:T(8,128)(2,1)S(1)}, bf16[24,16,128]{2,1,0:T(8,128)(2,1)S(1)}, u32[]{:S(2)}, u32[]{:S(2)}) collective-permute-start(bf16[24,16,128]{2,1,0:T(8,128)(2,1)S(1)} %get-tuple-element.38), channel_id=1, source_target_pairs={{0,15},{1,2},{2,1},{3,4},{4,3},{5,6},{6,5},{7,8},{8,7},{9,10},{10,... | collective-permute-start | bytes 294920 | tf_op jit(solution)/shard_map/ppermute | solution.py:25
  47.9 4.8 %collective-permute-start.15 = (f32[4,48,128]{2,1,0:T(8,128)S(1)}, f32[4,48,128]{2,1,0:T(8,128)S(1)}, u32[]{:S(2)}, u32[]{:S(2)}) collective-permute-start(f32[4,48,128]{2,1,0:T(8,128)S(1)} %get-tuple-element.46), channel_id=1, source_target_pairs={{0,64},{64,0},{128,192},{192,128},{1,65},{65,1},{129,193},{193,129... | collective-permute-start | bytes 294920 | tf_op jit(solution)/shard_map/ppermute | solution.py:19
  48.0 6.2 %collective-permute-start.16 = (f32[4,48,128]{2,1,0:T(8,128)S(1)}, f32[4,48,128]{2,1,0:T(8,128)S(1)}, u32[]{:S(2)}, u32[]{:S(2)}) collective-permute-start(f32[4,48,128]{2,1,0:T(8,128)S(1)} %get-tuple-element.47), channel_id=1, source_target_pairs={{0,128},{64,192},{128,0},{192,64},{1,129},{65,193},{129,1},{193,65... | collective-permute-start | bytes 294920 | tf_op jit(solution)/shard_map/ppermute | solution.py:19
  50.5 5.8 %collective-permute-start.17 = (f32[4,48,128]{2,1,0:T(8,128)S(1)}, f32[4,48,128]{2,1,0:T(8,128)S(1)}, u32[]{:S(2)}, u32[]{:S(2)}) collective-permute-start(f32[4,48,128]{2,1,0:T(8,128)S(1)} %get-tuple-element.48), channel_id=1, source_target_pairs={{0,192},{64,128},{128,64},{192,0},{1,193},{65,129},{129,65},{193,1... | collective-permute-start | bytes 294920 | tf_op jit(solution)/shard_map/ppermute | solution.py:19

commit v3 on v2

v3 whole, which is shorter than its diff:
```python
import functools

import jax
import jax.numpy as jnp
from jax import lax
from jax.experimental import pallas as pl
from jax.experimental.pallas import tpu as pltpu
from jax.sharding import PartitionSpec as P

BF = jnp.bfloat16
F32 = jnp.float32
VM = pl.BlockSpec(memory_space=pltpu.VMEM)
ANY = pl.BlockSpec(memory_space=pl.ANY)
HBM = pl.BlockSpec(memory_space=pltpu.HBM)
AXES = ("sec", "gz", "ta")


def swap(array, axis, distance):
    count = lax.axis_size(axis)
    return lax.ppermute(array, axis, [(i, i ^ distance) for i in range(count)])


def swap_other(array, axis):
    count = lax.axis_size(axis)
    pairs = [(i, (i + (1 if i % 2 else count - 1)) % count) for i in range(count)]
    return lax.ppermute(array, axis, pairs)


STARTS = ((3, 1, 2, 0), (2, 5, 3, 1, 0, 4))


def exchange(faces):
    names = AXES[-(len(faces) // 2):]
    order = STARTS[len(faces) == 6]
    moved = []
    for number in order:
        axis, face = names[number // 2], faces[number]
        moved.append(swap_other(face, axis) if number % 2 else swap(face, axis, 1))
    return moved


def parities():
    return [lax.rem(lax.axis_index(axis), 2) for axis in AXES]


def site_of(x, y, z, t, ny):
    return ((x * ny + y) * 2 + z) * 2 + t


def face_sites(axis, coordinate, i, ny):
    if axis == 0:
        return coordinate * ny * 4 + i
    if axis == 1:
        return (i // 2) * 4 + coordinate * 2 + i % 2
    return i * 2 + coordinate


def write_faces(ny, v_ref, faces):
    odd = parities()
    skip = 3 - len(faces) // 2
    for axis in range(skip, 3):
        for i in range(ny * 4):
            near, far = faces[2 * (axis - skip)], faces[2 * (axis - skip) + 1]
            near[i] = v_ref[face_sites(axis, 1 - odd[axis], i, ny)]
            far[i] = v_ref[face_sites(axis, odd[axis], i, ny)]


def variants(value):
    half = value.shape[-1] // 2
    lane = lax.broadcasted_iota(jnp.int32, value.shape, 1)
    wide = value.astype(F32)
    first = jnp.where(lane < half, wide, -wide)
    second = pltpu.roll(wide, half, 1)
    return jnp.concatenate([first, second], 0).astype(BF)


def product(vectors, matrices):
    columns = vectors[0].shape[0] // 2
    both = lax.dot_general(
        jnp.concatenate(vectors, 1),
        jnp.concatenate(matrices, 1),
        (((1,), (1,)), ((), ())),
        preferred_element_type=F32,
    )
    return jnp.concatenate([both[:columns], both[columns:]], 1)


def split_kernel(source, *rest):
    outs, sems = rest[:-1], rest[-1]
    me = lax.axis_index("sec")
    planes = source.shape[1]
    copies = []
    for k, out in enumerate(outs):
        first = 2 * (me ^ k)
        pieces = [
            (lax.rem(first + planes - 1, planes), 1, 0),
            (first, 2, 1),
            (lax.rem(first + 2, planes), 1, 3),
        ]
        for number, (at, count, to) in enumerate(pieces):
            copies.append(
                pltpu.make_async_copy(
                    source.at[:, pl.ds(at, count)], out.at[:, pl.ds(to, count)], sems.at[k, number]
                )
            )
            copies[-1].start()
    for copy in copies:
        copy.wait()


def load_kernel(links, out, sems):
    count = sems.shape[0]
    step = links.shape[0] // count
    copies = []
    for k in range(count):
        part = pl.ds(k * step, step)
        copies.append(pltpu.make_async_copy(links.at[part], out.at[part], sems.at[k]))
        copies[-1].start()
    for copy in copies:
        copy.wait()


def join_kernel(*refs):
    parts, out, sems = refs[:-2], refs[-2], refs[-1]
    me = lax.axis_index("sec")
    copies = []
    for k, part in enumerate(parts):
        copies.append(pltpu.make_async_copy(part, out.at[:, me ^ k], sems.at[k]))
        copies[-1].start()
    for copy in copies:
        copy.wait()


def pack_kernel(ny, parts, *refs):
    blocks, (v_ref, before, after) = refs[:parts], refs[parts + 1:parts + 4]
    faces, wide = refs[parts + 4:-1], refs[-1]
    own, rows = blocks[0].shape[0], blocks[0].shape[1]
    me = lax.axis_index("sec")
    for k in range(parts):
        at = (me ^ k) * (own * rows)
        for c in range(own):
            start = pl.multiple_of(at + c * rows, 8)
            wide[pl.ds(start, rows), :] = blocks[k][c].astype(F32)
    half = rows // 4
    for row in range(rows):
        value = wide[pl.ds(row, own * parts, stride=rows), :].astype(BF)
        if row < half:
            before[row] = value
        elif row < 3 * half:
            v_ref[row - half] = value
        else:
            after[row - 3 * half] = value
    write_faces(ny, v_ref, faces)


def local_kernel(ny, links, v_ref, source, *refs):
    sides, total, vv = refs[:-2], refs[-2], refs[-1]
    sites = v_ref.shape[0]
    for i in range(sites):
        vv[i] = variants(v_ref[i])
    for y in range(ny):
        for x in range(2):
            for z in range(2):
                for t in range(2):
                    site = site_of(x, y, z, t, ny)
                    terms = [
                        (0, site),
                        (1 + x, site_of(1 - x, y, z, t, ny)),
                        (3, site_of(x, (y + 1) % ny, z, t, ny)),
                        (4, site_of(x, (y - 1) % ny, z, t, ny)),
                        (5 + z, site_of(x, y, 1 - z, t, ny)),
                        (7 + t, site_of(x, y, z, 1 - t, ny)),
                    ]
                    vectors = [vv[p] for _, p in terms]
                    matrices = [links[site, k] for k, _ in terms]
                    if sides:
                        vectors.append(variants(sides[x][(y * 2 + z) * 2 + t]))
                        matrices.append(links[site, 2 - x])
                    total[site] = source[site].astype(F32) - product(vectors, matrices)


def near_terms(ny, links, total, moved, store):
    order = STARTS[len(moved) == 6]
    near = [moved[order.index(number)] for number in range(len(order))]
    odd = parities()
    for y in range(ny):
        for side_x in range(2):
            x = 1 - odd[0] if side_x == 0 else odd[0]
            link_x = 1 + (odd[0] if side_x == 0 else 1 - odd[0])
            for side_z in range(2):
                z = 1 - odd[1] if side_z == 0 else odd[1]
                link_z = 5 + (odd[1] if side_z == 0 else 1 - odd[1])
                for side_t in range(2):
                    t = 1 - odd[2] if side_t == 0 else odd[2]
                    link_t = 7 + (odd[2] if side_t == 0 else 1 - odd[2])
                    site = site_of(x, y, z, t, ny)
                    terms = [
                        (link_z, near[-4 + side_z][(x * ny + y) * 2 + t]),
                        (link_t, near[-2 + side_t][(x * ny + y) * 2 + z]),
                    ]
                    if len(near) == 6:
                        terms.append((link_x, near[side_x][(y * 2 + z) * 2 + t]))
                    hop = product([variants(v) for _, v in terms], [links[site, k] for k, _ in terms])
                    store(site, total[site] - hop)


def near_kernel(ny, count, links, total, *refs):
    moved, v_ref, faces = refs[:count], refs[count], refs[count + 1:]

    def store(site, value):
        v_ref[site] = value.astype(BF)

    near_terms(ny, links, total, moved, store)
    write_faces(ny, v_ref, faces)


def last_kernel(ny, count, links, total, *refs):
    moved, outs, wide = refs[:count], refs[count:-1], refs[-1]
    own, sites = outs[0].shape[0], outs[0].shape[1]
    columns = own * len(outs)

    def store(site, value):
        wide[pl.ds(site, columns, stride=sites), :] = value

    near_terms(ny, links, total, moved, store)
    me = lax.axis_index("sec")
    for k, out in enumerate(outs):
        at = (me ^ k) * (own * sites)
        for c in range(own):
            start = pl.multiple_of(at + c * sites, 8)
            out[c] = wide[pl.ds(start, sites), :]


def call(kernel, name, out_shape, inputs, scratch, flops=0, bytes_accessed=0, places=None, out_place=VM):
    several = isinstance(out_shape, list)
    return pl.pallas_call(
        kernel,
        out_shape=out_shape,
        in_specs=places or [VM] * len(inputs),
        out_specs=[out_place] * len(out_shape) if several else out_place,
        scratch_shapes=scratch,
        compiler_params=pltpu.CompilerParams(vmem_limit_bytes=40 * 1024 * 1024),
        cost_estimate=pl.CostEstimate(
            flops=flops, bytes_accessed=bytes_accessed, transcendentals=0
        ),
        name=name,
    )(*inputs)


def local(ny, source, coarse_links):
    own, planes = source.shape[0], source.shape[1]
    parts = lax.axis_size("sec")
    width = source.shape[-1]
    half = ny * 4
    sites = 2 * half
    columns = own * parts
    links = coarse_links.reshape((sites,) + coarse_links.shape[4:])
    shape = jax.ShapeDtypeStruct
    whole = shape((sites, columns, width), BF)
    total_shape = shape((sites, columns, width), F32)
    face = shape((half, columns, width), BF)
    dma = pltpu.SemaphoreType.DMA
    per_term = 2 * sites * 2 * columns * width * width // 2
    link_bytes = links.size * 2 // 9

    blocks = call(
        split_kernel, "split", [shape((own, 4, half, width), BF)] * parts,
        [pltpu.with_memory_space_constraint(source.reshape(own, planes, half, width), pltpu.HBM)],
        [dma((parts, 3))],
        bytes_accessed=source.size * 4, places=[HBM],
    )
    links = call(
        load_kernel, "load", pltpu.VMEM(links.shape, BF),
        [pltpu.with_memory_space_constraint(links, pltpu.HBM)], [dma((8,))],
        bytes_accessed=18 * link_bytes, places=[HBM],
    )
    blocks = [blocks[0]] + [swap(blocks[k], "sec", k) for k in range(1, parts)]
    blocks = [block.reshape(own, 2 * sites, width) for block in blocks]
    v, before, after, *faces = call(
        functools.partial(pack_kernel, ny, parts), "pack", [whole] + [face] * 6, blocks + [links],
        [pltpu.VMEM((columns * 2 * sites, width), F32)], bytes_accessed=source.size * 8,
        places=[VM] * parts + [ANY],
    )
    first, sides = v, [before, after]
    for sweep in range(2):
        moved = exchange(faces)
        total = call(
            functools.partial(local_kernel, ny), "local", total_shape, [links, v, first] + sides,
            [pltpu.VMEM((sites, 2 * columns, width), BF)],
            flops=6 * per_term, bytes_accessed=6 * link_bytes,
        )
        sides = []
        inputs = [links, total] + moved
        cost = dict(flops=3 * per_term, bytes_accessed=3 * link_bytes)
        if sweep == 0:
            v, *faces = call(
                functools.partial(near_kernel, ny, len(moved)), "near", [whole] + [face] * 6,
                inputs, [], **cost,
            )
        else:
            result = call(
                functools.partial(last_kernel, ny, len(moved)), "last",
                [shape((own, sites, width), F32)] * parts, inputs,
                [pltpu.VMEM((columns * sites, width), F32)], **cost,
            )
    result = [result[0]] + [swap(result[k], "sec", k) for k in range(1, parts)]
    joined = call(
        join_kernel, "join", shape((own, parts, sites, width), F32), result, [dma((parts,))],
        bytes_accessed=source.size * 8, out_place=HBM,
    )
    return joined.reshape(source.shape)


def solution(mesh):
    def whole(source, coarse_links):
        return jax.shard_map(
            functools.partial(local, source.shape[2]),
            mesh=mesh,
            in_specs=(
                P("sec", None, None, "gz", "ta", None),
                P("sec", None, "gz", "ta", None, None, None),
            ),
            out_specs=P("sec", None, None, "gz", "ta", None),
            check_vma=False,
        )(source, coarse_links)

    return whole
```

time: 57.3 us -> 50.1 us (0.87)
  local copies, waits for them, and re-layouts: 3.98 us -> 0 us
  Pallas kernels: 13.7 us -> 10.7 us
  starting transfers between devices: 23.3 us -> 25.3 us
  waiting for transfers between devices: 16 us -> 14 us
    ppermute x12 -> x11, waiting for transfers between devices: 12.3 us -> 8.27 us  [swap(): return lax.ppermute(array, axis, [(i, i ^ distance) for i in range(count)])]
    unnamed x6 -> x0, local copies, waits for them, and re-layouts: 3.98 us -> none
    pallas_call x9 -> x8, Pallas kernels: 13.7 us -> 10.7 us  [call(): pl.pallas_call(kernel, out_shape=out_shape, in_specs=places or [VM] * len...]
    ppermute x6 -> x5, waiting for transfers between devices: 3.69 us -> 5.71 us  [swap_other(): return lax.ppermute(array, axis, pairs)]
    ppermute x6 -> x5, starting transfers between devices: 13.3 us -> 14.4 us  [swap_other(): return lax.ppermute(array, axis, pairs)]
    ppermute x12 -> x11, starting transfers between devices: 10.1 us -> 10.9 us  [swap(): return lax.ppermute(array, axis, [(i, i ^ distance) for i in range(count)])]
  transfers between devices with their start and end apart: 18 -> 16, of which waited for: 7 -> 9; matrix products, arithmetic and copies ran while one was open for 0% -> 0% of each run, Pallas kernels for 21% -> 13%
where the time goes in v3:
time: 50.1 us; the launch traced here: 50 us
  starting transfers between devices  25.3 us (50%)
  waiting for transfers between devices  14 us (28%)
  Pallas kernels  10.7 us (21%)
    ppermute x5, starting transfers between devices, swap_other(): return lax.ppermute(array, axis, pairs)  14.4 us
    ppermute x11, starting transfers between devices, swap(): return lax.ppermute(array, axis, [(i, i ^ distance) for i in range(count)])  10.9 us
    pallas_call x8, Pallas kernels, call(): pl.pallas_call(kernel, out_shape=out_shape, in_specs=places or [VM] * len...  10.7 us
    ppermute x11, waiting for transfers between devices, swap(): return lax.ppermute(array, axis, [(i, i ^ distance) for i in range(count)])  8.27 us
    ppermute x5, waiting for transfers between devices, swap_other(): return lax.ppermute(array, axis, pairs)  5.71 us
  transfers between devices with their start and end apart: 16, of which 9 were waited for; matrix products, arithmetic and copies ran while one was open for 0% of the time, Pallas kernels for 13%

profile of v3, /device:TPU:32, one launch (start us, length us, event | category | flops | bytes accessed | tf_op | source)
XLA Modules:
  0.0 50.0 jit_solution(9774759260549973304)
XLA Ops:
  0.0 1.1 %split.1 = (bf16[4,4,24,128]{3,2,1,0:T(8,128)(2,1)S(1)}, bf16[4,4,24,128]{3,2,1,0:T(8,128)(2,1)S(1)}, bf16[4,4,24,128]{3,2,1,0:T(8,128)(2,1)S(1)}, bf16[4,4,24,128]{3,2,1,0:T(8,128)(2,1)S(1)}) custom-call(bf16[4,8,24,128]{3,2,1,0:T(8,128)(2,1)} %bitcast.12), custom_call_target="tpu_custom_call" | custom-call | bytes 393216 | tf_op jit(solution)/shard_map/split/pallas_call | solution.py:236
  1.1 1.7 %collective-permute-start = (bf16[4,4,24,128]{3,2,1,0:T(8,128)(2,1)S(1)}, bf16[4,4,24,128]{3,2,1,0:T(8,128)(2,1)S(1)}, u32[]{:S(2)}, u32[]{:S(2)}) collective-permute-start(bf16[4,4,24,128]{3,2,1,0:T(8,128)(2,1)S(1)} %get-tuple-element.28), channel_id=1, source_target_pairs={{0,64},{64,0},{128,192},{192,128},{1,65},{65,1},{129,193},{193,129... | collective-permute-start | bytes 294920 | tf_op jit(solution)/shard_map/ppermute | solution.py:20
  2.7 2.9 %collective-permute-start.1 = (bf16[4,4,24,128]{3,2,1,0:T(8,128)(2,1)S(1)}, bf16[4,4,24,128]{3,2,1,0:T(8,128)(2,1)S(1)}, u32[]{:S(2)}, u32[]{:S(2)}) collective-permute-start(bf16[4,4,24,128]{3,2,1,0:T(8,128)(2,1)S(1)} %get-tuple-element.29), channel_id=1, source_target_pairs={{0,128},{64,192},{128,0},{192,64},{1,129},{65,193},{129,1},{193,65... | collective-permute-start | bytes 294920 | tf_op jit(solution)/shard_map/ppermute | solution.py:20
  5.7 0.2 collective-permute-start.2
  5.9 3.1 %load.1.refs_4_.links = bf16[48,9,64,128]{3,2,1,0:T(8,128)(2,1)S(1)} custom-call(bf16[48,9,64,128]{3,2,1,0:T(8,128)(2,1)} %bitcast.11), custom_call_target="tpu_custom_call" | custom-call | bytes 14155776 | tf_op jit(solution)/shard_map/load/pallas_call | solution.py:236
  9.0 0.0 collective-permute-done
  9.0 1.4 %collective-permute-done.1 = bf16[4,4,24,128]{3,2,1,0:T(8,128)(2,1)S(1)} collective-permute-done((bf16[4,4,24,128]{3,2,1,0:T(8,128)(2,1)S(1)}, bf16[4,4,24,128]{3,2,1,0:T(8,128)(2,1)S(1)}, u32[]{:S(2)}, u32[]{:S(2)}) %collective-permute-start.1) | collective-permute-done | bytes 98336 | tf_op jit(solution)/shard_map/ppermute | solution.py:20
  10.4 1.7 %collective-permute-done.2 = bf16[4,4,24,128]{3,2,1,0:T(8,128)(2,1)S(1)} collective-permute-done((bf16[4,4,24,128]{3,2,1,0:T(8,128)(2,1)S(1)}, bf16[4,4,24,128]{3,2,1,0:T(8,128)(2,1)S(1)}, u32[]{:S(2)}, u32[]{:S(2)}) %collective-permute-start.2) | collective-permute-done | bytes 98336 | tf_op jit(solution)/shard_map/ppermute | solution.py:20
  12.1 0.5 %pack.1 = (bf16[48,16,128]{2,1,0:T(8,128)(2,1)S(1)}, bf16[24,16,128]{2,1,0:T(8,128)(2,1)S(1)}, bf16[24,16,128]{2,1,0:T(8,128)(2,1)S(1)}, bf16[24,16,128]{2,1,0:T...) custom-call(bf16[4,96,128]{2,1,0:T(8,128)(2,1)S(1)} %bitcast.7, ...), custom_call_target="tpu_custom_call" | custom-call | bytes 786432 | tf_op jit(solution)/shard_map/pack/pallas_call | solution.py:236
  12.6 7.7 %collective-permute-start.3 = (bf16[24,16,128]{2,1,0:T(8,128)(2,1)S(1)}, bf16[24,16,128]{2,1,0:T(8,128)(2,1)S(1)}, u32[]{:S(2)}, u32[]{:S(2)}) collective-permute-start(bf16[24,16,128]{2,1,0:T(8,128)(2,1)S(1)} %get-tuple-element.34), channel_id=1, source_target_pairs={{0,15},{1,2},{2,1},{3,4},{4,3},{5,6},{6,5},{7,8},{8,7},{9,10},{10,... | collective-permute-start | bytes 294920 | tf_op jit(solution)/shard_map/ppermute | solution.py:26
  20.3 0.0 collective-permute-start.4
  20.3 0.0 collective-permute-start.5
  20.3 1.1 %collective-permute-start.6 = (bf16[24,16,128]{2,1,0:T(8,128)(2,1)S(1)}, bf16[24,16,128]{2,1,0:T(8,128)(2,1)S(1)}, u32[]{:S(2)}, u32[]{:S(2)}) collective-permute-start(bf16[24,16,128]{2,1,0:T(8,128)(2,1)S(1)} %get-tuple-element.37), channel_id=1, source_target_pairs={{0,16},{16,0},{32,48},{48,32},{1,17},{17,1},{33,49},{49,33},{2,18}... | collective-permute-start | bytes 294920 | tf_op jit(solution)/shard_map/ppermute | solution.py:20
  21.4 1.9 %local.2.total = f32[48,16,128]{2,1,0:T(8,128)S(1)} custom-call(bf16[48,9,64,128]{3,2,1,0:T(8,128)(2,1)S(1)} %load.1.refs_4_.links, bf16[48,16,128]{2,1,0:T(8,128)(2,1)S(1)} %get-tuple-element.31.v_ref.source, bf16[48,16,128]{2,1,0:T(8,128)(2,1)S(1)} %get-tuple-element.31.v_ref.source, bf16[24,16,128]{2,1,0:T(8,128)(2,1)S(1)} %get-tuple-element.32.refs_0_, ...), custom_call_target="tpu_custom_call" | custom-call | flops 150994944 | bytes 4718592 | tf_op jit(solution)/shard_map/local/pallas_call | solution.py:236
  23.3 1.7 %collective-permute-done.3.refs_0_ = bf16[24,16,128]{2,1,0:T(8,128)(2,1)S(1)} collective-permute-done((bf16[24,16,128]{2,1,0:T(8,128)(2,1)S(1)}, bf16[24,16,128]{2,1,0:T(8,128)(2,1)S(1)}, u32[]{:S(2)}, u32[]{:S(2)}) %collective-permute-start.3) | collective-permute-done | bytes 98336 | tf_op jit(solution)/shard_map/ppermute | solution.py:26
  25.0 0.8 %collective-permute-done.5.refs_2_ = bf16[24,16,128]{2,1,0:T(8,128)(2,1)S(1)} collective-permute-done((bf16[24,16,128]{2,1,0:T(8,128)(2,1)S(1)}, bf16[24,16,128]{2,1,0:T(8,128)(2,1)S(1)}, u32[]{:S(2)}, u32[]{:S(2)}) %collective-permute-start.5) | collective-permute-done | bytes 98336 | tf_op jit(solution)/shard_map/ppermute | solution.py:20
  25.8 0.7 %near.1 = (bf16[48,16,128]{2,1,0:T(8,128)(2,1)S(1)}, bf16[24,16,128]{2,1,0:T(8,128)(2,1)S(1)}, bf16[24,16,128]{2,1,0:T(8,128)(2,1)S(1)}, bf16[24,16,128]{2,1,0:T...) custom-call(bf16[48,9,64,128]{3,2,1,0:T(8,128)(2,1)S(1)} %load.1.ref, ...), custom_call_target="tpu_custom_call" | custom-call | flops 75497472 | bytes 2359296 | tf_op jit(solution)/shard_map/near/pallas_call | solution.py:236
  26.5 0.2 collective-permute-start.7
  26.7 4.0 %collective-permute-start.8 = (bf16[24,16,128]{2,1,0:T(8,128)(2,1)S(1)}, bf16[24,16,128]{2,1,0:T(8,128)(2,1)S(1)}, u32[]{:S(2)}, u32[]{:S(2)}) collective-permute-start(bf16[24,16,128]{2,1,0:T(8,128)(2,1)S(1)} %get-tuple-element.40), channel_id=1, source_target_pairs={{0,15},{1,2},{2,1},{3,4},{4,3},{5,6},{6,5},{7,8},{8,7},{9,10},{10,... | collective-permute-start | bytes 294920 | tf_op jit(solution)/shard_map/ppermute | solution.py:26
  30.8 1.9 %collective-permute-start.9 = (bf16[24,16,128]{2,1,0:T(8,128)(2,1)S(1)}, bf16[24,16,128]{2,1,0:T(8,128)(2,1)S(1)}, u32[]{:S(2)}, u32[]{:S(2)}) collective-permute-start(bf16[24,16,128]{2,1,0:T(8,128)(2,1)S(1)} %get-tuple-element.41), channel_id=1, source_target_pairs={{0,48},{16,32},{32,16},{48,0},{1,49},{17,33},{33,17},{49,1},{2,50}... | collective-permute-start | bytes 294920 | tf_op jit(solution)/shard_map/ppermute | solution.py:26
  32.7 0.8 %collective-permute-start.10 = (bf16[24,16,128]{2,1,0:T(8,128)(2,1)S(1)}, bf16[24,16,128]{2,1,0:T(8,128)(2,1)S(1)}, u32[]{:S(2)}, u32[]{:S(2)}) collective-permute-start(bf16[24,16,128]{2,1,0:T(8,128)(2,1)S(1)} %get-tuple-element.42), channel_id=1, source_target_pairs={{0,192},{64,128},{128,64},{192,0},{1,193},{65,129},{129,65},{193,1... | collective-permute-start | bytes 294920 | tf_op jit(solution)/shard_map/ppermute | solution.py:26
  33.5 1.5 %local.3.total = f32[48,16,128]{2,1,0:T(8,128)S(1)} custom-call(bf16[48,9,64,128]{3,2,1,0:T(8,128)(2,1)S(1)} %load.1.refs_4_.links, bf16[48,16,128]{2,1,0:T(8,128)(2,1)S(1)} %get-tuple-element.38.v_ref, bf16[48,16,128]{2,1,0:T(8,128)(2,1)S(1)} %get-tuple-element.31.v_ref.source), custom_call_target="tpu_custom_call" | custom-call | flops 150994944 | bytes 4718592 | tf_op jit(solution)/shard_map/local/pallas_call | solution.py:236
  34.9 1.3 %collective-permute-done.8.refs_1_ = bf16[24,16,128]{2,1,0:T(8,128)(2,1)S(1)} collective-permute-done((bf16[24,16,128]{2,1,0:T(8,128)(2,1)S(1)}, bf16[24,16,128]{2,1,0:T(8,128)(2,1)S(1)}, u32[]{:S(2)}, u32[]{:S(2)}) %collective-permute-start.8) | collective-permute-done | bytes 98336 | tf_op jit(solution)/shard_map/ppermute | solution.py:26
  36.3 2.7 %collective-permute-done.10.refs_3_ = bf16[24,16,128]{2,1,0:T(8,128)(2,1)S(1)} collective-permute-done((bf16[24,16,128]{2,1,0:T(8,128)(2,1)S(1)}, bf16[24,16,128]{2,1,0:T(8,128)(2,1)S(1)}, u32[]{:S(2)}, u32[]{:S(2)}) %collective-permute-start.10) | collective-permute-done | bytes 98336 | tf_op jit(solution)/shard_map/ppermute | solution.py:26
  39.0 1.2 %last.1 = (f32[4,48,128]{2,1,0:T(8,128)S(1)}, f32[4,48,128]{2,1,0:T(8,128)S(1)}, f32[4,48,128]{2,1,0:T(8,128)S(1)}, f32[4,48,128]{2,1,0:T(8,128)S(1)}) custom-call(bf16[48,9,64,128]{3,2,1,0:T(8,128)(2,1)S(1)} %load.1.refs_4_.links, f32[48,16,128]{2,1,0:T(8,128)S(1)} %local.3.total, bf16[24,16,128]{2,1,0:T(8,128)(2,1)S(1)} %collective-permute-done.7.refs_0_, ...), custom_call_target="tpu_custom_call" | custom-call | flops 75497472 | bytes 2359296 | tf_op jit(solution)/shard_map/last/pallas_call | solution.py:236
  40.1 1.2 %collective-permute-start.13 = (f32[4,48,128]{2,1,0:T(8,128)S(1)}, f32[4,48,128]{2,1,0:T(8,128)S(1)}, u32[]{:S(2)}, u32[]{:S(2)}) collective-permute-start(f32[4,48,128]{2,1,0:T(8,128)S(1)} %get-tuple-element.46), channel_id=1, source_target_pairs={{0,64},{64,0},{128,192},{192,128},{1,65},{65,1},{129,193},{193,129... | collective-permute-start | bytes 294920 | tf_op jit(solution)/shard_map/ppermute | solution.py:20
  41.3 2.1 %collective-permute-start.14 = (f32[4,48,128]{2,1,0:T(8,128)S(1)}, f32[4,48,128]{2,1,0:T(8,128)S(1)}, u32[]{:S(2)}, u32[]{:S(2)}) collective-permute-start(f32[4,48,128]{2,1,0:T(8,128)S(1)} %get-tuple-element.47), channel_id=1, source_target_pairs={{0,128},{64,192},{128,0},{192,64},{1,129},{65,193},{129,1},{193,65... | collective-permute-start | bytes 294920 | tf_op jit(solution)/shard_map/ppermute | solution.py:20
  43.4 1.5 %collective-permute-start.15 = (f32[4,48,128]{2,1,0:T(8,128)S(1)}, f32[4,48,128]{2,1,0:T(8,128)S(1)}, u32[]{:S(2)}, u32[]{:S(2)}) collective-permute-start(f32[4,48,128]{2,1,0:T(8,128)S(1)} %get-tuple-element.48), channel_id=1, source_target_pairs={{0,192},{64,128},{128,64},{192,0},{1,193},{65,129},{129,65},{193,1... | collective-permute-start | bytes 294920 | tf_op jit(solution)/shard_map/ppermute | solution.py:20
  44.9 0.8 %collective-permute-done.13.refs_1_ = f32[4,48,128]{2,1,0:T(8,128)S(1)} collective-permute-done((f32[4,48,128]{2,1,0:T(8,128)S(1)}, f32[4,48,128]{2,1,0:T(8,128)S(1)}, u32[]{:S(2)}, u32[]{:S(2)}) %collective-permute-start.13) | collective-permute-done | bytes 98336 | tf_op jit(solution)/shard_map/ppermute | solution.py:20
  45.7 1.9 %collective-permute-done.14.refs_2_ = f32[4,48,128]{2,1,0:T(8,128)S(1)} collective-permute-done((f32[4,48,128]{2,1,0:T(8,128)S(1)}, f32[4,48,128]{2,1,0:T(8,128)S(1)}, u32[]{:S(2)}, u32[]{:S(2)}) %collective-permute-start.14) | collective-permute-done | bytes 98336 | tf_op jit(solution)/shard_map/ppermute | solution.py:20
  47.6 1.7 %collective-permute-done.15.refs_3_ = f32[4,48,128]{2,1,0:T(8,128)S(1)} collective-permute-done((f32[4,48,128]{2,1,0:T(8,128)S(1)}, f32[4,48,128]{2,1,0:T(8,128)S(1)}, u32[]{:S(2)}, u32[]{:S(2)}) %collective-permute-start.15) | collective-permute-done | bytes 98336 | tf_op jit(solution)/shard_map/ppermute | solution.py:20
  49.2 0.8 %join.1 = f32[4,4,48,128]{3,2,1,0:T(8,128)} custom-call(f32[4,48,128]{2,1,0:T(8,128)S(1)} %get-tuple-element.45.refs_0_, f32[4,48,128]{2,1,0:T(8,128)S(1)} %collective-permute-done.13.refs_1_, f32[4,48,128]{2,1,0:T(8,128)S(1)} %collective-permute-done.14.refs_2_, f32[4,48,128]{2,1,0:T(8,128)S(1)} %collective-permute-done.15.refs_3_), custom_call_target="tpu_custom_call" | custom-call | bytes 786432 | tf_op jit(solution)/shard_map/join/pallas_call | solution.py:236
  (8 shorter events, 0.0 us)
Async XLA Ops:
  1.1 7.9 %collective-permute-start = (bf16[4,4,24,128]{3,2,1,0:T(8,128)(2,1)S(1)}, bf16[4,4,24,128]{3,2,1,0:T(8,128)(2,1)S(1)}, u32[]{:S(2)}, u32[]{:S(2)}) collective-permute-start(bf16[4,4,24,128]{3,2,1,0:T(8,128)(2,1)S(1)} %get-tuple-element.28), channel_id=1, source_target_pairs={{0,64},{64,0},{128,192},{192,128},{1,65},{65,1},{129,193},{193,129... | collective-permute-start | bytes 294920 | tf_op jit(solution)/shard_map/ppermute | solution.py:20
  2.7 7.6 %collective-permute-start.1 = (bf16[4,4,24,128]{3,2,1,0:T(8,128)(2,1)S(1)}, bf16[4,4,24,128]{3,2,1,0:T(8,128)(2,1)S(1)}, u32[]{:S(2)}, u32[]{:S(2)}) collective-permute-start(bf16[4,4,24,128]{3,2,1,0:T(8,128)(2,1)S(1)} %get-tuple-element.29), channel_id=1, source_target_pairs={{0,128},{64,192},{128,0},{192,64},{1,129},{65,193},{129,1},{193,65... | collective-permute-start | bytes 294920 | tf_op jit(solution)/shard_map/ppermute | solution.py:20
  5.7 6.4 %collective-permute-start.2 = (bf16[4,4,24,128]{3,2,1,0:T(8,128)(2,1)S(1)}, bf16[4,4,24,128]{3,2,1,0:T(8,128)(2,1)S(1)}, u32[]{:S(2)}, u32[]{:S(2)}) collective-permute-start(bf16[4,4,24,128]{3,2,1,0:T(8,128)(2,1)S(1)} %get-tuple-element.30), channel_id=1, source_target_pairs={{0,192},{64,128},{128,64},{192,0},{1,193},{65,129},{129,65},{193,1... | collective-permute-start | bytes 294920 | tf_op jit(solution)/shard_map/ppermute | solution.py:20
  12.6 12.4 %collective-permute-start.3 = (bf16[24,16,128]{2,1,0:T(8,128)(2,1)S(1)}, bf16[24,16,128]{2,1,0:T(8,128)(2,1)S(1)}, u32[]{:S(2)}, u32[]{:S(2)}) collective-permute-start(bf16[24,16,128]{2,1,0:T(8,128)(2,1)S(1)} %get-tuple-element.34), channel_id=1, source_target_pairs={{0,15},{1,2},{2,1},{3,4},{4,3},{5,6},{6,5},{7,8},{8,7},{9,10},{10,... | collective-permute-start | bytes 294920 | tf_op jit(solution)/shard_map/ppermute | solution.py:26
  20.3 4.7 %collective-permute-start.4 = (bf16[24,16,128]{2,1,0:T(8,128)(2,1)S(1)}, bf16[24,16,128]{2,1,0:T(8,128)(2,1)S(1)}, u32[]{:S(2)}, u32[]{:S(2)}) collective-permute-start(bf16[24,16,128]{2,1,0:T(8,128)(2,1)S(1)} %get-tuple-element.35), channel_id=1, source_target_pairs={{0,48},{16,32},{32,16},{48,0},{1,49},{17,33},{33,17},{49,1},{2,50}... | collective-permute-start | bytes 294920 | tf_op jit(solution)/shard_map/ppermute | solution.py:26
  20.3 5.5 %collective-permute-start.5 = (bf16[24,16,128]{2,1,0:T(8,128)(2,1)S(1)}, bf16[24,16,128]{2,1,0:T(8,128)(2,1)S(1)}, u32[]{:S(2)}, u32[]{:S(2)}) collective-permute-start(bf16[24,16,128]{2,1,0:T(8,128)(2,1)S(1)} %get-tuple-element.36), channel_id=1, source_target_pairs={{0,1},{1,0},{2,3},{3,2},{4,5},{5,4},{6,7},{7,6},{8,9},{9,8},{10,11... | collective-permute-start | bytes 294920 | tf_op jit(solution)/shard_map/ppermute | solution.py:20
  20.3 5.5 %collective-permute-start.6 = (bf16[24,16,128]{2,1,0:T(8,128)(2,1)S(1)}, bf16[24,16,128]{2,1,0:T(8,128)(2,1)S(1)}, u32[]{:S(2)}, u32[]{:S(2)}) collective-permute-start(bf16[24,16,128]{2,1,0:T(8,128)(2,1)S(1)} %get-tuple-element.37), channel_id=1, source_target_pairs={{0,16},{16,0},{32,48},{48,32},{1,17},{17,1},{33,49},{49,33},{2,18}... | collective-permute-start | bytes 294920 | tf_op jit(solution)/shard_map/ppermute | solution.py:20
  26.5 6.9 %collective-permute-start.7 = (bf16[24,16,128]{2,1,0:T(8,128)(2,1)S(1)}, bf16[24,16,128]{2,1,0:T(8,128)(2,1)S(1)}, u32[]{:S(2)}, u32[]{:S(2)}) collective-permute-start(bf16[24,16,128]{2,1,0:T(8,128)(2,1)S(1)} %get-tuple-element.39), channel_id=1, source_target_pairs={{0,16},{16,0},{32,48},{48,32},{1,17},{17,1},{33,49},{49,33},{2,18}... | collective-permute-start | bytes 294920 | tf_op jit(solution)/shard_map/ppermute | solution.py:20
  26.7 9.5 %collective-permute-start.8 = (bf16[24,16,128]{2,1,0:T(8,128)(2,1)S(1)}, bf16[24,16,128]{2,1,0:T(8,128)(2,1)S(1)}, u32[]{:S(2)}, u32[]{:S(2)}) collective-permute-start(bf16[24,16,128]{2,1,0:T(8,128)(2,1)S(1)} %get-tuple-element.40), channel_id=1, source_target_pairs={{0,15},{1,2},{2,1},{3,4},{4,3},{5,6},{6,5},{7,8},{8,7},{9,10},{10,... | collective-permute-start | bytes 294920 | tf_op jit(solution)/shard_map/ppermute | solution.py:26
  30.8 5.5 %collective-permute-start.9 = (bf16[24,16,128]{2,1,0:T(8,128)(2,1)S(1)}, bf16[24,16,128]{2,1,0:T(8,128)(2,1)S(1)}, u32[]{:S(2)}, u32[]{:S(2)}) collective-permute-start(bf16[24,16,128]{2,1,0:T(8,128)(2,1)S(1)} %get-tuple-element.41), channel_id=1, source_target_pairs={{0,48},{16,32},{32,16},{48,0},{1,49},{17,33},{33,17},{49,1},{2,50}... | collective-permute-start | bytes 294920 | tf_op jit(solution)/shard_map/ppermute | solution.py:26
  32.7 6.3 %collective-permute-start.10 = (bf16[24,16,128]{2,1,0:T(8,128)(2,1)S(1)}, bf16[24,16,128]{2,1,0:T(8,128)(2,1)S(1)}, u32[]{:S(2)}, u32[]{:S(2)}) collective-permute-start(bf16[24,16,128]{2,1,0:T(8,128)(2,1)S(1)} %get-tuple-element.42), channel_id=1, source_target_pairs={{0,192},{64,128},{128,64},{192,0},{1,193},{65,129},{129,65},{193,1... | collective-permute-start | bytes 294920 | tf_op jit(solution)/shard_map/ppermute | solution.py:26
  33.5 5.5 %collective-permute-start.11 = (bf16[24,16,128]{2,1,0:T(8,128)(2,1)S(1)}, bf16[24,16,128]{2,1,0:T(8,128)(2,1)S(1)}, u32[]{:S(2)}, u32[]{:S(2)}) collective-permute-start(bf16[24,16,128]{2,1,0:T(8,128)(2,1)S(1)} %get-tuple-element.43), channel_id=1, source_target_pairs={{0,64},{64,0},{128,192},{192,128},{1,65},{65,1},{129,193},{193,129... | collective-permute-start | bytes 294920 | tf_op jit(solution)/shard_map/ppermute | solution.py:20
  33.5 5.5 %collective-permute-start.12 = (bf16[24,16,128]{2,1,0:T(8,128)(2,1)S(1)}, bf16[24,16,128]{2,1,0:T(8,128)(2,1)S(1)}, u32[]{:S(2)}, u32[]{:S(2)}) collective-permute-start(bf16[24,16,128]{2,1,0:T(8,128)(2,1)S(1)} %get-tuple-element.44), channel_id=1, source_target_pairs={{0,1},{1,0},{2,3},{3,2},{4,5},{5,4},{6,7},{7,6},{8,9},{9,8},{10,11... | collective-permute-start | bytes 294920 | tf_op jit(solution)/shard_map/ppermute | solution.py:20
  40.1 5.6 %collective-permute-start.13 = (f32[4,48,128]{2,1,0:T(8,128)S(1)}, f32[4,48,128]{2,1,0:T(8,128)S(1)}, u32[]{:S(2)}, u32[]{:S(2)}) collective-permute-start(f32[4,48,128]{2,1,0:T(8,128)S(1)} %get-tuple-element.46), channel_id=1, source_target_pairs={{0,64},{64,0},{128,192},{192,128},{1,65},{65,1},{129,193},{193,129... | collective-permute-start | bytes 294920 | tf_op jit(solution)/shard_map/ppermute | solution.py:20
  41.3 6.2 %collective-permute-start.14 = (f32[4,48,128]{2,1,0:T(8,128)S(1)}, f32[4,48,128]{2,1,0:T(8,128)S(1)}, u32[]{:S(2)}, u32[]{:S(2)}) collective-permute-start(f32[4,48,128]{2,1,0:T(8,128)S(1)} %get-tuple-element.47), channel_id=1, source_target_pairs={{0,128},{64,192},{128,0},{192,64},{1,129},{65,193},{129,1},{193,65... | collective-permute-start | bytes 294920 | tf_op jit(solution)/shard_map/ppermute | solution.py:20
  43.4 5.8 %collective-permute-start.15 = (f32[4,48,128]{2,1,0:T(8,128)S(1)}, f32[4,48,128]{2,1,0:T(8,128)S(1)}, u32[]{:S(2)}, u32[]{:S(2)}) collective-permute-start(f32[4,48,128]{2,1,0:T(8,128)S(1)} %get-tuple-element.48), channel_id=1, source_target_pairs={{0,192},{64,128},{128,64},{192,0},{1,193},{65,129},{129,65},{193,1... | collective-permute-start | bytes 294920 | tf_op jit(solution)/shard_map/ppermute | solution.py:20

commit v4 on v3

--- a/solution.py
+++ b/solution.py
@@ -26,6 +26,7 @@
     return lax.ppermute(array, axis, pairs)
 
 
+SWAPS = (0, 2, 1, 3)
 STARTS = ((3, 1, 2, 0), (2, 5, 3, 1, 0, 4))
 
 
@@ -90,7 +91,7 @@
     me = lax.axis_index("sec")
     planes = source.shape[1]
     copies = []
-    for k, out in enumerate(outs):
+    for number_out, (k, out) in enumerate(zip(SWAPS, outs)):
         first = 2 * (me ^ k)
         pieces = [
             (lax.rem(first + planes - 1, planes), 1, 0),
@@ -100,7 +101,7 @@
         for number, (at, count, to) in enumerate(pieces):
             copies.append(
                 pltpu.make_async_copy(
-                    source.at[:, pl.ds(at, count)], out.at[:, pl.ds(to, count)], sems.at[k, number]
+                    source.at[:, pl.ds(at, count)], out.at[:, pl.ds(to, count)], sems.at[number_out, number]
                 )
             )
             copies[-1].start()
@@ -124,38 +125,44 @@
     parts, out, sems = refs[:-2], refs[-2], refs[-1]
     me = lax.axis_index("sec")
     copies = []
-    for k, part in enumerate(parts):
-        copies.append(pltpu.make_async_copy(part, out.at[:, me ^ k], sems.at[k]))
+    for number, (k, part) in enumerate(zip(SWAPS, parts)):
+        copies.append(pltpu.make_async_copy(part, out.at[:, me ^ k], sems.at[number]))
         copies[-1].start()
     for copy in copies:
         copy.wait()
 
 
+def widen(blocks, wide, pieces):
+    own = blocks[0].shape[0]
+    count = sum(size for _, size in pieces)
+    me = lax.axis_index("sec")
+    for k, block in zip(SWAPS, blocks):
+        at = (me ^ k) * (own * count)
+        for c in range(own):
+            to = at + c * count
+            for start, size in pieces:
+                place = pl.ds(pl.multiple_of(to, 8), size)
+                wide[place, :] = block[c, start:start + size].astype(F32)
+                to = to + size
+
+
 def pack_kernel(ny, parts, *refs):
-    blocks, (v_ref, before, after) = refs[:parts], refs[parts + 1:parts + 4]
-    faces, wide = refs[parts + 4:-1], refs[-1]
-    own, rows = blocks[0].shape[0], blocks[0].shape[1]
-    me = lax.axis_index("sec")
-    for k in range(parts):
-        at = (me ^ k) * (own * rows)
-        for c in range(own):
-            start = pl.multiple_of(at + c * rows, 8)
-            wide[pl.ds(start, rows), :] = blocks[k][c].astype(F32)
-    half = rows // 4
-    for row in range(rows):
-        value = wide[pl.ds(row, own * parts, stride=rows), :].astype(BF)
-        if row < half:
-            before[row] = value
-        elif row < 3 * half:
-            v_ref[row - half] = value
-        else:
-            after[row - 3 * half] = value
+    blocks, v_ref, faces, wide = refs[:parts], refs[parts + 1], refs[parts + 2:-1], refs[-1]
+    sites, columns = v_ref.shape[0], v_ref.shape[1]
+    widen(blocks, wide, [(sites // 2, sites)])
+    for site in range(sites):
+        v_ref[site] = wide[pl.ds(site, columns, stride=sites), :].astype(BF)
     write_faces(ny, v_ref, faces)
 
 
 def local_kernel(ny, links, v_ref, source, *refs):
-    sides, total, vv = refs[:-2], refs[-2], refs[-1]
-    sites = v_ref.shape[0]
+    sites, columns = v_ref.shape[0], v_ref.shape[1]
+    half = sites // 2
+    blocks = refs[:-3] if len(refs) > 2 else ()
+    total, vv = refs[len(blocks):len(blocks) + 2]
+    if blocks:
+        wide = refs[-1]
+        widen(blocks, wide, [(0, half), (3 * half, half)])
     for i in range(sites):
         vv[i] = variants(v_ref[i])
     for y in range(ny):
@@ -173,8 +180,9 @@
                     ]
                     vectors = [vv[p] for _, p in terms]
                     matrices = [links[site, k] for k, _ in terms]
-                    if sides:
-                        vectors.append(variants(sides[x][(y * 2 + z) * 2 + t]))
+                    if blocks:
+                        row = x * half + (y * 2 + z) * 2 + t
+                        vectors.append(variants(wide[pl.ds(row, columns, stride=sites), :]))
                         matrices.append(links[site, 2 - x])
                     total[site] = source[site].astype(F32) - product(vectors, matrices)
 
@@ -224,7 +232,7 @@
 
     near_terms(ny, links, total, moved, store)
     me = lax.axis_index("sec")
-    for k, out in enumerate(outs):
+    for k, out in zip(SWAPS, outs):
         at = (me ^ k) * (own * sites)
         for c in range(own):
             start = pl.multiple_of(at + c * sites, 8)
@@ -274,22 +282,23 @@
         [pltpu.with_memory_space_constraint(links, pltpu.HBM)], [dma((8,))],
         bytes_accessed=18 * link_bytes, places=[HBM],
     )
-    blocks = [blocks[0]] + [swap(blocks[k], "sec", k) for k in range(1, parts)]
+    blocks = [blocks[0]] + [swap(block, "sec", k) for k, block in zip(SWAPS[1:], blocks[1:])]
     blocks = [block.reshape(own, 2 * sites, width) for block in blocks]
-    v, before, after, *faces = call(
-        functools.partial(pack_kernel, ny, parts), "pack", [whole] + [face] * 6, blocks + [links],
-        [pltpu.VMEM((columns * 2 * sites, width), F32)], bytes_accessed=source.size * 8,
+    wide = pltpu.VMEM((columns * sites, width), F32)
+    v, *faces = call(
+        functools.partial(pack_kernel, ny, parts), "pack", [whole] + [face] * 4, blocks + [links],
+        [wide], bytes_accessed=source.size * 8,
         places=[VM] * parts + [ANY],
     )
-    first, sides = v, [before, after]
+    first = v
     for sweep in range(2):
         moved = exchange(faces)
         total = call(
-            functools.partial(local_kernel, ny), "local", total_shape, [links, v, first] + sides,
-            [pltpu.VMEM((sites, 2 * columns, width), BF)],
+            functools.partial(local_kernel, ny), "local", total_shape, [links, v, first] + blocks,
+            [pltpu.VMEM((sites, 2 * columns, width), BF)] + [wide] * (sweep == 0),
             flops=6 * per_term, bytes_accessed=6 * link_bytes,
         )
-        sides = []
+        blocks = []
         inputs = [links, total] + moved
         cost = dict(flops=3 * per_term, bytes_accessed=3 * link_bytes)
         if sweep == 0:
@@ -301,9 +310,9 @@
             result = call(
                 functools.partial(last_kernel, ny, len(moved)), "last",
                 [shape((own, sites, width), F32)] * parts, inputs,
-                [pltpu.VMEM((columns * sites, width), F32)], **cost,
+                [wide], **cost,
             )
-    result = [result[0]] + [swap(result[k], "sec", k) for k in range(1, parts)]
+    result = [result[0]] + [swap(part, "sec", k) for k, part in zip(SWAPS[1:], result[1:])]
     joined = call(
         join_kernel, "join", shape((own, parts, sites, width), F32), result, [dma((parts,))],
         bytes_accessed=source.size * 8, out_place=HBM,

time: 50.1 us -> 47.8 us (0.954)
  waiting for transfers between devices: 14 us -> 11.8 us
    ppermute x5, waiting for transfers between devices: 5.71 us -> 4.12 us  [swap_other(): return lax.ppermute(array, axis, pairs)]
    ppermute x11, waiting for transfers between devices: 8.27 us -> 7.63 us  [swap(): return lax.ppermute(array, axis, [(i, i ^ distance) for i in range(count)])]
    ppermute x5, starting transfers between devices: 14.4 us -> 15 us  [swap_other(): return lax.ppermute(array, axis, pairs)]
    ppermute x11, starting transfers between devices: 10.9 us -> 10.4 us  [swap(): return lax.ppermute(array, axis, [(i, i ^ distance) for i in range(count)])]
  transfers between devices with their start and end apart: 16 -> 16, of which waited for: 9 -> 9; matrix products, arithmetic and copies ran while one was open for 0% -> 0% of each run, Pallas kernels for 13% -> 14%
where the time goes in v4:
time: 47.8 us; the launch traced here: 47.6 us
  starting transfers between devices  25.4 us (53%)
  waiting for transfers between devices  11.8 us (25%)
  Pallas kernels  10.4 us (22%)
    ppermute x5, starting transfers between devices, swap_other(): return lax.ppermute(array, axis, pairs)  15 us
    ppermute x11, starting transfers between devices, swap(): return lax.ppermute(array, axis, [(i, i ^ distance) for i in range(count)])  10.4 us
    pallas_call x8, Pallas kernels, call(): pl.pallas_call(kernel, out_shape=out_shape, in_specs=places or [VM] * len...  10.4 us
    ppermute x11, waiting for transfers between devices, swap(): return lax.ppermute(array, axis, [(i, i ^ distance) for i in range(count)])  7.63 us
    ppermute x5, waiting for transfers between devices, swap_other(): return lax.ppermute(array, axis, pairs)  4.12 us
  transfers between devices with their start and end apart: 16, of which 9 were waited for; matrix products, arithmetic and copies ran while one was open for 0% of the time, Pallas kernels for 14%

profile of v4, /device:TPU:32, one launch (start us, length us, event | category | flops | bytes accessed | tf_op | source)
XLA Modules:
  0.0 47.6 jit_solution(2699147345212007844)
XLA Ops:
  0.0 1.1 %split.1 = (bf16[4,4,24,128]{3,2,1,0:T(8,128)(2,1)S(1)}, bf16[4,4,24,128]{3,2,1,0:T(8,128)(2,1)S(1)}, bf16[4,4,24,128]{3,2,1,0:T(8,128)(2,1)S(1)}, bf16[4,4,24,128]{3,2,1,0:T(8,128)(2,1)S(1)}) custom-call(bf16[4,8,24,128]{3,2,1,0:T(8,128)(2,1)} %bitcast.16), custom_call_target="tpu_custom_call" | custom-call | bytes 393216 | tf_op jit(solution)/shard_map/split/pallas_call | solution.py:244
  1.1 3.3 %collective-permute-start = (bf16[4,4,24,128]{3,2,1,0:T(8,128)(2,1)S(1)}, bf16[4,4,24,128]{3,2,1,0:T(8,128)(2,1)S(1)}, u32[]{:S(2)}, u32[]{:S(2)}) collective-permute-start(bf16[4,4,24,128]{3,2,1,0:T(8,128)(2,1)S(1)} %get-tuple-element.26), channel_id=1, source_target_pairs={{0,128},{64,192},{128,0},{192,64},{1,129},{65,193},{129,1},{193,65... | collective-permute-start | bytes 294920 | tf_op jit(solution)/shard_map/ppermute | solution.py:20
  4.4 0.7 %collective-permute-start.1 = (bf16[4,4,24,128]{3,2,1,0:T(8,128)(2,1)S(1)}, bf16[4,4,24,128]{3,2,1,0:T(8,128)(2,1)S(1)}, u32[]{:S(2)}, u32[]{:S(2)}) collective-permute-start(bf16[4,4,24,128]{3,2,1,0:T(8,128)(2,1)S(1)} %get-tuple-element.27), channel_id=1, source_target_pairs={{0,64},{64,0},{128,192},{192,128},{1,65},{65,1},{129,193},{193,129... | collective-permute-start | bytes 294920 | tf_op jit(solution)/shard_map/ppermute | solution.py:20
  5.0 0.4 collective-permute-start.2
  5.4 3.1 %load.1.refs_4_.links = bf16[48,9,64,128]{3,2,1,0:T(8,128)(2,1)S(1)} custom-call(bf16[48,9,64,128]{3,2,1,0:T(8,128)(2,1)} %bitcast.15), custom_call_target="tpu_custom_call" | custom-call | bytes 14155776 | tf_op jit(solution)/shard_map/load/pallas_call | solution.py:244
  8.5 0.0 collective-permute-done
  8.5 1.1 %collective-permute-done.1 = bf16[4,4,24,128]{3,2,1,0:T(8,128)(2,1)S(1)} collective-permute-done((bf16[4,4,24,128]{3,2,1,0:T(8,128)(2,1)S(1)}, bf16[4,4,24,128]{3,2,1,0:T(8,128)(2,1)S(1)}, u32[]{:S(2)}, u32[]{:S(2)}) %collective-permute-start.1) | collective-permute-done | bytes 98336 | tf_op jit(solution)/shard_map/ppermute | solution.py:20
  9.7 1.2 %collective-permute-done.2 = bf16[4,4,24,128]{3,2,1,0:T(8,128)(2,1)S(1)} collective-permute-done((bf16[4,4,24,128]{3,2,1,0:T(8,128)(2,1)S(1)}, bf16[4,4,24,128]{3,2,1,0:T(8,128)(2,1)S(1)}, u32[]{:S(2)}, u32[]{:S(2)}) %collective-permute-start.2) | collective-permute-done | bytes 98336 | tf_op jit(solution)/shard_map/ppermute | solution.py:20
  10.9 0.2 pack.1
  11.1 7.7 %collective-permute-start.3 = (bf16[24,16,128]{2,1,0:T(8,128)(2,1)S(1)}, bf16[24,16,128]{2,1,0:T(8,128)(2,1)S(1)}, u32[]{:S(2)}, u32[]{:S(2)}) collective-permute-start(bf16[24,16,128]{2,1,0:T(8,128)(2,1)S(1)} %get-tuple-element.30), channel_id=1, source_target_pairs={{0,15},{1,2},{2,1},{3,4},{4,3},{5,6},{6,5},{7,8},{8,7},{9,10},{10,... | collective-permute-start | bytes 294920 | tf_op jit(solution)/shard_map/ppermute | solution.py:26
  18.8 1.1 %collective-permute-start.6 = (bf16[24,16,128]{2,1,0:T(8,128)(2,1)S(1)}, bf16[24,16,128]{2,1,0:T(8,128)(2,1)S(1)}, u32[]{:S(2)}, u32[]{:S(2)}) collective-permute-start(bf16[24,16,128]{2,1,0:T(8,128)(2,1)S(1)} %get-tuple-element.33), channel_id=1, source_target_pairs={{0,16},{16,0},{32,48},{48,32},{1,17},{17,1},{33,49},{49,33},{2,18}... | collective-permute-start | bytes 294920 | tf_op jit(solution)/shard_map/ppermute | solution.py:20
  19.9 1.9 %local.2.total = f32[48,16,128]{2,1,0:T(8,128)S(1)} custom-call(bf16[48,9,64,128]{3,2,1,0:T(8,128)(2,1)S(1)} %load.1.refs_4_.links, bf16[48,16,128]{2,1,0:T(8,128)(2,1)S(1)} %get-tuple-element.29.v_ref.source, bf16[48,16,128]{2,1,0:T(8,128)(2,1)S(1)} %get-tuple-element.29.v_ref.source, bf16[4,96,128]{2,1,0:T(8,128)(2,1)S(1)} %bitcast.8, ...), custom_call_target="tpu_custom_call" | custom-call | flops 150994944 | bytes 4718592 | tf_op jit(solution)/shard_map/local/pallas_call | solution.py:244
  21.8 0.2 collective-permute-done.3.refs_0_
  22.0 1.4 %collective-permute-done.4.refs_1_ = bf16[24,16,128]{2,1,0:T(8,128)(2,1)S(1)} collective-permute-done((bf16[24,16,128]{2,1,0:T(8,128)(2,1)S(1)}, bf16[24,16,128]{2,1,0:T(8,128)(2,1)S(1)}, u32[]{:S(2)}, u32[]{:S(2)}) %collective-permute-start.4) | collective-permute-done | bytes 98336 | tf_op jit(solution)/shard_map/ppermute | solution.py:26
  23.4 0.9 %collective-permute-done.5.refs_2_ = bf16[24,16,128]{2,1,0:T(8,128)(2,1)S(1)} collective-permute-done((bf16[24,16,128]{2,1,0:T(8,128)(2,1)S(1)}, bf16[24,16,128]{2,1,0:T(8,128)(2,1)S(1)}, u32[]{:S(2)}, u32[]{:S(2)}) %collective-permute-start.5) | collective-permute-done | bytes 98336 | tf_op jit(solution)/shard_map/ppermute | solution.py:20
  24.3 0.7 %near.1 = (bf16[48,16,128]{2,1,0:T(8,128)(2,1)S(1)}, bf16[24,16,128]{2,1,0:T(8,128)(2,1)S(1)}, bf16[24,16,128]{2,1,0:T(8,128)(2,1)S(1)}, bf16[24,16,128]{2,1,0:T...) custom-call(bf16[48,9,64,128]{3,2,1,0:T(8,128)(2,1)S(1)} %load.1.ref, ...), custom_call_target="tpu_custom_call" | custom-call | flops 75497472 | bytes 2359296 | tf_op jit(solution)/shard_map/near/pallas_call | solution.py:244
  25.0 0.2 collective-permute-start.7
  25.2 4.0 %collective-permute-start.8 = (bf16[24,16,128]{2,1,0:T(8,128)(2,1)S(1)}, bf16[24,16,128]{2,1,0:T(8,128)(2,1)S(1)}, u32[]{:S(2)}, u32[]{:S(2)}) collective-permute-start(bf16[24,16,128]{2,1,0:T(8,128)(2,1)S(1)} %get-tuple-element.36), channel_id=1, source_target_pairs={{0,15},{1,2},{2,1},{3,4},{4,3},{5,6},{6,5},{7,8},{8,7},{9,10},{10,... | collective-permute-start | bytes 294920 | tf_op jit(solution)/shard_map/ppermute | solution.py:26
  29.2 1.0 %collective-permute-start.9 = (bf16[24,16,128]{2,1,0:T(8,128)(2,1)S(1)}, bf16[24,16,128]{2,1,0:T(8,128)(2,1)S(1)}, u32[]{:S(2)}, u32[]{:S(2)}) collective-permute-start(bf16[24,16,128]{2,1,0:T(8,128)(2,1)S(1)} %get-tuple-element.37), channel_id=1, source_target_pairs={{0,48},{16,32},{32,16},{48,0},{1,49},{17,33},{33,17},{49,1},{2,50}... | collective-permute-start | bytes 294920 | tf_op jit(solution)/shard_map/ppermute | solution.py:26
  30.2 2.3 %collective-permute-start.10 = (bf16[24,16,128]{2,1,0:T(8,128)(2,1)S(1)}, bf16[24,16,128]{2,1,0:T(8,128)(2,1)S(1)}, u32[]{:S(2)}, u32[]{:S(2)}) collective-permute-start(bf16[24,16,128]{2,1,0:T(8,128)(2,1)S(1)} %get-tuple-element.38), channel_id=1, source_target_pairs={{0,192},{64,128},{128,64},{192,0},{1,193},{65,129},{129,65},{193,1... | collective-permute-start | bytes 294920 | tf_op jit(solution)/shard_map/ppermute | solution.py:26
  32.5 0.1 collective-permute-start.11
  32.6 1.5 %local.3.total = f32[48,16,128]{2,1,0:T(8,128)S(1)} custom-call(bf16[48,9,64,128]{3,2,1,0:T(8,128)(2,1)S(1)} %load.1.refs_4_.links, bf16[48,16,128]{2,1,0:T(8,128)(2,1)S(1)} %get-tuple-element.34.v_ref, bf16[48,16,128]{2,1,0:T(8,128)(2,1)S(1)} %get-tuple-element.29.v_ref.source), custom_call_target="tpu_custom_call" | custom-call | flops 150994944 | bytes 4718592 | tf_op jit(solution)/shard_map/local/pallas_call | solution.py:244
  34.1 2.5 %collective-permute-done.8.refs_1_ = bf16[24,16,128]{2,1,0:T(8,128)(2,1)S(1)} collective-permute-done((bf16[24,16,128]{2,1,0:T(8,128)(2,1)S(1)}, bf16[24,16,128]{2,1,0:T(8,128)(2,1)S(1)}, u32[]{:S(2)}, u32[]{:S(2)}) %collective-permute-start.8) | collective-permute-done | bytes 98336 | tf_op jit(solution)/shard_map/ppermute | solution.py:26
  36.6 0.7 %collective-permute-done.11.refs_4_ = bf16[24,16,128]{2,1,0:T(8,128)(2,1)S(1)} collective-permute-done((bf16[24,16,128]{2,1,0:T(8,128)(2,1)S(1)}, bf16[24,16,128]{2,1,0:T(8,128)(2,1)S(1)}, u32[]{:S(2)}, u32[]{:S(2)}) %collective-permute-start.11) | collective-permute-done | bytes 98336 | tf_op jit(solution)/shard_map/ppermute | solution.py:20
  37.3 0.0 collective-permute-done.12.refs_5_
  37.3 1.1 %last.1 = (f32[4,48,128]{2,1,0:T(8,128)S(1)}, f32[4,48,128]{2,1,0:T(8,128)S(1)}, f32[4,48,128]{2,1,0:T(8,128)S(1)}, f32[4,48,128]{2,1,0:T(8,128)S(1)}) custom-call(bf16[48,9,64,128]{3,2,1,0:T(8,128)(2,1)S(1)} %load.1.refs_4_.links, f32[48,16,128]{2,1,0:T(8,128)S(1)} %local.3.total, bf16[24,16,128]{2,1,0:T(8,128)(2,1)S(1)} %collective-permute-done.7.refs_0_, ...), custom_call_target="tpu_custom_call" | custom-call | flops 75497472 | bytes 2359296 | tf_op jit(solution)/shard_map/last/pallas_call | solution.py:244
  38.4 2.4 %collective-permute-start.13 = (f32[4,48,128]{2,1,0:T(8,128)S(1)}, f32[4,48,128]{2,1,0:T(8,128)S(1)}, u32[]{:S(2)}, u32[]{:S(2)}) collective-permute-start(f32[4,48,128]{2,1,0:T(8,128)S(1)} %get-tuple-element.42), channel_id=1, source_target_pairs={{0,128},{64,192},{128,0},{192,64},{1,129},{65,193},{129,1},{193,65... | collective-permute-start | bytes 294920 | tf_op jit(solution)/shard_map/ppermute | solution.py:20
  40.8 0.1 collective-permute-start.14
  40.9 2.2 %collective-permute-start.15 = (f32[4,48,128]{2,1,0:T(8,128)S(1)}, f32[4,48,128]{2,1,0:T(8,128)S(1)}, u32[]{:S(2)}, u32[]{:S(2)}) collective-permute-start(f32[4,48,128]{2,1,0:T(8,128)S(1)} %get-tuple-element.44), channel_id=1, source_target_pairs={{0,192},{64,128},{128,64},{192,0},{1,193},{65,129},{129,65},{193,1... | collective-permute-start | bytes 294920 | tf_op jit(solution)/shard_map/ppermute | solution.py:20
  43.1 2.6 %collective-permute-done.13.refs_1_ = f32[4,48,128]{2,1,0:T(8,128)S(1)} collective-permute-done((f32[4,48,128]{2,1,0:T(8,128)S(1)}, f32[4,48,128]{2,1,0:T(8,128)S(1)}, u32[]{:S(2)}, u32[]{:S(2)}) %collective-permute-start.13) | collective-permute-done | bytes 98336 | tf_op jit(solution)/shard_map/ppermute | solution.py:20
  45.7 1.1 %collective-permute-done.15.refs_3_ = f32[4,48,128]{2,1,0:T(8,128)S(1)} collective-permute-done((f32[4,48,128]{2,1,0:T(8,128)S(1)}, f32[4,48,128]{2,1,0:T(8,128)S(1)}, u32[]{:S(2)}, u32[]{:S(2)}) %collective-permute-start.15) | collective-permute-done | bytes 98336 | tf_op jit(solution)/shard_map/ppermute | solution.py:20
  46.8 0.8 %join.1 = f32[4,4,48,128]{3,2,1,0:T(8,128)} custom-call(f32[4,48,128]{2,1,0:T(8,128)S(1)} %get-tuple-element.41.refs_0_, f32[4,48,128]{2,1,0:T(8,128)S(1)} %collective-permute-done.13.refs_1_, f32[4,48,128]{2,1,0:T(8,128)S(1)} %collective-permute-done.14.refs_2_, f32[4,48,128]{2,1,0:T(8,128)S(1)} %collective-permute-done.15.refs_3_), custom_call_target="tpu_custom_call" | custom-call | bytes 786432 | tf_op jit(solution)/shard_map/join/pallas_call | solution.py:244
  (8 shorter events, 0.0 us)
Async XLA Ops:
  1.1 7.4 %collective-permute-start = (bf16[4,4,24,128]{3,2,1,0:T(8,128)(2,1)S(1)}, bf16[4,4,24,128]{3,2,1,0:T(8,128)(2,1)S(1)}, u32[]{:S(2)}, u32[]{:S(2)}) collective-permute-start(bf16[4,4,24,128]{3,2,1,0:T(8,128)(2,1)S(1)} %get-tuple-element.26), channel_id=1, source_target_pairs={{0,128},{64,192},{128,0},{192,64},{1,129},{65,193},{129,1},{193,65... | collective-permute-start | bytes 294920 | tf_op jit(solution)/shard_map/ppermute | solution.py:20
  4.4 5.3 %collective-permute-start.1 = (bf16[4,4,24,128]{3,2,1,0:T(8,128)(2,1)S(1)}, bf16[4,4,24,128]{3,2,1,0:T(8,128)(2,1)S(1)}, u32[]{:S(2)}, u32[]{:S(2)}) collective-permute-start(bf16[4,4,24,128]{3,2,1,0:T(8,128)(2,1)S(1)} %get-tuple-element.27), channel_id=1, source_target_pairs={{0,64},{64,0},{128,192},{192,128},{1,65},{65,1},{129,193},{193,129... | collective-permute-start | bytes 294920 | tf_op jit(solution)/shard_map/ppermute | solution.py:20
  5.0 5.8 %collective-permute-start.2 = (bf16[4,4,24,128]{3,2,1,0:T(8,128)(2,1)S(1)}, bf16[4,4,24,128]{3,2,1,0:T(8,128)(2,1)S(1)}, u32[]{:S(2)}, u32[]{:S(2)}) collective-permute-start(bf16[4,4,24,128]{3,2,1,0:T(8,128)(2,1)S(1)} %get-tuple-element.28), channel_id=1, source_target_pairs={{0,192},{64,128},{128,64},{192,0},{1,193},{65,129},{129,65},{193,1... | collective-permute-start | bytes 294920 | tf_op jit(solution)/shard_map/ppermute | solution.py:20
  11.1 11.0 %collective-permute-start.3 = (bf16[24,16,128]{2,1,0:T(8,128)(2,1)S(1)}, bf16[24,16,128]{2,1,0:T(8,128)(2,1)S(1)}, u32[]{:S(2)}, u32[]{:S(2)}) collective-permute-start(bf16[24,16,128]{2,1,0:T(8,128)(2,1)S(1)} %get-tuple-element.30), channel_id=1, source_target_pairs={{0,15},{1,2},{2,1},{3,4},{4,3},{5,6},{6,5},{7,8},{8,7},{9,10},{10,... | collective-permute-start | bytes 294920 | tf_op jit(solution)/shard_map/ppermute | solution.py:26
  18.7 4.7 %collective-permute-start.4 = (bf16[24,16,128]{2,1,0:T(8,128)(2,1)S(1)}, bf16[24,16,128]{2,1,0:T(8,128)(2,1)S(1)}, u32[]{:S(2)}, u32[]{:S(2)}) collective-permute-start(bf16[24,16,128]{2,1,0:T(8,128)(2,1)S(1)} %get-tuple-element.31), channel_id=1, source_target_pairs={{0,48},{16,32},{32,16},{48,0},{1,49},{17,33},{33,17},{49,1},{2,50}... | collective-permute-start | bytes 294920 | tf_op jit(solution)/shard_map/ppermute | solution.py:26
  18.7 5.5 %collective-permute-start.5 = (bf16[24,16,128]{2,1,0:T(8,128)(2,1)S(1)}, bf16[24,16,128]{2,1,0:T(8,128)(2,1)S(1)}, u32[]{:S(2)}, u32[]{:S(2)}) collective-permute-start(bf16[24,16,128]{2,1,0:T(8,128)(2,1)S(1)} %get-tuple-element.32), channel_id=1, source_target_pairs={{0,1},{1,0},{2,3},{3,2},{4,5},{5,4},{6,7},{7,6},{8,9},{9,8},{10,11... | collective-permute-start | bytes 294920 | tf_op jit(solution)/shard_map/ppermute | solution.py:20
  18.8 5.5 %collective-permute-start.6 = (bf16[24,16,128]{2,1,0:T(8,128)(2,1)S(1)}, bf16[24,16,128]{2,1,0:T(8,128)(2,1)S(1)}, u32[]{:S(2)}, u32[]{:S(2)}) collective-permute-start(bf16[24,16,128]{2,1,0:T(8,128)(2,1)S(1)} %get-tuple-element.33), channel_id=1, source_target_pairs={{0,16},{16,0},{32,48},{48,32},{1,17},{17,1},{33,49},{49,33},{2,18}... | collective-permute-start | bytes 294920 | tf_op jit(solution)/shard_map/ppermute | solution.py:20
  25.0 7.6 %collective-permute-start.7 = (bf16[24,16,128]{2,1,0:T(8,128)(2,1)S(1)}, bf16[24,16,128]{2,1,0:T(8,128)(2,1)S(1)}, u32[]{:S(2)}, u32[]{:S(2)}) collective-permute-start(bf16[24,16,128]{2,1,0:T(8,128)(2,1)S(1)} %get-tuple-element.35), channel_id=1, source_target_pairs={{0,16},{16,0},{32,48},{48,32},{1,17},{17,1},{33,49},{49,33},{2,18}... | collective-permute-start | bytes 294920 | tf_op jit(solution)/shard_map/ppermute | solution.py:20
  25.2 11.4 %collective-permute-start.8 = (bf16[24,16,128]{2,1,0:T(8,128)(2,1)S(1)}, bf16[24,16,128]{2,1,0:T(8,128)(2,1)S(1)}, u32[]{:S(2)}, u32[]{:S(2)}) collective-permute-start(bf16[24,16,128]{2,1,0:T(8,128)(2,1)S(1)} %get-tuple-element.36), channel_id=1, source_target_pairs={{0,15},{1,2},{2,1},{3,4},{4,3},{5,6},{6,5},{7,8},{8,7},{9,10},{10,... | collective-permute-start | bytes 294920 | tf_op jit(solution)/shard_map/ppermute | solution.py:26
  29.2 7.4 %collective-permute-start.9 = (bf16[24,16,128]{2,1,0:T(8,128)(2,1)S(1)}, bf16[24,16,128]{2,1,0:T(8,128)(2,1)S(1)}, u32[]{:S(2)}, u32[]{:S(2)}) collective-permute-start(bf16[24,16,128]{2,1,0:T(8,128)(2,1)S(1)} %get-tuple-element.37), channel_id=1, source_target_pairs={{0,48},{16,32},{32,16},{48,0},{1,49},{17,33},{33,17},{49,1},{2,50}... | collective-permute-start | bytes 294920 | tf_op jit(solution)/shard_map/ppermute | solution.py:26
  30.2 6.3 %collective-permute-start.10 = (bf16[24,16,128]{2,1,0:T(8,128)(2,1)S(1)}, bf16[24,16,128]{2,1,0:T(8,128)(2,1)S(1)}, u32[]{:S(2)}, u32[]{:S(2)}) collective-permute-start(bf16[24,16,128]{2,1,0:T(8,128)(2,1)S(1)} %get-tuple-element.38), channel_id=1, source_target_pairs={{0,192},{64,128},{128,64},{192,0},{1,193},{65,129},{129,65},{193,1... | collective-permute-start | bytes 294920 | tf_op jit(solution)/shard_map/ppermute | solution.py:26
  32.5 4.8 %collective-permute-start.11 = (bf16[24,16,128]{2,1,0:T(8,128)(2,1)S(1)}, bf16[24,16,128]{2,1,0:T(8,128)(2,1)S(1)}, u32[]{:S(2)}, u32[]{:S(2)}) collective-permute-start(bf16[24,16,128]{2,1,0:T(8,128)(2,1)S(1)} %get-tuple-element.39), channel_id=1, source_target_pairs={{0,64},{64,0},{128,192},{192,128},{1,65},{65,1},{129,193},{193,129... | collective-permute-start | bytes 294920 | tf_op jit(solution)/shard_map/ppermute | solution.py:20
  32.6 4.7 %collective-permute-start.12 = (bf16[24,16,128]{2,1,0:T(8,128)(2,1)S(1)}, bf16[24,16,128]{2,1,0:T(8,128)(2,1)S(1)}, u32[]{:S(2)}, u32[]{:S(2)}) collective-permute-start(bf16[24,16,128]{2,1,0:T(8,128)(2,1)S(1)} %get-tuple-element.40), channel_id=1, source_target_pairs={{0,1},{1,0},{2,3},{3,2},{4,5},{5,4},{6,7},{7,6},{8,9},{9,8},{10,11... | collective-permute-start | bytes 294920 | tf_op jit(solution)/shard_map/ppermute | solution.py:20
  38.4 7.2 %collective-permute-start.13 = (f32[4,48,128]{2,1,0:T(8,128)S(1)}, f32[4,48,128]{2,1,0:T(8,128)S(1)}, u32[]{:S(2)}, u32[]{:S(2)}) collective-permute-start(f32[4,48,128]{2,1,0:T(8,128)S(1)} %get-tuple-element.42), channel_id=1, source_target_pairs={{0,128},{64,192},{128,0},{192,64},{1,129},{65,193},{129,1},{193,65... | collective-permute-start | bytes 294920 | tf_op jit(solution)/shard_map/ppermute | solution.py:20
  40.8 4.9 %collective-permute-start.14 = (f32[4,48,128]{2,1,0:T(8,128)S(1)}, f32[4,48,128]{2,1,0:T(8,128)S(1)}, u32[]{:S(2)}, u32[]{:S(2)}) collective-permute-start(f32[4,48,128]{2,1,0:T(8,128)S(1)} %get-tuple-element.43), channel_id=1, source_target_pairs={{0,64},{64,0},{128,192},{192,128},{1,65},{65,1},{129,193},{193,129... | collective-permute-start | bytes 294920 | tf_op jit(solution)/shard_map/ppermute | solution.py:20
  40.9 5.9 %collective-permute-start.15 = (f32[4,48,128]{2,1,0:T(8,128)S(1)}, f32[4,48,128]{2,1,0:T(8,128)S(1)}, u32[]{:S(2)}, u32[]{:S(2)}) collective-permute-start(f32[4,48,128]{2,1,0:T(8,128)S(1)} %get-tuple-element.44), channel_id=1, source_target_pairs={{0,192},{64,128},{128,64},{192,0},{1,193},{65,129},{129,65},{193,1... | collective-permute-start | bytes 294920 | tf_op jit(solution)/shard_map/ppermute | solution.py:20

commit v5 on v4

--- a/solution.py
+++ b/solution.py
@@ -27,15 +27,14 @@
 
 
 SWAPS = (0, 2, 1, 3)
-STARTS = ((3, 1, 2, 0), (2, 5, 3, 1, 0, 4))
-
-
-def exchange(faces):
-    names = AXES[-(len(faces) // 2):]
-    order = STARTS[len(faces) == 6]
+FIRST = (5, 3, 4, 2)
+EARLY, LATE = (2,), (5, 3, 1, 0, 4)
+
+
+def exchange(faces, numbers):
     moved = []
-    for number in order:
-        axis, face = names[number // 2], faces[number]
+    for number in numbers:
+        axis, face = AXES[number // 2], faces[number - 6 + len(faces)]
         moved.append(swap_other(face, axis) if number % 2 else swap(face, axis, 1))
     return moved
 
@@ -158,8 +157,11 @@
 def local_kernel(ny, links, v_ref, source, *refs):
     sites, columns = v_ref.shape[0], v_ref.shape[1]
     half = sites // 2
-    blocks = refs[:-3] if len(refs) > 2 else ()
-    total, vv = refs[len(blocks):len(blocks) + 2]
+    blocks = refs[:-3] if len(refs) > 3 else ()
+    early = () if blocks else refs[0]
+    total, vv = refs[-3:-1] if blocks else refs[-2:]
+    odd = parities()[1]
+    meets = [odd.astype(F32), (1 - odd).astype(F32)]
     if blocks:
         wide = refs[-1]
         widen(blocks, wide, [(0, half), (3 * half, half)])
@@ -167,7 +169,8 @@
         vv[i] = variants(v_ref[i])
     for y in range(ny):
         for x in range(2):
-            for z in range(2):
+            for side in range(2):
+                z = side
                 for t in range(2):
                     site = site_of(x, y, z, t, ny)
                     terms = [
@@ -184,12 +187,13 @@
                         row = x * half + (y * 2 + z) * 2 + t
                         vectors.append(variants(wide[pl.ds(row, columns, stride=sites), :]))
                         matrices.append(links[site, 2 - x])
+                    else:
+                        vectors.append(variants(early[(x * ny + y) * 2 + t].astype(F32) * meets[z]))
+                        matrices.append(links[site, 6 - z])
                     total[site] = source[site].astype(F32) - product(vectors, matrices)
 
 
-def near_terms(ny, links, total, moved, store):
-    order = STARTS[len(moved) == 6]
-    near = [moved[order.index(number)] for number in range(len(order))]
+def near_terms(ny, links, total, near, store):
     odd = parities()
     for y in range(ny):
         for side_x in range(2):
@@ -202,35 +206,41 @@
                     t = 1 - odd[2] if side_t == 0 else odd[2]
                     link_t = 7 + (odd[2] if side_t == 0 else 1 - odd[2])
                     site = site_of(x, y, z, t, ny)
-                    terms = [
-                        (link_z, near[-4 + side_z][(x * ny + y) * 2 + t]),
-                        (link_t, near[-2 + side_t][(x * ny + y) * 2 + z]),
+                    places = [
+                        (side_x, link_x, (y * 2 + z) * 2 + t),
+                        (2 + side_z, link_z, (x * ny + y) * 2 + t),
+                        (4 + side_t, link_t, (x * ny + y) * 2 + z),
                     ]
-                    if len(near) == 6:
-                        terms.append((link_x, near[side_x][(y * 2 + z) * 2 + t]))
-                    hop = product([variants(v) for _, v in terms], [links[site, k] for k, _ in terms])
-                    store(site, total[site] - hop)
-
-
-def near_kernel(ny, count, links, total, *refs):
-    moved, v_ref, faces = refs[:count], refs[count], refs[count + 1:]
+                    terms = [(k, near[f][i]) for f, k, i in places if f in near]
+                    value = total[site]
+                    if terms:
+                        value = value - product(
+                            [variants(v) for _, v in terms], [links[site, k] for k, _ in terms]
+                        )
+                    store(site, value)
+
+
+def near_kernel(ny, numbers, links, total, *refs):
+    near = dict(zip(numbers, refs))
+    v_ref, faces = refs[len(near)], refs[len(near) + 1:]
 
     def store(site, value):
         v_ref[site] = value.astype(BF)
 
-    near_terms(ny, links, total, moved, store)
+    near_terms(ny, links, total, near, store)
     write_faces(ny, v_ref, faces)
 
 
-def last_kernel(ny, count, links, total, *refs):
-    moved, outs, wide = refs[:count], refs[count:-1], refs[-1]
+def last_kernel(ny, numbers, links, total, *refs):
+    near = dict(zip(numbers, refs))
+    outs, wide = refs[len(near):-1], refs[-1]
     own, sites = outs[0].shape[0], outs[0].shape[1]
     columns = own * len(outs)
 
     def store(site, value):
         wide[pl.ds(site, columns, stride=sites), :] = value
 
-    near_terms(ny, links, total, moved, store)
+    near_terms(ny, links, total, near, store)
     me = lax.axis_index("sec")
     for k, out in zip(SWAPS, outs):
         at = (me ^ k) * (own * sites)
@@ -292,25 +302,24 @@
     )
     first = v
     for sweep in range(2):
-        moved = exchange(faces)
+        moved = exchange(faces, FIRST if sweep == 0 else EARLY)
+        late = [] if sweep == 0 else exchange(faces, LATE)
         total = call(
-            functools.partial(local_kernel, ny), "local", total_shape, [links, v, first] + blocks,
+            functools.partial(local_kernel, ny), "local", total_shape, [links, v, first] + (blocks or moved),
             [pltpu.VMEM((sites, 2 * columns, width), BF)] + [wide] * (sweep == 0),
             flops=6 * per_term, bytes_accessed=6 * link_bytes,
         )
         blocks = []
-        inputs = [links, total] + moved
         cost = dict(flops=3 * per_term, bytes_accessed=3 * link_bytes)
         if sweep == 0:
             v, *faces = call(
-                functools.partial(near_kernel, ny, len(moved)), "near", [whole] + [face] * 6,
-                inputs, [], **cost,
+                functools.partial(near_kernel, ny, FIRST), "near", [whole] + [face] * 6,
+                [links, total] + moved, [], **cost,
             )
         else:
             result = call(
-                functools.partial(last_kernel, ny, len(moved)), "last",
-                [shape((own, sites, width), F32)] * parts, inputs,
-                [wide], **cost,
+                functools.partial(last_kernel, ny, LATE), "last",
+                [shape((own, sites, width), F32)] * parts, [links, total] + late, [wide], **cost,
             )
     result = [result[0]] + [swap(part, "sec", k) for k, part in zip(SWAPS[1:], result[1:])]
     joined = call(

time: 47.8 us -> 47.6 us (level)
  waiting for transfers between devices: 11.8 us -> 11.3 us
  transfers between devices with their start and end apart: 16 -> 16, of which waited for: 9 -> 9; matrix products, arithmetic and copies ran while one was open for 0% -> 0% of each run, Pallas kernels for 14% -> 15%
where the time goes in v5:
time: 47.6 us; the launch traced here: 47.3 us
  starting transfers between devices  25.4 us (53%)
  waiting for transfers between devices  11.3 us (24%)
  Pallas kernels  10.6 us (22%)
    ppermute x5, starting transfers between devices, swap_other(): return lax.ppermute(array, axis, pairs)  15 us
    pallas_call x8, Pallas kernels, call(): pl.pallas_call(kernel, out_shape=out_shape, in_specs=places or [VM] * len...  10.6 us
    ppermute x11, starting transfers between devices, swap(): return lax.ppermute(array, axis, [(i, i ^ distance) for i in range(count)])  10.4 us
    ppermute x11, waiting for transfers between devices, swap(): return lax.ppermute(array, axis, [(i, i ^ distance) for i in range(count)])  7.63 us
    ppermute x5, waiting for transfers between devices, swap_other(): return lax.ppermute(array, axis, pairs)  3.71 us
  transfers between devices with their start and end apart: 16, of which 9 were waited for; matrix products, arithmetic and copies ran while one was open for 0% of the time, Pallas kernels for 15%

profile of v5, /device:TPU:32, one launch (start us, length us, event | category | flops | bytes accessed | tf_op | source)
XLA Modules:
  0.0 47.3 jit_solution(17959654422728425247)
XLA Ops:
  0.0 1.1 %split.1 = (bf16[4,4,24,128]{3,2,1,0:T(8,128)(2,1)S(1)}, bf16[4,4,24,128]{3,2,1,0:T(8,128)(2,1)S(1)}, bf16[4,4,24,128]{3,2,1,0:T(8,128)(2,1)S(1)}, bf16[4,4,24,128]{3,2,1,0:T(8,128)(2,1)S(1)}) custom-call(bf16[4,8,24,128]{3,2,1,0:T(8,128)(2,1)} %bitcast.16), custom_call_target="tpu_custom_call" | custom-call | bytes 393216 | tf_op jit(solution)/shard_map/split/pallas_call | solution.py:254
  1.1 3.3 %collective-permute-start = (bf16[4,4,24,128]{3,2,1,0:T(8,128)(2,1)S(1)}, bf16[4,4,24,128]{3,2,1,0:T(8,128)(2,1)S(1)}, u32[]{:S(2)}, u32[]{:S(2)}) collective-permute-start(bf16[4,4,24,128]{3,2,1,0:T(8,128)(2,1)S(1)} %get-tuple-element.26), channel_id=1, source_target_pairs={{0,128},{64,192},{128,0},{192,64},{1,129},{65,193},{129,1},{193,65... | collective-permute-start | bytes 294920 | tf_op jit(solution)/shard_map/ppermute | solution.py:20
  4.4 0.7 %collective-permute-start.1 = (bf16[4,4,24,128]{3,2,1,0:T(8,128)(2,1)S(1)}, bf16[4,4,24,128]{3,2,1,0:T(8,128)(2,1)S(1)}, u32[]{:S(2)}, u32[]{:S(2)}) collective-permute-start(bf16[4,4,24,128]{3,2,1,0:T(8,128)(2,1)S(1)} %get-tuple-element.27), channel_id=1, source_target_pairs={{0,64},{64,0},{128,192},{192,128},{1,65},{65,1},{129,193},{193,129... | collective-permute-start | bytes 294920 | tf_op jit(solution)/shard_map/ppermute | solution.py:20
  5.0 0.4 collective-permute-start.2
  5.4 3.1 %load.1.refs_4_.links = bf16[48,9,64,128]{3,2,1,0:T(8,128)(2,1)S(1)} custom-call(bf16[48,9,64,128]{3,2,1,0:T(8,128)(2,1)} %bitcast.15), custom_call_target="tpu_custom_call" | custom-call | bytes 14155776 | tf_op jit(solution)/shard_map/load/pallas_call | solution.py:254
  8.5 0.0 collective-permute-done
  8.5 1.1 %collective-permute-done.1 = bf16[4,4,24,128]{3,2,1,0:T(8,128)(2,1)S(1)} collective-permute-done((bf16[4,4,24,128]{3,2,1,0:T(8,128)(2,1)S(1)}, bf16[4,4,24,128]{3,2,1,0:T(8,128)(2,1)S(1)}, u32[]{:S(2)}, u32[]{:S(2)}) %collective-permute-start.1) | collective-permute-done | bytes 98336 | tf_op jit(solution)/shard_map/ppermute | solution.py:20
  9.7 1.2 %collective-permute-done.2 = bf16[4,4,24,128]{3,2,1,0:T(8,128)(2,1)S(1)} collective-permute-done((bf16[4,4,24,128]{3,2,1,0:T(8,128)(2,1)S(1)}, bf16[4,4,24,128]{3,2,1,0:T(8,128)(2,1)S(1)}, u32[]{:S(2)}, u32[]{:S(2)}) %collective-permute-start.2) | collective-permute-done | bytes 98336 | tf_op jit(solution)/shard_map/ppermute | solution.py:20
  10.9 0.2 pack.1
  11.1 7.7 %collective-permute-start.3 = (bf16[24,16,128]{2,1,0:T(8,128)(2,1)S(1)}, bf16[24,16,128]{2,1,0:T(8,128)(2,1)S(1)}, u32[]{:S(2)}, u32[]{:S(2)}) collective-permute-start(bf16[24,16,128]{2,1,0:T(8,128)(2,1)S(1)} %get-tuple-element.30), channel_id=1, source_target_pairs={{0,15},{1,2},{2,1},{3,4},{4,3},{5,6},{6,5},{7,8},{8,7},{9,10},{10,... | collective-permute-start | bytes 294920 | tf_op jit(solution)/shard_map/ppermute | solution.py:26
  18.8 1.1 %collective-permute-start.6 = (bf16[24,16,128]{2,1,0:T(8,128)(2,1)S(1)}, bf16[24,16,128]{2,1,0:T(8,128)(2,1)S(1)}, u32[]{:S(2)}, u32[]{:S(2)}) collective-permute-start(bf16[24,16,128]{2,1,0:T(8,128)(2,1)S(1)} %get-tuple-element.33), channel_id=1, source_target_pairs={{0,16},{16,0},{32,48},{48,32},{1,17},{17,1},{33,49},{49,33},{2,18}... | collective-permute-start | bytes 294920 | tf_op jit(solution)/shard_map/ppermute | solution.py:20
  19.9 1.9 %local.2.total = f32[48,16,128]{2,1,0:T(8,128)S(1)} custom-call(bf16[48,9,64,128]{3,2,1,0:T(8,128)(2,1)S(1)} %load.1.refs_4_.links, bf16[48,16,128]{2,1,0:T(8,128)(2,1)S(1)} %get-tuple-element.29.v_ref.source, bf16[48,16,128]{2,1,0:T(8,128)(2,1)S(1)} %get-tuple-element.29.v_ref.source, bf16[4,96,128]{2,1,0:T(8,128)(2,1)S(1)} %bitcast.8, ...), custom_call_target="tpu_custom_call" | custom-call | flops 150994944 | bytes 4718592 | tf_op jit(solution)/shard_map/local/pallas_call | solution.py:254
  21.8 0.2 collective-permute-done.3.refs_0_
  22.0 1.4 %collective-permute-done.4.refs_1_ = bf16[24,16,128]{2,1,0:T(8,128)(2,1)S(1)} collective-permute-done((bf16[24,16,128]{2,1,0:T(8,128)(2,1)S(1)}, bf16[24,16,128]{2,1,0:T(8,128)(2,1)S(1)}, u32[]{:S(2)}, u32[]{:S(2)}) %collective-permute-start.4) | collective-permute-done | bytes 98336 | tf_op jit(solution)/shard_map/ppermute | solution.py:26
  23.4 0.9 %collective-permute-done.5.refs_2_ = bf16[24,16,128]{2,1,0:T(8,128)(2,1)S(1)} collective-permute-done((bf16[24,16,128]{2,1,0:T(8,128)(2,1)S(1)}, bf16[24,16,128]{2,1,0:T(8,128)(2,1)S(1)}, u32[]{:S(2)}, u32[]{:S(2)}) %collective-permute-start.5) | collective-permute-done | bytes 98336 | tf_op jit(solution)/shard_map/ppermute | solution.py:20
  24.3 0.7 %near.1 = (bf16[48,16,128]{2,1,0:T(8,128)(2,1)S(1)}, bf16[24,16,128]{2,1,0:T(8,128)(2,1)S(1)}, bf16[24,16,128]{2,1,0:T(8,128)(2,1)S(1)}, bf16[24,16,128]{2,1,0:T...) custom-call(bf16[48,9,64,128]{3,2,1,0:T(8,128)(2,1)S(1)} %load.1.ref, ...), custom_call_target="tpu_custom_call" | custom-call | flops 75497472 | bytes 2359296 | tf_op jit(solution)/shard_map/near/pallas_call | solution.py:254
  25.0 0.2 collective-permute-start.7
  25.2 4.0 %collective-permute-start.8 = (bf16[24,16,128]{2,1,0:T(8,128)(2,1)S(1)}, bf16[24,16,128]{2,1,0:T(8,128)(2,1)S(1)}, u32[]{:S(2)}, u32[]{:S(2)}) collective-permute-start(bf16[24,16,128]{2,1,0:T(8,128)(2,1)S(1)} %get-tuple-element.36), channel_id=1, source_target_pairs={{0,15},{1,2},{2,1},{3,4},{4,3},{5,6},{6,5},{7,8},{8,7},{9,10},{10,... | collective-permute-start | bytes 294920 | tf_op jit(solution)/shard_map/ppermute | solution.py:26
  29.2 1.0 %collective-permute-start.9 = (bf16[24,16,128]{2,1,0:T(8,128)(2,1)S(1)}, bf16[24,16,128]{2,1,0:T(8,128)(2,1)S(1)}, u32[]{:S(2)}, u32[]{:S(2)}) collective-permute-start(bf16[24,16,128]{2,1,0:T(8,128)(2,1)S(1)} %get-tuple-element.37), channel_id=1, source_target_pairs={{0,48},{16,32},{32,16},{48,0},{1,49},{17,33},{33,17},{49,1},{2,50}... | collective-permute-start | bytes 294920 | tf_op jit(solution)/shard_map/ppermute | solution.py:26
  30.2 2.3 %collective-permute-start.10 = (bf16[24,16,128]{2,1,0:T(8,128)(2,1)S(1)}, bf16[24,16,128]{2,1,0:T(8,128)(2,1)S(1)}, u32[]{:S(2)}, u32[]{:S(2)}) collective-permute-start(bf16[24,16,128]{2,1,0:T(8,128)(2,1)S(1)} %get-tuple-element.38), channel_id=1, source_target_pairs={{0,192},{64,128},{128,64},{192,0},{1,193},{65,129},{129,65},{193,1... | collective-permute-start | bytes 294920 | tf_op jit(solution)/shard_map/ppermute | solution.py:26
  32.5 0.1 collective-permute-start.11
  32.6 1.9 %local.3.total = f32[48,16,128]{2,1,0:T(8,128)S(1)} custom-call(bf16[48,9,64,128]{3,2,1,0:T(8,128)(2,1)S(1)} %load.1.refs_4_.links, bf16[48,16,128]{2,1,0:T(8,128)(2,1)S(1)} %get-tuple-element.34.v_ref, bf16[48,16,128]{2,1,0:T(8,128)(2,1)S(1)} %get-tuple-element.29.v_ref.source, bf16[24,16,128]{2,1,0:T(8,128)(2,1)S(1)} %collective-permute-done.7.refs_0_), custom_call_target="tpu_custom_call" | custom-call | flops 150994944 | bytes 4718592 | tf_op jit(solution)/shard_map/local/pallas_call | solution.py:254
  34.5 2.1 %collective-permute-done.8.refs_0_ = bf16[24,16,128]{2,1,0:T(8,128)(2,1)S(1)} collective-permute-done((bf16[24,16,128]{2,1,0:T(8,128)(2,1)S(1)}, bf16[24,16,128]{2,1,0:T(8,128)(2,1)S(1)}, u32[]{:S(2)}, u32[]{:S(2)}) %collective-permute-start.8) | collective-permute-done | bytes 98336 | tf_op jit(solution)/shard_map/ppermute | solution.py:26
  36.6 0.7 %collective-permute-done.11.refs_3_ = bf16[24,16,128]{2,1,0:T(8,128)(2,1)S(1)} collective-permute-done((bf16[24,16,128]{2,1,0:T(8,128)(2,1)S(1)}, bf16[24,16,128]{2,1,0:T(8,128)(2,1)S(1)}, u32[]{:S(2)}, u32[]{:S(2)}) %collective-permute-start.11) | collective-permute-done | bytes 98336 | tf_op jit(solution)/shard_map/ppermute | solution.py:20
  37.3 0.0 collective-permute-done.12.refs_4_
  37.3 0.9 %last.1 = (f32[4,48,128]{2,1,0:T(8,128)S(1)}, f32[4,48,128]{2,1,0:T(8,128)S(1)}, f32[4,48,128]{2,1,0:T(8,128)S(1)}, f32[4,48,128]{2,1,0:T(8,128)S(1)}) custom-call(bf16[48,9,64,128]{3,2,1,0:T(8,128)(2,1)S(1)} %load.1.refs_4_.links, f32[48,16,128]{2,1,0:T(8,128)S(1)} %local.3.total, bf16[24,16,128]{2,1,0:T(8,128)(2,1)S(1)} %collective-permute-done.8.refs_0_, ...), custom_call_target="tpu_custom_call" | custom-call | flops 75497472 | bytes 2359296 | tf_op jit(solution)/shard_map/last/pallas_call | solution.py:254
  38.2 2.4 %collective-permute-start.13 = (f32[4,48,128]{2,1,0:T(8,128)S(1)}, f32[4,48,128]{2,1,0:T(8,128)S(1)}, u32[]{:S(2)}, u32[]{:S(2)}) collective-permute-start(f32[4,48,128]{2,1,0:T(8,128)S(1)} %get-tuple-element.42), channel_id=1, source_target_pairs={{0,128},{64,192},{128,0},{192,64},{1,129},{65,193},{129,1},{193,65... | collective-permute-start | bytes 294920 | tf_op jit(solution)/shard_map/ppermute | solution.py:20
  40.6 0.1 collective-permute-start.14
  40.7 2.2 %collective-permute-start.15 = (f32[4,48,128]{2,1,0:T(8,128)S(1)}, f32[4,48,128]{2,1,0:T(8,128)S(1)}, u32[]{:S(2)}, u32[]{:S(2)}) collective-permute-start(f32[4,48,128]{2,1,0:T(8,128)S(1)} %get-tuple-element.44), channel_id=1, source_target_pairs={{0,192},{64,128},{128,64},{192,0},{1,193},{65,129},{129,65},{193,1... | collective-permute-start | bytes 294920 | tf_op jit(solution)/shard_map/ppermute | solution.py:20
  42.8 2.6 %collective-permute-done.13.refs_1_ = f32[4,48,128]{2,1,0:T(8,128)S(1)} collective-permute-done((f32[4,48,128]{2,1,0:T(8,128)S(1)}, f32[4,48,128]{2,1,0:T(8,128)S(1)}, u32[]{:S(2)}, u32[]{:S(2)}) %collective-permute-start.13) | collective-permute-done | bytes 98336 | tf_op jit(solution)/shard_map/ppermute | solution.py:20
  45.4 1.1 %collective-permute-done.15.refs_3_ = f32[4,48,128]{2,1,0:T(8,128)S(1)} collective-permute-done((f32[4,48,128]{2,1,0:T(8,128)S(1)}, f32[4,48,128]{2,1,0:T(8,128)S(1)}, u32[]{:S(2)}, u32[]{:S(2)}) %collective-permute-start.15) | collective-permute-done | bytes 98336 | tf_op jit(solution)/shard_map/ppermute | solution.py:20
  46.6 0.8 %join.1 = f32[4,4,48,128]{3,2,1,0:T(8,128)} custom-call(f32[4,48,128]{2,1,0:T(8,128)S(1)} %get-tuple-element.41.refs_0_, f32[4,48,128]{2,1,0:T(8,128)S(1)} %collective-permute-done.13.refs_1_, f32[4,48,128]{2,1,0:T(8,128)S(1)} %collective-permute-done.14.refs_2_, f32[4,48,128]{2,1,0:T(8,128)S(1)} %collective-permute-done.15.refs_3_), custom_call_target="tpu_custom_call" | custom-call | bytes 786432 | tf_op jit(solution)/shard_map/join/pallas_call | solution.py:254
  (8 shorter events, 0.0 us)
Async XLA Ops:
  1.1 7.4 %collective-permute-start = (bf16[4,4,24,128]{3,2,1,0:T(8,128)(2,1)S(1)}, bf16[4,4,24,128]{3,2,1,0:T(8,128)(2,1)S(1)}, u32[]{:S(2)}, u32[]{:S(2)}) collective-permute-start(bf16[4,4,24,128]{3,2,1,0:T(8,128)(2,1)S(1)} %get-tuple-element.26), channel_id=1, source_target_pairs={{0,128},{64,192},{128,0},{192,64},{1,129},{65,193},{129,1},{193,65... | collective-permute-start | bytes 294920 | tf_op jit(solution)/shard_map/ppermute | solution.py:20
  4.4 5.3 %collective-permute-start.1 = (bf16[4,4,24,128]{3,2,1,0:T(8,128)(2,1)S(1)}, bf16[4,4,24,128]{3,2,1,0:T(8,128)(2,1)S(1)}, u32[]{:S(2)}, u32[]{:S(2)}) collective-permute-start(bf16[4,4,24,128]{3,2,1,0:T(8,128)(2,1)S(1)} %get-tuple-element.27), channel_id=1, source_target_pairs={{0,64},{64,0},{128,192},{192,128},{1,65},{65,1},{129,193},{193,129... | collective-permute-start | bytes 294920 | tf_op jit(solution)/shard_map/ppermute | solution.py:20
  5.0 5.8 %collective-permute-start.2 = (bf16[4,4,24,128]{3,2,1,0:T(8,128)(2,1)S(1)}, bf16[4,4,24,128]{3,2,1,0:T(8,128)(2,1)S(1)}, u32[]{:S(2)}, u32[]{:S(2)}) collective-permute-start(bf16[4,4,24,128]{3,2,1,0:T(8,128)(2,1)S(1)} %get-tuple-element.28), channel_id=1, source_target_pairs={{0,192},{64,128},{128,64},{192,0},{1,193},{65,129},{129,65},{193,1... | collective-permute-start | bytes 294920 | tf_op jit(solution)/shard_map/ppermute | solution.py:20
  11.1 11.0 %collective-permute-start.3 = (bf16[24,16,128]{2,1,0:T(8,128)(2,1)S(1)}, bf16[24,16,128]{2,1,0:T(8,128)(2,1)S(1)}, u32[]{:S(2)}, u32[]{:S(2)}) collective-permute-start(bf16[24,16,128]{2,1,0:T(8,128)(2,1)S(1)} %get-tuple-element.30), channel_id=1, source_target_pairs={{0,15},{1,2},{2,1},{3,4},{4,3},{5,6},{6,5},{7,8},{8,7},{9,10},{10,... | collective-permute-start | bytes 294920 | tf_op jit(solution)/shard_map/ppermute | solution.py:26
  18.7 4.7 %collective-permute-start.4 = (bf16[24,16,128]{2,1,0:T(8,128)(2,1)S(1)}, bf16[24,16,128]{2,1,0:T(8,128)(2,1)S(1)}, u32[]{:S(2)}, u32[]{:S(2)}) collective-permute-start(bf16[24,16,128]{2,1,0:T(8,128)(2,1)S(1)} %get-tuple-element.31), channel_id=1, source_target_pairs={{0,48},{16,32},{32,16},{48,0},{1,49},{17,33},{33,17},{49,1},{2,50}... | collective-permute-start | bytes 294920 | tf_op jit(solution)/shard_map/ppermute | solution.py:26
  18.7 5.5 %collective-permute-start.5 = (bf16[24,16,128]{2,1,0:T(8,128)(2,1)S(1)}, bf16[24,16,128]{2,1,0:T(8,128)(2,1)S(1)}, u32[]{:S(2)}, u32[]{:S(2)}) collective-permute-start(bf16[24,16,128]{2,1,0:T(8,128)(2,1)S(1)} %get-tuple-element.32), channel_id=1, source_target_pairs={{0,1},{1,0},{2,3},{3,2},{4,5},{5,4},{6,7},{7,6},{8,9},{9,8},{10,11... | collective-permute-start | bytes 294920 | tf_op jit(solution)/shard_map/ppermute | solution.py:20
  18.8 5.5 %collective-permute-start.6 = (bf16[24,16,128]{2,1,0:T(8,128)(2,1)S(1)}, bf16[24,16,128]{2,1,0:T(8,128)(2,1)S(1)}, u32[]{:S(2)}, u32[]{:S(2)}) collective-permute-start(bf16[24,16,128]{2,1,0:T(8,128)(2,1)S(1)} %get-tuple-element.33), channel_id=1, source_target_pairs={{0,16},{16,0},{32,48},{48,32},{1,17},{17,1},{33,49},{49,33},{2,18}... | collective-permute-start | bytes 294920 | tf_op jit(solution)/shard_map/ppermute | solution.py:20
  25.0 7.6 %collective-permute-start.7 = (bf16[24,16,128]{2,1,0:T(8,128)(2,1)S(1)}, bf16[24,16,128]{2,1,0:T(8,128)(2,1)S(1)}, u32[]{:S(2)}, u32[]{:S(2)}) collective-permute-start(bf16[24,16,128]{2,1,0:T(8,128)(2,1)S(1)} %get-tuple-element.35), channel_id=1, source_target_pairs={{0,16},{16,0},{32,48},{48,32},{1,17},{17,1},{33,49},{49,33},{2,18}... | collective-permute-start | bytes 294920 | tf_op jit(solution)/shard_map/ppermute | solution.py:20
  25.2 11.4 %collective-permute-start.8 = (bf16[24,16,128]{2,1,0:T(8,128)(2,1)S(1)}, bf16[24,16,128]{2,1,0:T(8,128)(2,1)S(1)}, u32[]{:S(2)}, u32[]{:S(2)}) collective-permute-start(bf16[24,16,128]{2,1,0:T(8,128)(2,1)S(1)} %get-tuple-element.36), channel_id=1, source_target_pairs={{0,15},{1,2},{2,1},{3,4},{4,3},{5,6},{6,5},{7,8},{8,7},{9,10},{10,... | collective-permute-start | bytes 294920 | tf_op jit(solution)/shard_map/ppermute | solution.py:26
  29.2 7.4 %collective-permute-start.9 = (bf16[24,16,128]{2,1,0:T(8,128)(2,1)S(1)}, bf16[24,16,128]{2,1,0:T(8,128)(2,1)S(1)}, u32[]{:S(2)}, u32[]{:S(2)}) collective-permute-start(bf16[24,16,128]{2,1,0:T(8,128)(2,1)S(1)} %get-tuple-element.37), channel_id=1, source_target_pairs={{0,48},{16,32},{32,16},{48,0},{1,49},{17,33},{33,17},{49,1},{2,50}... | collective-permute-start | bytes 294920 | tf_op jit(solution)/shard_map/ppermute | solution.py:26
  30.2 6.3 %collective-permute-start.10 = (bf16[24,16,128]{2,1,0:T(8,128)(2,1)S(1)}, bf16[24,16,128]{2,1,0:T(8,128)(2,1)S(1)}, u32[]{:S(2)}, u32[]{:S(2)}) collective-permute-start(bf16[24,16,128]{2,1,0:T(8,128)(2,1)S(1)} %get-tuple-element.38), channel_id=1, source_target_pairs={{0,192},{64,128},{128,64},{192,0},{1,193},{65,129},{129,65},{193,1... | collective-permute-start | bytes 294920 | tf_op jit(solution)/shard_map/ppermute | solution.py:26
  32.5 4.8 %collective-permute-start.11 = (bf16[24,16,128]{2,1,0:T(8,128)(2,1)S(1)}, bf16[24,16,128]{2,1,0:T(8,128)(2,1)S(1)}, u32[]{:S(2)}, u32[]{:S(2)}) collective-permute-start(bf16[24,16,128]{2,1,0:T(8,128)(2,1)S(1)} %get-tuple-element.39), channel_id=1, source_target_pairs={{0,64},{64,0},{128,192},{192,128},{1,65},{65,1},{129,193},{193,129... | collective-permute-start | bytes 294920 | tf_op jit(solution)/shard_map/ppermute | solution.py:20
  32.6 4.7 %collective-permute-start.12 = (bf16[24,16,128]{2,1,0:T(8,128)(2,1)S(1)}, bf16[24,16,128]{2,1,0:T(8,128)(2,1)S(1)}, u32[]{:S(2)}, u32[]{:S(2)}) collective-permute-start(bf16[24,16,128]{2,1,0:T(8,128)(2,1)S(1)} %get-tuple-element.40), channel_id=1, source_target_pairs={{0,1},{1,0},{2,3},{3,2},{4,5},{5,4},{6,7},{7,6},{8,9},{9,8},{10,11... | collective-permute-start | bytes 294920 | tf_op jit(solution)/shard_map/ppermute | solution.py:20
  38.2 7.2 %collective-permute-start.13 = (f32[4,48,128]{2,1,0:T(8,128)S(1)}, f32[4,48,128]{2,1,0:T(8,128)S(1)}, u32[]{:S(2)}, u32[]{:S(2)}) collective-permute-start(f32[4,48,128]{2,1,0:T(8,128)S(1)} %get-tuple-element.42), channel_id=1, source_target_pairs={{0,128},{64,192},{128,0},{192,64},{1,129},{65,193},{129,1},{193,65... | collective-permute-start | bytes 294920 | tf_op jit(solution)/shard_map/ppermute | solution.py:20
  40.6 4.9 %collective-permute-start.14 = (f32[4,48,128]{2,1,0:T(8,128)S(1)}, f32[4,48,128]{2,1,0:T(8,128)S(1)}, u32[]{:S(2)}, u32[]{:S(2)}) collective-permute-start(f32[4,48,128]{2,1,0:T(8,128)S(1)} %get-tuple-element.43), channel_id=1, source_target_pairs={{0,64},{64,0},{128,192},{192,128},{1,65},{65,1},{129,193},{193,129... | collective-permute-start | bytes 294920 | tf_op jit(solution)/shard_map/ppermute | solution.py:20
  40.7 5.9 %collective-permute-start.15 = (f32[4,48,128]{2,1,0:T(8,128)S(1)}, f32[4,48,128]{2,1,0:T(8,128)S(1)}, u32[]{:S(2)}, u32[]{:S(2)}) collective-permute-start(f32[4,48,128]{2,1,0:T(8,128)S(1)} %get-tuple-element.44), channel_id=1, source_target_pairs={{0,192},{64,128},{128,64},{192,0},{1,193},{65,129},{129,65},{193,1... | collective-permute-start | bytes 294920 | tf_op jit(solution)/shard_map/ppermute | solution.py:20

commit v6 on v5

--- a/solution.py
+++ b/solution.py
@@ -120,11 +120,11 @@
         copy.wait()
 
 
-def join_kernel(*refs):
-    parts, out, sems = refs[:-2], refs[-2], refs[-1]
+def join_kernel(order, *refs):
+    parts, out, sems = refs[:len(order)], refs[-2], refs[-1]
     me = lax.axis_index("sec")
     copies = []
-    for number, (k, part) in enumerate(zip(SWAPS, parts)):
+    for number, (k, part) in enumerate(zip(order, parts)):
         copies.append(pltpu.make_async_copy(part, out.at[:, me ^ k], sems.at[number]))
         copies[-1].start()
     for copy in copies:
@@ -249,7 +249,7 @@
             out[c] = wide[pl.ds(start, sites), :]
 
 
-def call(kernel, name, out_shape, inputs, scratch, flops=0, bytes_accessed=0, places=None, out_place=VM):
+def call(kernel, name, out_shape, inputs, scratch, flops=0, bytes_accessed=0, places=None, out_place=VM, aliases=None):
     several = isinstance(out_shape, list)
     return pl.pallas_call(
         kernel,
@@ -257,6 +257,7 @@
         in_specs=places or [VM] * len(inputs),
         out_specs=[out_place] * len(out_shape) if several else out_place,
         scratch_shapes=scratch,
+        input_output_aliases=aliases or {},
         compiler_params=pltpu.CompilerParams(vmem_limit_bytes=40 * 1024 * 1024),
         cost_estimate=pl.CostEstimate(
             flops=flops, bytes_accessed=bytes_accessed, transcendentals=0
@@ -322,9 +323,15 @@
                 [shape((own, sites, width), F32)] * parts, [links, total] + late, [wide], **cost,
             )
     result = [result[0]] + [swap(part, "sec", k) for k, part in zip(SWAPS[1:], result[1:])]
+    joined = shape((own, parts, sites, width), F32)
     joined = call(
-        join_kernel, "join", shape((own, parts, sites, width), F32), result, [dma((parts,))],
-        bytes_accessed=source.size * 8, out_place=HBM,
+        functools.partial(join_kernel, SWAPS[:2]), "join", joined, result[:2], [dma((2,))],
+        bytes_accessed=source.size * 4, out_place=HBM,
+    )
+    joined = call(
+        functools.partial(join_kernel, SWAPS[2:]), "join", shape(joined.shape, F32),
+        result[2:] + [joined], [dma((2,))], bytes_accessed=source.size * 4,
+        places=[VM] * 2 + [HBM], out_place=HBM, aliases={2: 0},
     )
     return joined.reshape(source.shape)
 

time: 47.6 us -> 47.5 us (level)
  waiting for transfers between devices: 11.3 us -> 10.6 us
  Pallas kernels: 10.6 us -> 11.2 us
    ppermute x11, waiting for transfers between devices: 7.63 us -> 6.93 us  [swap(): return lax.ppermute(array, axis, [(i, i ^ distance) for i in range(count)])]
    pallas_call x8 -> x9, Pallas kernels: 10.6 us -> 11.2 us  [call(): pl.pallas_call(kernel, out_shape=out_shape, in_specs=places or [VM] * len...]
  transfers between devices with their start and end apart: 16 -> 16, of which waited for: 9 -> 9; matrix products, arithmetic and copies ran while one was open for 0% -> 0% of each run, Pallas kernels for 15% -> 16%
where the time goes in v6:
time: 47.5 us; the launch traced here: 47.3 us
  starting transfers between devices  25.4 us (53%)
  Pallas kernels  11.2 us (24%)
  waiting for transfers between devices  10.6 us (22%)
    ppermute x5, starting transfers between devices, swap_other(): return lax.ppermute(array, axis, pairs)  15 us
    pallas_call x9, Pallas kernels, call(): pl.pallas_call(kernel, out_shape=out_shape, in_specs=places or [VM] * len...  11.2 us
    ppermute x11, starting transfers between devices, swap(): return lax.ppermute(array, axis, [(i, i ^ distance) for i in range(count)])  10.4 us
    ppermute x11, waiting for transfers between devices, swap(): return lax.ppermute(array, axis, [(i, i ^ distance) for i in range(count)])  6.93 us
    ppermute x5, waiting for transfers between devices, swap_other(): return lax.ppermute(array, axis, pairs)  3.71 us
  transfers between devices with their start and end apart: 16, of which 9 were waited for; matrix products, arithmetic and copies ran while one was open for 0% of the time, Pallas kernels for 16%

profile of v6, /device:TPU:32, one launch (start us, length us, event | category | flops | bytes accessed | tf_op | source)
XLA Modules:
  0.0 47.3 jit_solution(15589614039617463357)
XLA Ops:
  0.0 1.1 %split.1 = (bf16[4,4,24,128]{3,2,1,0:T(8,128)(2,1)S(1)}, bf16[4,4,24,128]{3,2,1,0:T(8,128)(2,1)S(1)}, bf16[4,4,24,128]{3,2,1,0:T(8,128)(2,1)S(1)}, bf16[4,4,24,128]{3,2,1,0:T(8,128)(2,1)S(1)}) custom-call(bf16[4,8,24,128]{3,2,1,0:T(8,128)(2,1)} %bitcast.16), custom_call_target="tpu_custom_call" | custom-call | bytes 393216 | tf_op jit(solution)/shard_map/split/pallas_call | solution.py:254
  1.1 3.3 %collective-permute-start = (bf16[4,4,24,128]{3,2,1,0:T(8,128)(2,1)S(1)}, bf16[4,4,24,128]{3,2,1,0:T(8,128)(2,1)S(1)}, u32[]{:S(2)}, u32[]{:S(2)}) collective-permute-start(bf16[4,4,24,128]{3,2,1,0:T(8,128)(2,1)S(1)} %get-tuple-element.26), channel_id=1, source_target_pairs={{0,128},{64,192},{128,0},{192,64},{1,129},{65,193},{129,1},{193,65... | collective-permute-start | bytes 294920 | tf_op jit(solution)/shard_map/ppermute | solution.py:20
  4.4 0.7 %collective-permute-start.1 = (bf16[4,4,24,128]{3,2,1,0:T(8,128)(2,1)S(1)}, bf16[4,4,24,128]{3,2,1,0:T(8,128)(2,1)S(1)}, u32[]{:S(2)}, u32[]{:S(2)}) collective-permute-start(bf16[4,4,24,128]{3,2,1,0:T(8,128)(2,1)S(1)} %get-tuple-element.27), channel_id=1, source_target_pairs={{0,64},{64,0},{128,192},{192,128},{1,65},{65,1},{129,193},{193,129... | collective-permute-start | bytes 294920 | tf_op jit(solution)/shard_map/ppermute | solution.py:20
  5.0 0.4 collective-permute-start.2
  5.4 3.1 %load.1.refs_4_.links = bf16[48,9,64,128]{3,2,1,0:T(8,128)(2,1)S(1)} custom-call(bf16[48,9,64,128]{3,2,1,0:T(8,128)(2,1)} %bitcast.15), custom_call_target="tpu_custom_call" | custom-call | bytes 14155776 | tf_op jit(solution)/shard_map/load/pallas_call | solution.py:254
  8.5 1.1 %collective-permute-done.1 = bf16[4,4,24,128]{3,2,1,0:T(8,128)(2,1)S(1)} collective-permute-done((bf16[4,4,24,128]{3,2,1,0:T(8,128)(2,1)S(1)}, bf16[4,4,24,128]{3,2,1,0:T(8,128)(2,1)S(1)}, u32[]{:S(2)}, u32[]{:S(2)}) %collective-permute-start.1) | collective-permute-done | bytes 98336 | tf_op jit(solution)/shard_map/ppermute | solution.py:20
  9.7 1.2 %collective-permute-done.2 = bf16[4,4,24,128]{3,2,1,0:T(8,128)(2,1)S(1)} collective-permute-done((bf16[4,4,24,128]{3,2,1,0:T(8,128)(2,1)S(1)}, bf16[4,4,24,128]{3,2,1,0:T(8,128)(2,1)S(1)}, u32[]{:S(2)}, u32[]{:S(2)}) %collective-permute-start.2) | collective-permute-done | bytes 98336 | tf_op jit(solution)/shard_map/ppermute | solution.py:20
  10.9 0.2 pack.1
  11.1 7.7 %collective-permute-start.3 = (bf16[24,16,128]{2,1,0:T(8,128)(2,1)S(1)}, bf16[24,16,128]{2,1,0:T(8,128)(2,1)S(1)}, u32[]{:S(2)}, u32[]{:S(2)}) collective-permute-start(bf16[24,16,128]{2,1,0:T(8,128)(2,1)S(1)} %get-tuple-element.30), channel_id=1, source_target_pairs={{0,15},{1,2},{2,1},{3,4},{4,3},{5,6},{6,5},{7,8},{8,7},{9,10},{10,... | collective-permute-start | bytes 294920 | tf_op jit(solution)/shard_map/ppermute | solution.py:26
  18.8 1.1 %collective-permute-start.6 = (bf16[24,16,128]{2,1,0:T(8,128)(2,1)S(1)}, bf16[24,16,128]{2,1,0:T(8,128)(2,1)S(1)}, u32[]{:S(2)}, u32[]{:S(2)}) collective-permute-start(bf16[24,16,128]{2,1,0:T(8,128)(2,1)S(1)} %get-tuple-element.33), channel_id=1, source_target_pairs={{0,16},{16,0},{32,48},{48,32},{1,17},{17,1},{33,49},{49,33},{2,18}... | collective-permute-start | bytes 294920 | tf_op jit(solution)/shard_map/ppermute | solution.py:20
  19.9 1.9 %local.2.total = f32[48,16,128]{2,1,0:T(8,128)S(1)} custom-call(bf16[48,9,64,128]{3,2,1,0:T(8,128)(2,1)S(1)} %load.1.refs_4_.links, bf16[48,16,128]{2,1,0:T(8,128)(2,1)S(1)} %get-tuple-element.29.v_ref.source, bf16[48,16,128]{2,1,0:T(8,128)(2,1)S(1)} %get-tuple-element.29.v_ref.source, bf16[4,96,128]{2,1,0:T(8,128)(2,1)S(1)} %bitcast.8, ...), custom_call_target="tpu_custom_call" | custom-call | flops 150994944 | bytes 4718592 | tf_op jit(solution)/shard_map/local/pallas_call | solution.py:254
  21.8 0.2 collective-permute-done.3.refs_0_
  22.0 1.4 %collective-permute-done.4.refs_1_ = bf16[24,16,128]{2,1,0:T(8,128)(2,1)S(1)} collective-permute-done((bf16[24,16,128]{2,1,0:T(8,128)(2,1)S(1)}, bf16[24,16,128]{2,1,0:T(8,128)(2,1)S(1)}, u32[]{:S(2)}, u32[]{:S(2)}) %collective-permute-start.4) | collective-permute-done | bytes 98336 | tf_op jit(solution)/shard_map/ppermute | solution.py:26
  23.4 0.9 %collective-permute-done.5.refs_2_ = bf16[24,16,128]{2,1,0:T(8,128)(2,1)S(1)} collective-permute-done((bf16[24,16,128]{2,1,0:T(8,128)(2,1)S(1)}, bf16[24,16,128]{2,1,0:T(8,128)(2,1)S(1)}, u32[]{:S(2)}, u32[]{:S(2)}) %collective-permute-start.5) | collective-permute-done | bytes 98336 | tf_op jit(solution)/shard_map/ppermute | solution.py:20
  24.3 0.7 %near.1 = (bf16[48,16,128]{2,1,0:T(8,128)(2,1)S(1)}, bf16[24,16,128]{2,1,0:T(8,128)(2,1)S(1)}, bf16[24,16,128]{2,1,0:T(8,128)(2,1)S(1)}, bf16[24,16,128]{2,1,0:T...) custom-call(bf16[48,9,64,128]{3,2,1,0:T(8,128)(2,1)S(1)} %load.1.ref, ...), custom_call_target="tpu_custom_call" | custom-call | flops 75497472 | bytes 2359296 | tf_op jit(solution)/shard_map/near/pallas_call | solution.py:254
  25.0 0.2 collective-permute-start.7
  25.2 4.0 %collective-permute-start.8 = (bf16[24,16,128]{2,1,0:T(8,128)(2,1)S(1)}, bf16[24,16,128]{2,1,0:T(8,128)(2,1)S(1)}, u32[]{:S(2)}, u32[]{:S(2)}) collective-permute-start(bf16[24,16,128]{2,1,0:T(8,128)(2,1)S(1)} %get-tuple-element.36), channel_id=1, source_target_pairs={{0,15},{1,2},{2,1},{3,4},{4,3},{5,6},{6,5},{7,8},{8,7},{9,10},{10,... | collective-permute-start | bytes 294920 | tf_op jit(solution)/shard_map/ppermute | solution.py:26
  29.2 1.0 %collective-permute-start.9 = (bf16[24,16,128]{2,1,0:T(8,128)(2,1)S(1)}, bf16[24,16,128]{2,1,0:T(8,128)(2,1)S(1)}, u32[]{:S(2)}, u32[]{:S(2)}) collective-permute-start(bf16[24,16,128]{2,1,0:T(8,128)(2,1)S(1)} %get-tuple-element.37), channel_id=1, source_target_pairs={{0,48},{16,32},{32,16},{48,0},{1,49},{17,33},{33,17},{49,1},{2,50}... | collective-permute-start | bytes 294920 | tf_op jit(solution)/shard_map/ppermute | solution.py:26
  30.2 2.3 %collective-permute-start.10 = (bf16[24,16,128]{2,1,0:T(8,128)(2,1)S(1)}, bf16[24,16,128]{2,1,0:T(8,128)(2,1)S(1)}, u32[]{:S(2)}, u32[]{:S(2)}) collective-permute-start(bf16[24,16,128]{2,1,0:T(8,128)(2,1)S(1)} %get-tuple-element.38), channel_id=1, source_target_pairs={{0,192},{64,128},{128,64},{192,0},{1,193},{65,129},{129,65},{193,1... | collective-permute-start | bytes 294920 | tf_op jit(solution)/shard_map/ppermute | solution.py:26
  32.5 0.1 collective-permute-start.11
  32.6 1.9 %local.3.total = f32[48,16,128]{2,1,0:T(8,128)S(1)} custom-call(bf16[48,9,64,128]{3,2,1,0:T(8,128)(2,1)S(1)} %load.1.refs_4_.links, bf16[48,16,128]{2,1,0:T(8,128)(2,1)S(1)} %get-tuple-element.34.v_ref, bf16[48,16,128]{2,1,0:T(8,128)(2,1)S(1)} %get-tuple-element.29.v_ref.source, bf16[24,16,128]{2,1,0:T(8,128)(2,1)S(1)} %collective-permute-done.7.refs_0_), custom_call_target="tpu_custom_call" | custom-call | flops 150994944 | bytes 4718592 | tf_op jit(solution)/shard_map/local/pallas_call | solution.py:254
  34.5 2.1 %collective-permute-done.8.refs_0_ = bf16[24,16,128]{2,1,0:T(8,128)(2,1)S(1)} collective-permute-done((bf16[24,16,128]{2,1,0:T(8,128)(2,1)S(1)}, bf16[24,16,128]{2,1,0:T(8,128)(2,1)S(1)}, u32[]{:S(2)}, u32[]{:S(2)}) %collective-permute-start.8) | collective-permute-done | bytes 98336 | tf_op jit(solution)/shard_map/ppermute | solution.py:26
  36.6 0.7 %collective-permute-done.11.refs_3_ = bf16[24,16,128]{2,1,0:T(8,128)(2,1)S(1)} collective-permute-done((bf16[24,16,128]{2,1,0:T(8,128)(2,1)S(1)}, bf16[24,16,128]{2,1,0:T(8,128)(2,1)S(1)}, u32[]{:S(2)}, u32[]{:S(2)}) %collective-permute-start.11) | collective-permute-done | bytes 98336 | tf_op jit(solution)/shard_map/ppermute | solution.py:20
  37.3 0.0 collective-permute-done.12.refs_4_
  37.3 0.9 %last.1 = (f32[4,48,128]{2,1,0:T(8,128)S(1)}, f32[4,48,128]{2,1,0:T(8,128)S(1)}, f32[4,48,128]{2,1,0:T(8,128)S(1)}, f32[4,48,128]{2,1,0:T(8,128)S(1)}) custom-call(bf16[48,9,64,128]{3,2,1,0:T(8,128)(2,1)S(1)} %load.1.refs_4_.links, f32[48,16,128]{2,1,0:T(8,128)S(1)} %local.3.total, bf16[24,16,128]{2,1,0:T(8,128)(2,1)S(1)} %collective-permute-done.8.refs_0_, ...), custom_call_target="tpu_custom_call" | custom-call | flops 75497472 | bytes 2359296 | tf_op jit(solution)/shard_map/last/pallas_call | solution.py:254
  38.2 2.4 %collective-permute-start.15 = (f32[4,48,128]{2,1,0:T(8,128)S(1)}, f32[4,48,128]{2,1,0:T(8,128)S(1)}, u32[]{:S(2)}, u32[]{:S(2)}) collective-permute-start(f32[4,48,128]{2,1,0:T(8,128)S(1)} %get-tuple-element.44), channel_id=1, source_target_pairs={{0,128},{64,192},{128,0},{192,64},{1,129},{65,193},{129,1},{193,65... | collective-permute-start | bytes 294920 | tf_op jit(solution)/shard_map/ppermute | solution.py:20
  40.6 0.1 collective-permute-start.13
  40.7 2.2 %collective-permute-start.14 = (f32[4,48,128]{2,1,0:T(8,128)S(1)}, f32[4,48,128]{2,1,0:T(8,128)S(1)}, u32[]{:S(2)}, u32[]{:S(2)}) collective-permute-start(f32[4,48,128]{2,1,0:T(8,128)S(1)} %get-tuple-element.42), channel_id=1, source_target_pairs={{0,192},{64,128},{128,64},{192,0},{1,193},{65,129},{129,65},{193,1... | collective-permute-start | bytes 294920 | tf_op jit(solution)/shard_map/ppermute | solution.py:20
  42.8 2.6 %collective-permute-done.15.refs_1_ = f32[4,48,128]{2,1,0:T(8,128)S(1)} collective-permute-done((f32[4,48,128]{2,1,0:T(8,128)S(1)}, f32[4,48,128]{2,1,0:T(8,128)S(1)}, u32[]{:S(2)}, u32[]{:S(2)}) %collective-permute-start.15) | collective-permute-done | bytes 98336 | tf_op jit(solution)/shard_map/ppermute | solution.py:20
  45.4 0.7 %join.2.refs_2_ = f32[4,4,48,128]{3,2,1,0:T(8,128)} custom-call(f32[4,48,128]{2,1,0:T(8,128)S(1)} %get-tuple-element.43.refs_0_, f32[4,48,128]{2,1,0:T(8,128)S(1)} %collective-permute-done.15.refs_1_), custom_call_target="tpu_custom_call" | custom-call | bytes 393216 | tf_op jit(solution)/shard_map/join/pallas_call | solution.py:254
  46.1 0.4 collective-permute-done.14.refs_1_
  46.6 0.7 %join.3 = f32[4,4,48,128]{3,2,1,0:T(8,128)} custom-call(f32[4,48,128]{2,1,0:T(8,128)S(1)} %collective-permute-done.13.refs_0_, f32[4,48,128]{2,1,0:T(8,128)S(1)} %collective-permute-done.14.refs_1_, f32[4,4,48,128]{3,2,1,0:T(8,128)} %join.2.refs_2_), custom_call_target="tpu_custom_call", output_to_operand_aliasing={{}: (2, {})} | custom-call | bytes 393216 | tf_op jit(solution)/shard_map/join/pallas_call | solution.py:254
  (9 shorter events, 0.0 us)
Async XLA Ops:
  1.1 7.4 %collective-permute-start = (bf16[4,4,24,128]{3,2,1,0:T(8,128)(2,1)S(1)}, bf16[4,4,24,128]{3,2,1,0:T(8,128)(2,1)S(1)}, u32[]{:S(2)}, u32[]{:S(2)}) collective-permute-start(bf16[4,4,24,128]{3,2,1,0:T(8,128)(2,1)S(1)} %get-tuple-element.26), channel_id=1, source_target_pairs={{0,128},{64,192},{128,0},{192,64},{1,129},{65,193},{129,1},{193,65... | collective-permute-start | bytes 294920 | tf_op jit(solution)/shard_map/ppermute | solution.py:20
  4.4 5.3 %collective-permute-start.1 = (bf16[4,4,24,128]{3,2,1,0:T(8,128)(2,1)S(1)}, bf16[4,4,24,128]{3,2,1,0:T(8,128)(2,1)S(1)}, u32[]{:S(2)}, u32[]{:S(2)}) collective-permute-start(bf16[4,4,24,128]{3,2,1,0:T(8,128)(2,1)S(1)} %get-tuple-element.27), channel_id=1, source_target_pairs={{0,64},{64,0},{128,192},{192,128},{1,65},{65,1},{129,193},{193,129... | collective-permute-start | bytes 294920 | tf_op jit(solution)/shard_map/ppermute | solution.py:20
  5.0 5.8 %collective-permute-start.2 = (bf16[4,4,24,128]{3,2,1,0:T(8,128)(2,1)S(1)}, bf16[4,4,24,128]{3,2,1,0:T(8,128)(2,1)S(1)}, u32[]{:S(2)}, u32[]{:S(2)}) collective-permute-start(bf16[4,4,24,128]{3,2,1,0:T(8,128)(2,1)S(1)} %get-tuple-element.28), channel_id=1, source_target_pairs={{0,192},{64,128},{128,64},{192,0},{1,193},{65,129},{129,65},{193,1... | collective-permute-start | bytes 294920 | tf_op jit(solution)/shard_map/ppermute | solution.py:20
  11.1 11.0 %collective-permute-start.3 = (bf16[24,16,128]{2,1,0:T(8,128)(2,1)S(1)}, bf16[24,16,128]{2,1,0:T(8,128)(2,1)S(1)}, u32[]{:S(2)}, u32[]{:S(2)}) collective-permute-start(bf16[24,16,128]{2,1,0:T(8,128)(2,1)S(1)} %get-tuple-element.30), channel_id=1, source_target_pairs={{0,15},{1,2},{2,1},{3,4},{4,3},{5,6},{6,5},{7,8},{8,7},{9,10},{10,... | collective-permute-start | bytes 294920 | tf_op jit(solution)/shard_map/ppermute | solution.py:26
  18.7 4.7 %collective-permute-start.4 = (bf16[24,16,128]{2,1,0:T(8,128)(2,1)S(1)}, bf16[24,16,128]{2,1,0:T(8,128)(2,1)S(1)}, u32[]{:S(2)}, u32[]{:S(2)}) collective-permute-start(bf16[24,16,128]{2,1,0:T(8,128)(2,1)S(1)} %get-tuple-element.31), channel_id=1, source_target_pairs={{0,48},{16,32},{32,16},{48,0},{1,49},{17,33},{33,17},{49,1},{2,50}... | collective-permute-start | bytes 294920 | tf_op jit(solution)/shard_map/ppermute | solution.py:26
  18.7 5.5 %collective-permute-start.5 = (bf16[24,16,128]{2,1,0:T(8,128)(2,1)S(1)}, bf16[24,16,128]{2,1,0:T(8,128)(2,1)S(1)}, u32[]{:S(2)}, u32[]{:S(2)}) collective-permute-start(bf16[24,16,128]{2,1,0:T(8,128)(2,1)S(1)} %get-tuple-element.32), channel_id=1, source_target_pairs={{0,1},{1,0},{2,3},{3,2},{4,5},{5,4},{6,7},{7,6},{8,9},{9,8},{10,11... | collective-permute-start | bytes 294920 | tf_op jit(solution)/shard_map/ppermute | solution.py:20
  18.8 5.5 %collective-permute-start.6 = (bf16[24,16,128]{2,1,0:T(8,128)(2,1)S(1)}, bf16[24,16,128]{2,1,0:T(8,128)(2,1)S(1)}, u32[]{:S(2)}, u32[]{:S(2)}) collective-permute-start(bf16[24,16,128]{2,1,0:T(8,128)(2,1)S(1)} %get-tuple-element.33), channel_id=1, source_target_pairs={{0,16},{16,0},{32,48},{48,32},{1,17},{17,1},{33,49},{49,33},{2,18}... | collective-permute-start | bytes 294920 | tf_op jit(solution)/shard_map/ppermute | solution.py:20
  25.0 7.6 %collective-permute-start.7 = (bf16[24,16,128]{2,1,0:T(8,128)(2,1)S(1)}, bf16[24,16,128]{2,1,0:T(8,128)(2,1)S(1)}, u32[]{:S(2)}, u32[]{:S(2)}) collective-permute-start(bf16[24,16,128]{2,1,0:T(8,128)(2,1)S(1)} %get-tuple-element.35), channel_id=1, source_target_pairs={{0,16},{16,0},{32,48},{48,32},{1,17},{17,1},{33,49},{49,33},{2,18}... | collective-permute-start | bytes 294920 | tf_op jit(solution)/shard_map/ppermute | solution.py:20
  25.2 11.4 %collective-permute-start.8 = (bf16[24,16,128]{2,1,0:T(8,128)(2,1)S(1)}, bf16[24,16,128]{2,1,0:T(8,128)(2,1)S(1)}, u32[]{:S(2)}, u32[]{:S(2)}) collective-permute-start(bf16[24,16,128]{2,1,0:T(8,128)(2,1)S(1)} %get-tuple-element.36), channel_id=1, source_target_pairs={{0,15},{1,2},{2,1},{3,4},{4,3},{5,6},{6,5},{7,8},{8,7},{9,10},{10,... | collective-permute-start | bytes 294920 | tf_op jit(solution)/shard_map/ppermute | solution.py:26
  29.2 7.4 %collective-permute-start.9 = (bf16[24,16,128]{2,1,0:T(8,128)(2,1)S(1)}, bf16[24,16,128]{2,1,0:T(8,128)(2,1)S(1)}, u32[]{:S(2)}, u32[]{:S(2)}) collective-permute-start(bf16[24,16,128]{2,1,0:T(8,128)(2,1)S(1)} %get-tuple-element.37), channel_id=1, source_target_pairs={{0,48},{16,32},{32,16},{48,0},{1,49},{17,33},{33,17},{49,1},{2,50}... | collective-permute-start | bytes 294920 | tf_op jit(solution)/shard_map/ppermute | solution.py:26
  30.2 6.3 %collective-permute-start.10 = (bf16[24,16,128]{2,1,0:T(8,128)(2,1)S(1)}, bf16[24,16,128]{2,1,0:T(8,128)(2,1)S(1)}, u32[]{:S(2)}, u32[]{:S(2)}) collective-permute-start(bf16[24,16,128]{2,1,0:T(8,128)(2,1)S(1)} %get-tuple-element.38), channel_id=1, source_target_pairs={{0,192},{64,128},{128,64},{192,0},{1,193},{65,129},{129,65},{193,1... | collective-permute-start | bytes 294920 | tf_op jit(solution)/shard_map/ppermute | solution.py:26
  32.5 4.8 %collective-permute-start.11 = (bf16[24,16,128]{2,1,0:T(8,128)(2,1)S(1)}, bf16[24,16,128]{2,1,0:T(8,128)(2,1)S(1)}, u32[]{:S(2)}, u32[]{:S(2)}) collective-permute-start(bf16[24,16,128]{2,1,0:T(8,128)(2,1)S(1)} %get-tuple-element.39), channel_id=1, source_target_pairs={{0,64},{64,0},{128,192},{192,128},{1,65},{65,1},{129,193},{193,129... | collective-permute-start | bytes 294920 | tf_op jit(solution)/shard_map/ppermute | solution.py:20
  32.6 4.7 %collective-permute-start.12 = (bf16[24,16,128]{2,1,0:T(8,128)(2,1)S(1)}, bf16[24,16,128]{2,1,0:T(8,128)(2,1)S(1)}, u32[]{:S(2)}, u32[]{:S(2)}) collective-permute-start(bf16[24,16,128]{2,1,0:T(8,128)(2,1)S(1)} %get-tuple-element.40), channel_id=1, source_target_pairs={{0,1},{1,0},{2,3},{3,2},{4,5},{5,4},{6,7},{7,6},{8,9},{9,8},{10,11... | collective-permute-start | bytes 294920 | tf_op jit(solution)/shard_map/ppermute | solution.py:20
  38.2 7.2 %collective-permute-start.15 = (f32[4,48,128]{2,1,0:T(8,128)S(1)}, f32[4,48,128]{2,1,0:T(8,128)S(1)}, u32[]{:S(2)}, u32[]{:S(2)}) collective-permute-start(f32[4,48,128]{2,1,0:T(8,128)S(1)} %get-tuple-element.44), channel_id=1, source_target_pairs={{0,128},{64,192},{128,0},{192,64},{1,129},{65,193},{129,1},{193,65... | collective-permute-start | bytes 294920 | tf_op jit(solution)/shard_map/ppermute | solution.py:20
  40.6 5.6 %collective-permute-start.13 = (f32[4,48,128]{2,1,0:T(8,128)S(1)}, f32[4,48,128]{2,1,0:T(8,128)S(1)}, u32[]{:S(2)}, u32[]{:S(2)}) collective-permute-start(f32[4,48,128]{2,1,0:T(8,128)S(1)} %get-tuple-element.41), channel_id=1, source_target_pairs={{0,64},{64,0},{128,192},{192,128},{1,65},{65,1},{129,193},{193,129... | collective-permute-start | bytes 294920 | tf_op jit(solution)/shard_map/ppermute | solution.py:20
  40.7 5.9 %collective-permute-start.14 = (f32[4,48,128]{2,1,0:T(8,128)S(1)}, f32[4,48,128]{2,1,0:T(8,128)S(1)}, u32[]{:S(2)}, u32[]{:S(2)}) collective-permute-start(f32[4,48,128]{2,1,0:T(8,128)S(1)} %get-tuple-element.42), channel_id=1, source_target_pairs={{0,192},{64,128},{128,64},{192,0},{1,193},{65,129},{129,65},{193,1... | collective-permute-start | bytes 294920 | tf_op jit(solution)/shard_map/ppermute | solution.py:20
